TPU v7x, 128 devices: a whole 4x4x4 slice. The times are simulated.
128 devices in a mesh: fsdp: 16 (over y, z), seq: 8 (over x, core).
Axes of the slice: x: 4, y: 4, z: 4, core: 2. Of those that a mesh axis runs over, the one named last changes fastest.
Arguments:
- tokens: bfloat16 [16384, 2048], P(('fsdp', 'seq')), may hold values from -6 to 6
- segments: int32 [16, 1024], P('fsdp'), may hold values from 0 to 2, as said below
- adapter_index: int32 [16], P('fsdp'), may hold values from 0 to 7
- attn_gain: float32 [2048], replicated, may hold values from 0.5 to 1.5
- w_qkv: bfloat16 [2048, 6144], P(None, 'fsdp'), may hold values from -0.125 to 0.125
- w_beta: bfloat16 [2048, 16], replicated, may hold values from -0.125 to 0.125
- conv_weight: float32 [4, 16, 384], replicated, may hold values from -3 to 3
- head_gain: float32 [128], replicated, may hold values from 0.5 to 1.5
- w_out: bfloat16 [2048, 2048], P(None, 'fsdp'), may hold values from -0.125 to 0.125
- ffn_gain: float32 [2048], replicated, may hold values from 0.5 to 1.5
- w_gateup: bfloat16 [2048, 11264], P(None, 'fsdp'), may hold values from -0.125 to 0.125
- w_down: bfloat16 [5632, 2048], P(None, 'fsdp'), may hold values from -0.078125 to 0.078125
- qkv_down: bfloat16 [8, 2048, 16], replicated, may hold values from -0.125 to 0.125
- qkv_up: bfloat16 [8, 16, 6144], replicated, may hold values from -0.75 to 0.75
- mixout_down: bfloat16 [8, 2048, 16], replicated, may hold values from -0.125 to 0.125
- mixout_up: bfloat16 [8, 16, 2048], replicated, may hold values from -0.75 to 0.75
- gateup_down: bfloat16 [8, 2048, 16], replicated, may hold values from -0.125 to 0.125
- gateup_up: bfloat16 [8, 16, 11264], replicated, may hold values from -0.75 to 0.75
- ffnout_down: bfloat16 [8, 5632, 16], replicated, may hold values from -0.078125 to 0.078125
- ffnout_up: bfloat16 [8, 16, 2048], replicated, may hold values from -0.75 to 0.75
- cotangent: bfloat16 [16384, 2048], P(('fsdp', 'seq')), may hold values from -6 to 6
Outputs:
- layer_out: bfloat16 [16384, 2048], P(('fsdp', 'seq'))
- input_grad: bfloat16 [16384, 2048], P(('fsdp', 'seq'))
- grad_qkvdown: float32 [8, 2048, 16], replicated
- grad_qkvup: float32 [8, 16, 6144], replicated
- grad_mixdown: float32 [8, 2048, 16], replicated
- grad_mixup: float32 [8, 16, 2048], replicated
- grad_gudown: float32 [8, 2048, 16], replicated
- grad_guup: float32 [8, 16, 11264], replicated
- grad_ffdown: float32 [8, 5632, 16], replicated
- grad_ffup: float32 [8, 16, 2048], replicated
Inputs may be any that keep to these rules, and one draw needn't show every extreme that they name: `segments`: each row holds exactly three documents, ids 0, 1, 2, never falling; document 1 starts within the first 128 tokens and ends within the last 128.
All inputs are finite; a program needn't handle non-finite values.
Results may differ from a plain program's by a relative error of at most 0.017.
Values may be sent and summed in bfloat16 or wider, within the bound.
A program may use at most 320 MiB of HBM per device.

v0:
```python
import jax
import jax.numpy as jnp
from jax import lax
from jax.sharding import PartitionSpec as P

BLOCK = 64


HIGH = lax.Precision.HIGHEST


def rms_scale(values, gain):
    return values * lax.rsqrt(jnp.mean(values * values, axis=-1, keepdims=True) + 1e-05) * gain


def norm_back(values, gain, grad):
    scale = lax.rsqrt(jnp.mean(values * values, axis=-1, keepdims=True) + 1e-05)
    weighted = grad * gain
    return scale * weighted - values * scale * scale * scale * jnp.mean(
        weighted * values, axis=-1, keepdims=True
    )


def delta_block(state, block):
    query, keys, values, strength, doc_ids, enter = block
    size = doc_ids.shape[0]
    live = (doc_ids == enter).astype(jnp.float32)
    same = (doc_ids[:, None] == doc_ids[None, :]).astype(jnp.float32)
    row_pos = lax.broadcasted_iota(jnp.int32, (size, size), 0)
    col_pos = lax.broadcasted_iota(jnp.int32, (size, size), 1)
    strict = same * (row_pos > col_pos).astype(jnp.float32)
    causal = same * (row_pos >= col_pos).astype(jnp.float32)
    inner = jnp.einsum("ihd,jhd->hij", keys, keys, precision=HIGH)
    lower = jnp.transpose(strength)[:, :, None] * inner * strict[None]
    recalled = jnp.einsum("ihd,hde->ihe", keys, state, precision=HIGH)
    target = strength[:, :, None] * (values - live[:, None, None] * recalled)
    target = jnp.transpose(target, (1, 0, 2))
    update = jax.scipy.linalg.solve_triangular(lower, target, lower=True, unit_diagonal=True)
    scores = jnp.einsum("ihd,jhd->hij", query, keys, precision=HIGH) * causal[None]
    output = live[:, None, None] * jnp.einsum("ihd,hde->ihe", query, state, precision=HIGH)
    output = output + jnp.einsum("hij,hje->ihe", scores, update, precision=HIGH)
    tail = (doc_ids == doc_ids[size - 1]).astype(jnp.float32)
    state = live[size - 1] * state + jnp.einsum(
        "jhd,j,hje->hde", keys, tail, update, precision=HIGH
    )
    return (state, output)


def mixer(joined, beta_raw, conv_w, head_gain, doc_ids):
    length = joined.shape[0]
    kernel = conv_w.shape[0]
    mixed = conv_w[kernel - 1] * joined
    for lag in range(1, kernel):
        shifted = jnp.concatenate(
            [jnp.zeros((lag,) + joined.shape[1:], jnp.float32), joined[: length - lag]], axis=0
        )
        keep = jnp.concatenate(
            [
                jnp.zeros((lag,), jnp.float32),
                (doc_ids[lag:] == doc_ids[: length - lag]).astype(jnp.float32),
            ]
        )
        mixed = mixed + conv_w[kernel - 1 - lag] * shifted * keep[:, None, None]
    active = jax.nn.silu(mixed)
    width = joined.shape[-1] // 3
    heads = joined.shape[1]
    query = active[..., :width]
    keys = active[..., width : 2 * width]
    values = active[..., 2 * width :]
    query = (
        query * lax.rsqrt(jnp.sum(query * query, axis=-1, keepdims=True) + 1e-06) * width ** (-0.5)
    )
    keys = keys * lax.rsqrt(jnp.sum(keys * keys, axis=-1, keepdims=True) + 1e-06)
    strength = jax.nn.sigmoid(beta_raw[..., 0])
    blocks = length // BLOCK
    previous = jnp.concatenate([jnp.full((1,), -1, jnp.int32), doc_ids[:-1]])
    enter = previous.reshape(blocks, BLOCK)[:, 0]

    def cut(array):
        return array.reshape((blocks, BLOCK) + array.shape[1:])

    start_state = jnp.zeros((heads, width, width), jnp.float32)
    final_state, outputs = lax.scan(
        jax.checkpoint(delta_block),
        start_state,
        (cut(query), cut(keys), cut(values), cut(strength), cut(doc_ids), enter),
    )
    result = outputs.reshape(length, heads, width)
    return rms_scale(result, head_gain)


def right_product(left, piece):
    return jnp.dot(left, piece, preferred_element_type=jnp.float32)


def transposed(grad, weight):
    return lax.dot_general(
        grad, weight, (((1,), (1,)), ((), ())), preferred_element_type=jnp.float32
    )


def back_product(grad, piece):
    return transposed(grad, piece)


def adapter_fwd(inputs, down, upper):
    inner = jnp.dot(inputs, down, preferred_element_type=jnp.float32).astype(jnp.bfloat16)
    return (inner, jnp.dot(inner, upper, preferred_element_type=jnp.float32))


def adapter_back(inputs, inner, down, upper, grad):
    grad_upper = lax.dot_general(
        inner, grad, (((0,), (0,)), ((), ())), preferred_element_type=jnp.float32
    )
    inner_grad = transposed(grad, upper).astype(jnp.bfloat16)
    grad_down = lax.dot_general(
        inputs, inner_grad, (((0,), (0,)), ((), ())), preferred_element_type=jnp.float32
    )
    return (transposed(inner_grad, down), grad_down, grad_upper)


def body(
    tokens,
    segments,
    adapter_index,
    attn_gain,
    w_qkv,
    w_beta,
    conv_weight,
    head_gain,
    w_out,
    ffn_gain,
    w_gateup,
    w_down,
    qkv_down,
    qkv_up,
    mixout_down,
    mixout_up,
    gateup_down,
    gateup_up,
    ffnout_down,
    ffnout_up,
    cotangent,
):
    rows = tokens.shape[0]
    width = tokens.shape[1]
    heads = w_beta.shape[1]
    head_size = width // heads
    local_heads = heads // lax.axis_size("seq")
    hidden_width = w_down.shape[0]
    count = qkv_down.shape[0]
    which = adapter_index[0]
    doc_ids = segments[0]

    def pick(array):
        return lax.dynamic_index_in_dim(array, which, 0, keepdims=False)

    base = tokens.astype(jnp.float32)
    normed = rms_scale(base, attn_gain).astype(jnp.bfloat16)
    main_qkv = right_product(normed, lax.all_gather(w_qkv, "fsdp", axis=1, tiled=True))
    qkv_inner, qkv_extra = adapter_fwd(normed, pick(qkv_down), pick(qkv_up))
    joined = (main_qkv + qkv_extra).astype(jnp.bfloat16).reshape(rows, heads, 3 * head_size)
    raw_beta = (
        jnp.dot(normed, w_beta, preferred_element_type=jnp.float32)
        .astype(jnp.bfloat16)
        .reshape(rows, heads, 1)
    )
    head_joined, head_beta = (
        lax.all_to_all(joined, "seq", split_axis=1, concat_axis=0, tiled=True),
        lax.all_to_all(raw_beta, "seq", split_axis=1, concat_axis=0, tiled=True),
    )
    conv_local = lax.dynamic_slice_in_dim(
        conv_weight, lax.axis_index("seq") * local_heads, local_heads, 1
    )

    def local_mixer(joined_in, beta_in):
        return mixer(joined_in, beta_in, conv_local, head_gain, doc_ids)

    mixed, mixer_back = jax.vjp(
        local_mixer, head_joined.astype(jnp.float32), head_beta.astype(jnp.float32)
    )
    returned = lax.all_to_all(
        mixed.astype(jnp.bfloat16), "seq", split_axis=0, concat_axis=1, tiled=True
    ).reshape(rows, width)
    main_out = right_product(returned, lax.all_gather(w_out, "fsdp", axis=1, tiled=True))
    out_inner, out_extra = adapter_fwd(returned, pick(mixout_down), pick(mixout_up))
    middle = base + (main_out + out_extra)
    normed2 = rms_scale(middle, ffn_gain).astype(jnp.bfloat16)
    main_gateup = right_product(normed2, lax.all_gather(w_gateup, "fsdp", axis=1, tiled=True))
    gu_inner, gu_extra = adapter_fwd(normed2, pick(gateup_down), pick(gateup_up))
    gateup = main_gateup + gu_extra
    gate = gateup[:, :hidden_width]
    upper = gateup[:, hidden_width:]
    hidden = (jax.nn.silu(gate) * upper).astype(jnp.bfloat16)
    main_down = right_product(hidden, lax.all_gather(w_down, "fsdp", axis=1, tiled=True))
    ff_inner, ff_extra = adapter_fwd(hidden, pick(ffnout_down), pick(ffnout_up))
    layer_out = (middle + (main_down + ff_extra)).astype(jnp.bfloat16)
    hidden_main = back_product(cotangent, lax.all_gather(w_down, "fsdp", axis=1, tiled=True))
    hidden_extra, grad_ffdown, grad_ffup = adapter_back(
        hidden, ff_inner, pick(ffnout_down), pick(ffnout_up), cotangent
    )
    grad_hidden = hidden_main + hidden_extra
    sigma = jax.nn.sigmoid(gate)
    grad_gate = grad_hidden * upper * sigma * (1.0 + gate * (1.0 - sigma))
    grad_upper = grad_hidden * gate * sigma
    grad_gateup = jnp.concatenate([grad_gate, grad_upper], axis=1).astype(jnp.bfloat16)
    normed2_main = back_product(grad_gateup, lax.all_gather(w_gateup, "fsdp", axis=1, tiled=True))
    normed2_extra, grad_gudown, grad_guup = adapter_back(
        normed2, gu_inner, pick(gateup_down), pick(gateup_up), grad_gateup
    )
    grad_middle = cotangent.astype(jnp.float32) + norm_back(
        middle, ffn_gain, normed2_main + normed2_extra
    )
    grad_branch = grad_middle.astype(jnp.bfloat16)
    returned_main = back_product(grad_branch, lax.all_gather(w_out, "fsdp", axis=1, tiled=True))
    returned_extra, grad_mixdown, grad_mixup = adapter_back(
        returned, out_inner, pick(mixout_down), pick(mixout_up), grad_branch
    )
    grad_returned = (
        (returned_main + returned_extra).astype(jnp.bfloat16).reshape(rows, heads, head_size)
    )
    head_grad = lax.all_to_all(grad_returned, "seq", split_axis=1, concat_axis=0, tiled=True)
    grad_joined_heads, grad_beta_heads = mixer_back(head_grad.astype(jnp.float32))
    grad_joined, grad_beta = (
        lax.all_to_all(
            grad_joined_heads.astype(jnp.bfloat16), "seq", split_axis=0, concat_axis=1, tiled=True
        ),
        lax.all_to_all(
            grad_beta_heads.astype(jnp.bfloat16), "seq", split_axis=0, concat_axis=1, tiled=True
        ),
    )
    grad_joined = grad_joined.reshape(rows, 3 * width)
    grad_beta = grad_beta.reshape(rows, heads)
    normed_main = back_product(grad_joined, lax.all_gather(w_qkv, "fsdp", axis=1, tiled=True))
    normed_extra, grad_qkvdown, grad_qkvup = adapter_back(
        normed, qkv_inner, pick(qkv_down), pick(qkv_up), grad_joined
    )
    grad_normed = normed_main + normed_extra + transposed(grad_beta, w_beta)
    input_grad = (grad_middle + norm_back(base, attn_gain, grad_normed)).astype(jnp.bfloat16)
    spread = (jnp.arange(count, dtype=jnp.int32) == which).astype(jnp.float32)[:, None, None]
    summed = lax.psum(
        (
            spread * grad_qkvdown[None],
            spread * grad_qkvup[None],
            spread * grad_mixdown[None],
            spread * grad_mixup[None],
            spread * grad_gudown[None],
            spread * grad_guup[None],
            spread * grad_ffdown[None],
            spread * grad_ffup[None],
        ),
        ("fsdp", "seq"),
    )
    return (
        layer_out,
        input_grad,
        summed[0],
        summed[1],
        summed[2],
        summed[3],
        summed[4],
        summed[5],
        summed[6],
        summed[7],
    )


def solution(mesh):
    placed = (
        P(("fsdp", "seq"), None),
        P("fsdp", None),
        P("fsdp"),
        P(),
        P(None, "fsdp"),
        P(),
        P(),
        P(),
        P(None, "fsdp"),
        P(),
        P(None, "fsdp"),
        P(None, "fsdp"),
        P(),
        P(),
        P(),
        P(),
        P(),
        P(),
        P(),
        P(),
        P(("fsdp", "seq"), None),
    )
    return jax.shard_map(
        body,
        mesh=mesh,
        in_specs=placed,
        out_specs=(
            P(("fsdp", "seq"), None),
            P(("fsdp", "seq"), None),
            P(),
            P(),
            P(),
            P(),
            P(),
            P(),
            P(),
            P(),
        ),
        check_vma=False,
    )
```

profile of v0, /device:TPU:1, one launch (start us, length us, event | category | flops | bytes accessed | tf_op | source)
XLA Modules:
  0.0 1558.4 jit_solution(14387890348730029877)
XLA Ops:
  18.8 157.7 %all-gather.5.cloned.1.call-done = bf16[2048,6144]{1,0:T(8,128)(2,1)} async-done(((bf16[2048,384]{1,0:T(8,128)(2,1)}), bf16[2048,6144]{1,0:T(8,128)(2,1)}) %all-gather.5.cloned.1.call-update) | async-done | bytes 25165840 | tf_op jit(solution)/shard_map/all_gather | solution.py:160
  176.5 10.1 fusion.188
  228.7 427.5 %while.38 = (s32[]{:T(128)}, f32[2,128,128]{2,1,0:T(8,128)S(1)}, f32[16,64,2,128]{3,1,2,0:T(8,128)}, f32[16,2,128,128]{3,2,1,0:T(8,128)}, s32[16,64]{1,0:T(8,128...) while((s32[]{:T(128)}, f32[2,128,128]{2,1,0:T(8,128)S(1)}, ...), condition=%wide.region_4.6_spmd.clone, body=%wide.region_3.5_spmd.clone.sunk | while | flops 126206272 | bytes 2034094 | solution.py:83
  234.4 11.2 custom-call.26
  261.1 11.2 custom-call.26
  287.8 11.2 custom-call.26
  314.5 11.2 custom-call.26
  341.2 11.2 custom-call.26
  367.9 11.2 custom-call.26
  394.6 11.2 custom-call.26
  421.3 11.2 custom-call.26
  448.1 11.2 custom-call.26
  474.8 11.2 custom-call.26
  501.6 11.2 custom-call.26
  528.4 11.2 custom-call.26
  555.1 11.2 custom-call.26
  581.8 11.2 custom-call.26
  608.6 11.2 custom-call.26
  635.3 11.2 custom-call.26
  668.5 13.3 fusion.197
  696.2 22.2 %fusion.195 = f32[128,11264]{1,0:T(8,128)} fusion(bf16[128,2048]{1,0:T(8,128)(2,1)} %copy-done.15, bf16[2048,11264]{0,1:T(8,128)(2,1)} %all-gather.9.cloned.1.call-done), kind=kOutput, calls=%fused_computation.336 | convolution fusion | flops 5905580032 | bytes 52428800 | tf_op jit(solution)/shard_map/dot_general | solution.py:93
  729.7 18.5 %fusion.123 = f32[128,2048]{1,0:T(8,128)S(1)} fusion(bf16[2048,11264]{0,1:T(8,128)(2,1)} %all-gather.9.cloned.1.call-done, bf16[128,5632]{1,0:T(8,128)(2,1)} %copy-done.22, bf16[128,5632]{1,0:T(8,128)(2,1)} %copy-done.21), kind=kOutput, calls=%fused_computation.234 | convolution fusion | flops 5911347200 | bytes 50069504 | tf_op jit(solution)/shard_map/dot_general | solution.py:97
  783.2 485.4 %while.39 = (s32[]{:T(128)}, f32[2,128,128]{2,1,0:T(8,128)S(1)}, f32[16,64,2,128]{3,1,0,2:T(8,128)S(1)}, f32[16,64,2,128]{3,1,0,2:T(8,128)}, f32[16,64,2,128]{3,...) while((s32[]{:T(128)}, f32[2,128,128]{2,1,0:T(8,128)S(1)}, ...), condition=%wide.region_12.14_spmd.clone, body=%wide.region_9.13_spmd.clone.sunk | while | flops 321499328 | bytes 5858335 | solution.py:83
  851.0 9.8 custom-call.27
  881.4 9.8 custom-call.27
  1002.8 9.8 custom-call.27
  1184.8 9.8 custom-call.27
  1245.4 9.8 custom-call.27
  1288.5 17.6 %all-to-all-done.4 = bf16[1024,2,384]{2,1,0:T(2,128)(2,1)S(1)} async-done(((bf16[1024,2,384]{2,1,0:T(2,128)(2,1)}), bf16[1024,2,384]{2,1,0:T(2,128)(2,1)S(1)}, u32[]{:S(2)}, u32[]{:S(2)}) %all-to-all-start.4) | async-done | bytes 1572896 | tf_op jit(solution)/shard_map/all_to_all | solution.py:225
  1315.4 12.9 fusion.196
  1343.7 13.7 fusion.198
  1360.3 174.9 %all-reduce.14.cloned.1.call-done = (f32[8,2048,16]{1,2,0:T(8,128)}, f32[8,16,6144]{2,1,0:T(8,128)}, f32[8,2048,16]{1,2,0:T(8,128)}, f32[8,16,2048]{2,1,0:T(8,12...) async-done(((f32[8,2048,16]{1,2,0:T(8,128)}, f32[8,16,6144]{2,1,0:T(8,128)}, f32[8,2048,16]{1,2,0:T(8,128)}, ...) | async-done | bytes 17039376 | tf_op jit(solution)/shard_map/psum | solution.py:241
  (1194 shorter events, 868.7 us)
Async XLA Ops:
  7.2 711.3 %copy-start = (bf16[8,16,11264]{2,1,0:T(8,128)(2,1)S(1)}, bf16[8,16,11264]{2,1,0:T(8,128)(2,1)}, u32[]{:S(2)}) copy-start(bf16[8,16,11264]{2,1,0:T(8,128)(2,1)} %param.44) | copy-start | bytes 8650756
  7.2 169.3 %all-gather.5.cloned.1.call-start = ((), (), s32[]{:S(2)}) async-start(), calls=%async_computation.6 | async-start | bytes 26738688 | tf_op jit(solution)/shard_map/all_gather | solution.py:160
  8.0 660.6 %all-gather.11.cloned.1.call-start = ((), (), s32[]{:S(2)}) async-start(), calls=%async_computation.9 | async-start | bytes 24510464 | tf_op jit(solution)/shard_map/all_gather | solution.py:195
  8.7 678.3 %all-gather.7.cloned.1.call-start = ((), (), s32[]{:S(2)}) async-start(), calls=%async_computation.7 | async-start | bytes 8912896 | tf_op jit(solution)/shard_map/all_gather | solution.py:185
  9.4 686.8 %all-gather.9.cloned.1.call-start = ((), (), s32[]{:S(2)}) async-start(), calls=%async_computation.8 | async-start | bytes 49020928 | tf_op jit(solution)/shard_map/all_gather | solution.py:189
  10.2 176.3 %copy-start.70 = (f32[128]{0:T(128)}, f32[128]{0:T(128)S(1)}, u32[]{:S(2)}) copy-start(f32[128]{0:T(128)S(1)} %add_rsqrt_fusion.3) | copy-start | bytes 1540
  11.2 178.3 %all-to-all-start.1 = ((bf16[8,2,128]{2,1,0:T(2,128)(2,1)}), bf16[8,2,128]{2,1,0:T(2,128)(2,1)S(1)}, u32[]{:S(2)}, u32[]{:S(2)}) async-start(bf16[8,2,128]{2,1,0:T(2,128)(2,1)} %bitcast.384), calls=%async_computation.1 | async-start | bytes 8192 | tf_op jit(solution)/shard_map/all_to_all | solution.py:170
  18.8 167.8 %copy-start.63 = (bf16[128,16]{0,1:T(8,128)(2,1)}, bf16[128,16]{0,1:T(8,128)(2,1)S(1)}, u32[]{:S(2)}) copy-start(bf16[128,16]{0,1:T(8,128)(2,1)S(1)} %convolution_convert_fusion.8) | copy-start | bytes 12292
  188.1 7.2 copy-start.29
  189.5 5.9 copy-start.62
  189.5 26.7 %all-to-all-start = ((bf16[128,16,384]{2,0,1:T(8,128)(2,1)}), bf16[128,16,384]{2,0,1:T(8,128)(2,1)}, u32[]{:S(2)}, u32[]{:S(2)}) async-start(bf16[128,16,384]{2,0,1:T(8,128)(2,1)} %bitcast.564), calls=%async_computation | async-start | bytes 3145728 | tf_op jit(solution)/shard_map/all_to_all | solution.py:169
  200.3 8.6 copy-start.49
  208.9 9.3 copy-start.40
  660.1 21.7 %copy-start.30 = (f32[16,64,2]{1,0,2:T(8,128)}, f32[16,64,2]{1,0,2:T(8,128)S(1)}, u32[]{:S(2)}) copy-start(f32[16,64,2]{1,0,2:T(8,128)S(1)} %fusion.157) | copy-start | bytes 24580
  663.1 18.7 %all-to-all-start.2 = ((bf16[1024,2,128]{2,1,0:T(2,128)(2,1)}), bf16[1024,2,128]{2,1,0:T(2,128)(2,1)}, u32[]{:S(2)}, u32[]{:S(2)}) async-start(bf16[1024,2,128]{2,1,0:T(2,128)(2,1)} %copy.270), calls=%async_computation.2 | async-start | bytes 1048576 | tf_op jit(solution)/shard_map/all_to_all | solution.py:182
  687.0 7.2 copy-start.51
  729.7 18.5 %copy-start.5 = (f32[128,2048]{1,0:T(8,128)S(1)}, f32[128,2048]{1,0:T(8,128)}, u32[]{:S(2)}) copy-start(f32[128,2048]{1,0:T(8,128)} %copy-done.4) | copy-start | bytes 3145732
  753.1 8.4 copy-start.45
  761.5 7.2 copy-start.68
  763.6 14.5 all-to-all-start.3
  773.0 5.4 copy-start.73
  1278.2 7.4 copy-start.69
  1281.0 25.1 %all-to-all-start.4 = ((bf16[1024,2,384]{2,1,0:T(2,128)(2,1)}), bf16[1024,2,384]{2,1,0:T(2,128)(2,1)S(1)}, u32[]{:S(2)}, u32[]{:S(2)}) async-start(bf16[1024,2,384]{2,1,0:T(2,128)(2,1)} %copy.285), calls=%async_computation.4 | async-start | bytes 3145728 | tf_op jit(solution)/shard_map/all_to_all | solution.py:225
  1285.3 249.9 %all-reduce.14.cloned.1.call-start = ((), (), s32[]{:S(2)}) async-start(), calls=%async_computation.10 | async-start | bytes 34078720 | tf_op jit(solution)/shard_map/psum | solution.py:241
  1315.4 13.0 copy-start.44
  1315.4 13.0 copy-start.41
  1315.4 22.8 %copy-start.46 = (bf16[128,16]{0,1:T(8,128)(2,1)S(1)}, bf16[128,16]{0,1:T(8,128)(2,1)}, u32[]{:S(2)}) copy-start(bf16[128,16]{0,1:T(8,128)(2,1)} %copy-done.45) | copy-start | bytes 12292
  1334.1 8.6 all-to-all-start.5
  1343.7 14.9 copy-start.43
  1535.2 9.4 slice-start
  1537.7 6.9 slice-start.1
  1544.6 6.8 copy-start.1
  (70 other events, 141.0 us)
Sparse Core Ops, SparseCore 0:
  10.2 166.2 all-gather.4
  178.6 152.1 all-gather.10
  332.9 79.1 all-gather.6
  414.2 261.2 all-gather.8
  1315.5 219.6 all-reduce.13
where the time goes:
time: 1580 us; the launch traced here: 1560 us
  other arithmetic  456 us (29%)
  matrix products  426 us (27%)
  waiting for transfers between devices  364 us (23%)
  local copies, waits for them, and re-layouts  262 us (17%)
  starting transfers between devices  30.9 us (2%)
  between operations  15.9 us (1%)
    another operation x112, other arithmetic, delta_block(): jax.scipy.linalg.solve_triangular(lower, target, lower=True, unit_diagona...  341 us
    psum x1, waiting for transfers between devices, body(): lax.psum((spread * grad_qkvdown[None], spread * grad_qkvup[None], spread...  175 us
    all_gather x1, waiting for transfers between devices, body(): lax.all_gather(w_qkv, 'fsdp', axis=1, tiled=True)  158 us
    squeeze x96, local copies, waits for them, and re-layouts, mixer(): lax.scan(jax.checkpoint(delta_block), start_state, (cut(query), cut(keys)...  87.5 us
    dot_general x13, matrix products, transposed(): lax.dot_general(grad, weight, (((1,), (1,)), ((), ())), preferred_element...  65.2 us
    dot_general x64, matrix products, delta_block(): inner = jnp.einsum('ihd,jhd->hij', keys, keys, precision=HIGH)  52.3 us
    dot_general x48, matrix products, delta_block(): jnp.einsum('jhd,j,hje->hde', keys, tail, update, precision=HIGH)  50.5 us
    dot_general x4, matrix products, right_product(): return jnp.dot(left, piece, preferred_element_type=jnp.float32)  50.1 us
  transfers between devices with their start and end apart: 11, of which 6 were waited for; matrix products, arithmetic and copies ran while one was open for 35% of the time, Pallas kernels for 0%

commit v1 on v0

v1 whole, which is shorter than its diff:
```python
import functools
import jax
import jax.numpy as jnp
from jax import lax
from jax.experimental import pallas as pl
from jax.experimental.pallas import tpu as pltpu
from jax.sharding import PartitionSpec as P

F32 = jnp.float32
BF16 = jnp.bfloat16
CH = 128
PAD = 16


def mm(a, b):
    return jnp.dot(a.astype(BF16), b.astype(BF16), preferred_element_type=F32)


def mm_nt(a, b):
    return lax.dot_general(
        a.astype(BF16), b.astype(BF16), (((1,), (1,)), ((), ())), preferred_element_type=F32
    )


def mm_tn(a, b):
    return lax.dot_general(
        a.astype(BF16), b.astype(BF16), (((0,), (0,)), ((), ())), preferred_element_type=F32
    )


def split(a):
    high = a.astype(BF16)
    return high, (a - high.astype(F32)).astype(BF16)


def mm_fine(a, b):
    ah, al = split(a)
    bh, bl = split(b)
    return jnp.dot(
        jnp.concatenate([ah, al, ah], axis=1),
        jnp.concatenate([bh, bh, bl], axis=0),
        preferred_element_type=F32,
    )


def unit_lower_inverse(lower, row, col, product):
    near = jnp.where((row >> 3) == (col >> 3), lower, 0.0)
    eye = (row == col).astype(F32)
    second = product(near, near)
    fourth = product(second, second)
    inverse = eye - near + second - product(near, second)
    inverse = inverse + product(inverse, fourth)
    for bits in (3, 4, 5, 6):
        joining = ((row >> (bits + 1)) == (col >> (bits + 1))) & ((row >> bits) != (col >> bits))
        below = jnp.where(joining, lower, 0.0)
        inverse = inverse - product(inverse, product(below, inverse))
    return inverse


def sigmoid(v):
    return 1.0 / (1.0 + jnp.exp(-v))


def chunk_masks(c, dcol, drow):
    start = pl.multiple_of(c * CH, CH)
    docs = dcol[pl.ds(start + PAD, CH), :]
    before = dcol[pl.ds(start + PAD - 8, 8), :][7:8, :]
    last = docs[CH - 1 :, :]
    same = docs == drow[pl.ds(c, 1), :]
    live = (docs == before).astype(F32)
    tail = (docs == last).astype(F32)
    live_last = (last == before).astype(F32)
    return docs, same, live, tail, live_last


def conv_chunk(c, joined, dcol, taps, docs):
    start = pl.multiple_of(c * CH, CH)
    window = joined[pl.ds(start, CH + PAD), : taps.shape[1]].astype(F32)
    ids = dcol[pl.ds(start, CH + PAD), :]
    total = window[PAD:, :] * taps[3:4, :]
    for lag in (1, 2, 3):
        keep = (ids[PAD - lag : PAD - lag + CH, :] == docs).astype(F32)
        keep = jnp.concatenate([keep] * (taps.shape[1] // CH), axis=1)
        total = total + window[PAD - lag : PAD - lag + CH, :] * keep * taps[3 - lag : 4 - lag, :]
    return total


def raw_chunk(c, joined, taps):
    rows = pl.ds(pl.multiple_of(c * CH + PAD, PAD), CH)
    return joined[rows, taps.shape[1] :].astype(F32)


def bring(source, joined, sem):
    copy = pltpu.make_async_copy(source, joined.at[pl.ds(PAD, source.shape[0]), :], sem)
    copy.start()
    joined[pl.ds(0, PAD), :] = jnp.zeros((PAD, joined.shape[1]), joined.dtype)
    copy.wait()


def normal_parts(act):
    query, keys, values = act[:, :CH], act[:, CH : 2 * CH], act[:, 2 * CH :]
    q_scale = lax.rsqrt(jnp.sum(query * query, axis=-1, keepdims=True) + 1e-06)
    k_scale = lax.rsqrt(jnp.sum(keys * keys, axis=-1, keepdims=True) + 1e-06)
    return query * q_scale * CH**-0.5, keys * k_scale, values, q_scale, k_scale


def mixer_fwd_kernel(
    heads, chunks, source, dcol, drow, taps, gain,
    mixed, o_out, t_out, d_out, s_out,
    joined, q_s, k_s, u_s, w_s, p_s, sem,
):
    bring(source, joined, sem)
    row = lax.broadcasted_iota(jnp.int32, (CH, CH), 0)
    col = lax.broadcasted_iota(jnp.int32, (CH, CH), 1)

    def prepare(c, h, docs, same, live, act, raws):
        start = pl.multiple_of(c * CH, CH)
        rows = pl.ds(start, CH)
        query, keys, values, _, _ = normal_parts(act[:, h * 3 * CH : (h + 1) * 3 * CH])
        beta = sigmoid(raws[:, h : h + 1])
        inner = mm_nt(keys, keys)
        lower = jnp.where(same & (row > col), inner * beta, 0.0)
        inverse = unit_lower_inverse(lower, row, col, mm_fine)
        t_out[h, rows, :] = inverse
        both = mm(inverse, jnp.concatenate([values * beta, keys * (beta * live)], axis=1))
        u_s[h, rows, :] = both[:, :CH]
        w_s[h, rows, :] = both[:, CH:].astype(BF16)
        scores = jnp.where(same & (row >= col), mm_nt(query, keys), 0.0)
        p_s[h, rows, :] = scores.astype(BF16)
        q_s[h, rows, :] = (query * live).astype(BF16)
        k_s[h, rows, :] = keys

    def first(step, carry):
        for part in range(2):
            c = step * 2 + part
            docs, same, live, tail, live_last = chunk_masks(c, dcol, drow)
            conv = conv_chunk(c, joined, dcol, taps, docs)
            act = conv * sigmoid(conv)
            raws = raw_chunk(c, joined, taps)
            for h in range(heads):
                prepare(c, h, docs, same, live, act, raws)
        return carry

    lax.fori_loop(0, chunks // 2, first, 0)

    def second(c, states):
        rows = pl.ds(pl.multiple_of(c * CH, CH), CH)
        docs, same, live, tail, live_last = chunk_masks(c, dcol, drow)
        after = []
        for h in range(heads):
            state = states[h]
            s_out[h, rows, :] = state
            update = u_s[h, rows, :] - mm(w_s[h, rows, :], state)
            d_out[h, rows, :] = update
            after.append(state * live_last + mm_tn(k_s[h, rows, :] * tail, update))
        return tuple(after)

    zero = jnp.zeros((CH, CH), F32)
    lax.fori_loop(0, chunks, second, (zero,) * heads)

    def third(c, carry):
        rows = pl.ds(pl.multiple_of(c * CH, CH), CH)
        for h in range(heads):
            out = mm(
                jnp.concatenate([q_s[h, rows, :], p_s[h, rows, :]], axis=1),
                jnp.concatenate(
                    [s_out[h, rows, :].astype(BF16), d_out[h, rows, :].astype(BF16)], axis=0
                ),
            )
            o_out[h, rows, :] = out
            scale = lax.rsqrt(jnp.mean(out * out, axis=-1, keepdims=True) + 1e-05)
            mixed[rows, h * CH : (h + 1) * CH] = (out * scale * gain[...]).astype(BF16)
        return carry

    lax.fori_loop(0, chunks, third, 0)


def mixer_fwd(joined, dcol, drow, taps, gain):
    tokens, wide = joined.shape
    heads = wide // (3 * CH)
    chunks = tokens // CH
    square = jax.ShapeDtypeStruct((heads, tokens, CH), F32)
    return pl.pallas_call(
        functools.partial(mixer_fwd_kernel, heads, chunks),
        out_shape=(jax.ShapeDtypeStruct((tokens, heads * CH), BF16), square, square, square, square),
        in_specs=[pl.BlockSpec(memory_space=pl.ANY)] + [pl.BlockSpec(memory_space=pltpu.VMEM)] * 4,
        out_specs=(pl.BlockSpec(memory_space=pltpu.VMEM),) * 5,
        scratch_shapes=[
            pltpu.VMEM((tokens + PAD, wide), BF16),
            pltpu.VMEM((heads, tokens, CH), BF16),
            pltpu.VMEM((heads, tokens, CH), F32),
            pltpu.VMEM((heads, tokens, CH), F32),
            pltpu.VMEM((heads, tokens, CH), BF16),
            pltpu.VMEM((heads, tokens, CH), BF16),
            pltpu.SemaphoreType.DMA,
        ],
        compiler_params=pltpu.CompilerParams(vmem_limit_bytes=48 << 20),
        name="mixer_fwd",
    )(joined, dcol, drow, taps, gain)


def mixer_bwd_kernel(
    heads, chunks, source, dcol, drow, taps, gain, grad, o_in, t_in, d_in, s_in,
    dj_out,
    joined, e_s, f_s, w_s, x_s, ds_s, go_s, dc_s, sem,
):
    bring(source, joined, sem)
    row = lax.broadcasted_iota(jnp.int32, (CH, CH), 0)
    col = lax.broadcasted_iota(jnp.int32, (CH, CH), 1)
    width = 3 * CH

    def revive(c):
        docs, same, live, tail, live_last = chunk_masks(c, dcol, drow)
        conv = conv_chunk(c, joined, dcol, taps, docs)
        raws = raw_chunk(c, joined, taps)
        return docs, same, live, tail, live_last, conv, raws

    def first(c, carry):
        docs, same, live, tail, live_last, conv, raws = revive(c)
        act = conv * sigmoid(conv)
        rows = pl.ds(pl.multiple_of(c * CH, CH), CH)
        for h in range(heads):
            query, keys, values, _, _ = normal_parts(act[:, h * width : (h + 1) * width])
            beta = sigmoid(raws[:, h : h + 1])
            out = o_in[h, rows, :]
            weighted = grad[rows, h * CH : (h + 1) * CH].astype(F32) * gain[...]
            scale = lax.rsqrt(jnp.mean(out * out, axis=-1, keepdims=True) + 1e-05)
            grad_o = scale * weighted - out * (
                scale * scale * scale * jnp.mean(weighted * out, axis=-1, keepdims=True)
            )
            go_s[h, rows, :] = grad_o
            scores = jnp.where(same & (row >= col), mm_nt(query, keys), 0.0)
            ef = mm_tn(jnp.concatenate([scores, query * live], axis=1), grad_o)
            e_s[h, rows, :] = ef[:CH]
            f_s[h, rows, :] = ef[CH:]
            w_s[h, rows, :] = mm(t_in[h, rows, :], keys * (beta * live)).astype(BF16)
            x_s[h, rows, :] = keys * tail
        return carry

    lax.fori_loop(0, chunks, first, 0)

    def second(step, states):
        c = chunks - 1 - step
        rows = pl.ds(pl.multiple_of(c * CH, CH), CH)
        docs, same, live, tail, live_last = chunk_masks(c, dcol, drow)
        before = []
        for h in range(heads):
            state = states[h]
            ds_s[h, rows, :] = state
            grad_update = e_s[h, rows, :] + mm(x_s[h, rows, :], state)
            x_s[h, rows, :] = grad_update
            before.append(
                state * live_last + f_s[h, rows, :] - mm_tn(w_s[h, rows, :], grad_update)
            )
        return tuple(before)

    zero = jnp.zeros((CH, CH), F32)
    lax.fori_loop(0, chunks, second, (zero,) * heads)

    dc_s[pl.ds(chunks * CH, PAD), :] = jnp.zeros((PAD, heads * width), F32)

    def third(c, carry):
        docs, same, live, tail, live_last, conv, raws = revive(c)
        gate = sigmoid(conv)
        act = conv * gate
        slope = gate * (1.0 + conv * (1.0 - gate))
        rows = pl.ds(pl.multiple_of(c * CH, CH), CH)
        lane = lax.broadcasted_iota(jnp.int32, (CH, CH), 1)
        grad_raw = jnp.zeros((CH, CH), F32)
        for h in range(heads):
            part = act[:, h * width : (h + 1) * width]
            query, keys, values, q_scale, k_scale = normal_parts(part)
            beta = sigmoid(raws[:, h : h + 1])
            state, update, state_grad = s_in[h, rows, :], d_in[h, rows, :], ds_s[h, rows, :]
            grad_o = go_s[h, rows, :]
            grad_target = mm_tn(t_in[h, rows, :], x_s[h, rows, :])
            pair = mm_nt(jnp.concatenate([grad_target, grad_o], axis=0), update)
            grad_lower = jnp.where(same & (row > col), -pair[:CH], 0.0)
            grad_scores = jnp.where(same & (row >= col), pair[CH:], 0.0)
            inner = mm_nt(keys, keys)
            recalled = mm(keys, state)
            grad_beta = jnp.sum(
                grad_lower * inner + grad_target * (values - live * recalled),
                axis=-1,
                keepdims=True,
            )
            grad_inner = grad_lower * beta
            back = mm_nt(
                jnp.concatenate([grad_o * live, -grad_target * (beta * live)], axis=0), state
            )
            grad_query = back[:CH] + mm(grad_scores, keys)
            grad_keys = (
                back[CH:]
                + mm_tn(
                    jnp.concatenate([grad_scores, grad_inner], axis=0),
                    jnp.concatenate([query, keys], axis=0),
                )
                + mm(grad_inner, keys)
                + mm_nt(update * tail, state_grad)
            )
            grad_values = grad_target * beta
            raw_q, raw_k = part[:, :CH], part[:, CH : 2 * CH]
            grad_query = grad_query * CH**-0.5
            grad_q = q_scale * grad_query - raw_q * (
                q_scale * q_scale * q_scale * jnp.sum(grad_query * raw_q, axis=-1, keepdims=True)
            )
            grad_k = k_scale * grad_keys - raw_k * (
                k_scale * k_scale * k_scale * jnp.sum(grad_keys * raw_k, axis=-1, keepdims=True)
            )
            dc_s[rows, h * width : (h + 1) * width] = (
                jnp.concatenate([grad_q, grad_k, grad_values], axis=1)
                * slope[:, h * width : (h + 1) * width]
            )
            grad_raw = jnp.where(lane == h, grad_beta * beta * (1.0 - beta), grad_raw)
        dj_out[rows, heads * width :] = grad_raw.astype(BF16)
        return carry

    lax.fori_loop(0, chunks, third, 0)

    def fourth(c, carry):
        start = pl.multiple_of(c * CH, CH)
        rows = pl.ds(start, CH)
        window = dc_s[pl.ds(start, CH + PAD), :]
        ids = dcol[pl.ds(start + PAD, CH + PAD), :]
        total = window[:CH] * taps[3:4, :]
        for lag in (1, 2, 3):
            keep = (ids[lag : lag + CH] == ids[:CH]).astype(F32)
            keep = jnp.concatenate([keep] * (heads * 3), axis=1)
            total = total + window[lag : lag + CH] * keep * taps[3 - lag : 4 - lag, :]
        dj_out[rows, : heads * width] = total.astype(BF16)
        return carry

    lax.fori_loop(0, chunks, fourth, 0)


def mixer_bwd(joined, dcol, drow, taps, gain, grad, o, t, d, s):
    tokens, wide = joined.shape
    heads = wide // (3 * CH)
    chunks = tokens // CH
    square = (heads, tokens, CH)
    return pl.pallas_call(
        functools.partial(mixer_bwd_kernel, heads, chunks),
        out_shape=jax.ShapeDtypeStruct((tokens, wide), BF16),
        in_specs=[pl.BlockSpec(memory_space=pl.ANY)] + [pl.BlockSpec(memory_space=pltpu.VMEM)] * 9,
        out_specs=pl.BlockSpec(memory_space=pltpu.VMEM),
        scratch_shapes=[
            pltpu.VMEM((tokens + PAD, wide), BF16),
            pltpu.VMEM(square, F32),
            pltpu.VMEM(square, F32),
            pltpu.VMEM(square, BF16),
            pltpu.VMEM(square, F32),
            pltpu.VMEM(square, F32),
            pltpu.VMEM(square, F32),
            pltpu.VMEM((tokens + PAD, heads * 3 * CH), F32),
            pltpu.SemaphoreType.DMA,
        ],
        compiler_params=pltpu.CompilerParams(vmem_limit_bytes=48 << 20),
        name="mixer_bwd",
    )(joined, dcol, drow, taps, gain, grad, o, t, d, s)

MESH = pl.DeviceIdType.MESH
SIDE = 128


class Line:
    def __init__(self, send_sems, recv_sems, local_sems):
        self.send_sems, self.recv_sems, self.local_sems = send_sems, recv_sems, local_sems
        self.used, self.used_local = 0, 0

    def make(self, src, dst, device):
        at = self.used
        self.used += 1
        return pltpu.make_async_remote_copy(
            src_ref=src, dst_ref=dst, send_sem=self.send_sems.at[at],
            recv_sem=self.recv_sems.at[at], device_id=device, device_id_type=MESH,
        )

    def send(self, src, dst, device):
        copy = self.make(src, dst, device)
        copy.start()
        return copy

    def local(self, src, dst):
        at = self.used_local
        self.used_local += 1
        copy = pltpu.make_async_copy(src, dst, self.local_sems.at[at])
        copy.start()
        return copy


def seq_places():
    s = lax.axis_index("seq")
    x, core = s // 2, lax.rem(s, 2)
    there = lambda d: lax.rem(x + d, 4) * 2 + core
    return s, x * 2 + 1 - core, there(1), there(3), there(2)


def greet(seq_peers, plane_peers):
    barrier = pltpu.get_barrier_semaphore()
    for p in seq_peers:
        pl.semaphore_signal(barrier, inc=1, device_id={"seq": p}, device_id_type=MESH)
    for p in plane_peers:
        pl.semaphore_signal(barrier, inc=1, device_id={"fsdp": p}, device_id_type=MESH)
    pl.semaphore_wait(barrier, len(seq_peers) + len(plane_peers))


class RingGather:
    def __init__(self, line, block, out):
        self.line, self.block, self.out = line, block, out
        half = block.shape[0] // 2
        self.low, self.high = pl.ds(0, half), pl.ds(half, half)

    def pass_on(self, s, rows, peer):
        return self.line.send(self.out.at[s, rows], self.out.at[s, rows], {"seq": peer})

    def start(self):
        s, partner, right, left, far = seq_places()
        send = lambda rows, p: self.line.send(
            self.block.at[rows], self.out.at[s, rows], {"seq": p}
        )
        self.a0, self.b0 = send(self.low, right), send(self.high, left)
        self.a1, self.b1 = send(self.high, right), send(self.low, left)
        self.p = self.line.send(self.block, self.out.at[s], {"seq": partner})
        self.own = self.line.local(self.block, self.out.at[s])

    def middle(self):
        s, partner, right, left, far = seq_places()
        self.a0.wait_recv()
        self.f0 = self.pass_on(left, self.low, right)
        self.g = [self.pass_on(left, self.low, partner)]
        self.b0.wait_recv()
        self.f1 = self.pass_on(right, self.high, left)
        self.g.append(self.pass_on(right, self.high, partner))
        self.a1.wait_recv()
        self.g.append(self.pass_on(left, self.high, partner))
        self.b1.wait_recv()
        self.g.append(self.pass_on(right, self.low, partner))

    def finish(self):
        s, partner, right, left, far = seq_places()
        self.f0.wait_recv()
        self.g.append(self.pass_on(far, self.low, partner))
        self.f1.wait_recv()
        self.g.append(self.pass_on(far, self.high, partner))
        for copy in (self.a0, self.b0, self.a1, self.b1, self.f0, self.f1):
            copy.wait_send()
        for copy in [self.p] + self.g:
            copy.wait()
        self.own.wait()


RING_COPIES = 13


def plane_places():
    f = lax.axis_index("fsdp")
    return f, f // 4, lax.rem(f, 4)


class PlaneGather:
    COPIES = 30

    def __init__(self, line, place):
        self.line, self.place = line, place

    def to(self, y, z):
        return lax.rem(y, 4) * 4 + lax.rem(z, 4)

    def first(self):
        f, y, z = plane_places()
        self.one = []
        for half in (0, 1):
            ref = self.place(f, half)
            row = []
            for d in (1, 3, 2):
                peer = self.to(y, z + d) if half == 0 else self.to(y + d, z)
                row.append(self.line.send(ref, ref, {"fsdp": peer}))
            self.one.append(row)

    def second(self):
        f, y, z = plane_places()
        self.two = []
        for k, d in enumerate((0, 1, 3, 2)):
            for half in (0, 1):
                if k:
                    self.one[half][k - 1].wait_recv()
                source = self.to(y, z + 4 - d) if half == 0 else self.to(y + 4 - d, z)
                ref = self.place(source, half)
                for e in (1, 3, 2):
                    peer = self.to(y + e, z) if half == 0 else self.to(y, z + e)
                    self.two.append(self.line.send(ref, ref, {"fsdp": peer}))

    def finish(self):
        for row in self.one:
            for copy in row:
                copy.wait_send()
        for copy in self.two:
            copy.wait()


class Scatter:
    COPIES = 17

    def __init__(self, line, sources, source_block, into):
        self.line, self.sources = line, sources
        self.source_block, self.into = source_block, into

    def start(self):
        f, _, _ = plane_places()
        line = self.line
        self.at = line.used
        line.used += self.COPIES
        self.local_at = line.used_local
        line.used_local += 2
        for j, source in enumerate(self.sources):
            @pl.when(f == source)
            def _():
                for d in range(1, 16):
                    self.copy(j, d, lax.rem(f + d, 16)).start()
                self.keep(j).start()

    def copy(self, j, d, t):
        line = self.line
        return pltpu.make_async_remote_copy(
            src_ref=self.source_block(t), dst_ref=self.into(t, j),
            send_sem=line.send_sems.at[self.at + d], recv_sem=line.recv_sems.at[self.at + j],
            device_id={"fsdp": t}, device_id_type=MESH,
        )

    def keep(self, j):
        f, _, _ = plane_places()
        return pltpu.make_async_copy(
            self.source_block(f), self.into(f, j), self.line.local_sems.at[self.local_at + j]
        )

    def arrive(self):
        f, _, _ = plane_places()
        for j, source in enumerate(self.sources):
            @pl.when(f == source)
            def _():
                self.keep(j).wait()

            @pl.when(f != source)
            def _():
                ref = self.into(f, j)
                pltpu.make_async_remote_copy(
                    src_ref=ref, dst_ref=ref, send_sem=self.line.send_sems.at[self.at],
                    recv_sem=self.line.recv_sems.at[self.at + j],
                    device_id={"fsdp": lax.rem(f + 1, 16)}, device_id_type=MESH,
                ).wait_recv()

    def finish(self):
        f, _, _ = plane_places()
        for j, source in enumerate(self.sources):
            @pl.when(f == source)
            def _():
                for d in range(1, 16):
                    self.copy(j, d, lax.rem(f + d, 16)).wait_send()


def all_plane():
    f = lax.axis_index("fsdp")
    return [lax.rem(f + d, 16) for d in range(1, 16)]


def line_peers():
    f, y, z = plane_places()
    return [y * 4 + lax.rem(z + d, 4) for d in (1, 2, 3)] + [
        lax.rem(y + d, 4) * 4 + z for d in (1, 2, 3)
    ]


def sems(copies, local):
    return [
        pltpu.SemaphoreType.DMA((copies,)),
        pltpu.SemaphoreType.DMA((copies,)),
        pltpu.SemaphoreType.DMA((local,)),
    ]


ANY = pl.BlockSpec(memory_space=pl.ANY)
VMEM = pl.BlockSpec(memory_space=pltpu.VMEM)


def columns_place(out):
    rows = out.shape[0] // 2
    return lambda f, half: out.at[pl.ds(half * rows, rows), pl.ds(pl.multiple_of(f * 128, 128), 128)]


def block_of(ref, t):
    return ref.at[:, pl.ds(pl.multiple_of(t * 128, 128), 128)]


def start_kernel(
    payload, w_qkv, w_out, q_side, beta_side, out_side, everyone, wq, wo, send, recv, local
):
    s, partner, right, left, far = seq_places()
    f, _, _ = plane_places()
    greet([partner, right, left], all_plane())
    line = Line(send, recv, local)
    depth, width = w_qkv.shape
    scatter = Scatter(
        line, (2 * s, 2 * s + 1),
        lambda t: w_qkv.at[pl.ds(t * 128, 128), :],
        lambda t, j: wq.at[pl.ds(t * 128, 128), pl.ds(j * width, width)],
    )
    scatter.start()
    ring = RingGather(line, payload, everyone)
    ring.start()
    share = wo.shape[0]
    mine = line.local(w_out.at[pl.ds(s * share, share), :], block_of(wo, f))
    sides = [
        line.local(q_side, wq.at[pl.ds(depth, SIDE), :]),
        line.local(beta_side, wq.at[pl.ds(0, depth), pl.ds(2 * width, SIDE)]),
        line.local(out_side, wo.at[:, pl.ds(wo.shape[1] - SIDE, SIDE)]),
    ]
    qkv = PlaneGather(
        line,
        lambda t, half: wq.at[pl.ds(t * 128 + half * 64, 64), pl.ds(0, 2 * width)],
    )
    out = PlaneGather(line, columns_place(wo))
    scatter.arrive()
    qkv.first()
    mine.wait()
    out.first()
    ring.middle()
    qkv.second()
    out.second()
    ring.finish()
    for item in [scatter, qkv, out]:
        item.finish()
    for copy in sides:
        copy.wait()


def start_gather(payload, w_qkv, w_out, q_side, beta_side, out_side):
    seq, wide = lax.axis_size("seq"), payload.shape[1]
    copies = RING_COPIES + Scatter.COPIES + 2 * PlaneGather.COPIES
    return pl.pallas_call(
        start_kernel,
        out_shape=(
            jax.ShapeDtypeStruct((seq,) + payload.shape, BF16),
            jax.ShapeDtypeStruct((wide, q_side.shape[1]), BF16),
            jax.ShapeDtypeStruct((out_side.shape[0], wide), BF16),
        ),
        in_specs=[ANY] * 6,
        out_specs=(ANY,) * 3,
        scratch_shapes=sems(copies, 8),
        compiler_params=pltpu.CompilerParams(collective_id=0, has_side_effects=True),
        name="start_gather",
    )(payload, w_qkv, w_out, q_side, beta_side, out_side)


def feed_kernel(
    cot, gate_t, down, g_side, u_side, f_side, everyone, wg, wu, wd, send, recv, local
):
    s, partner, right, left, far = seq_places()
    f, _, _ = plane_places()
    greet([partner, right, left], all_plane())
    line = Line(send, recv, local)
    scatters = [
        Scatter(line, (source,), lambda t: block_of(gate_t, t), lambda t, j, o=o: block_of(o, t))
        for source, o in ((s, wg), (s + 8, wu))
    ]
    for item in scatters:
        item.start()
    ring = RingGather(line, cot, everyone)
    ring.start()
    share = wd.shape[0]
    mine = line.local(down.at[pl.ds(s * share, share), :], block_of(wd, f))
    last = pl.ds(wd.shape[1] - SIDE, SIDE)
    sides = [
        line.local(side, o.at[:, last]) for side, o in ((g_side, wg), (u_side, wu), (f_side, wd))
    ]
    gathers = [PlaneGather(line, columns_place(o)) for o in (wg, wu, wd)]
    for item, gather in zip(scatters, gathers):
        item.arrive()
        gather.first()
    mine.wait()
    gathers[2].first()
    ring.middle()
    for gather in gathers:
        gather.second()
    ring.finish()
    for item in scatters + gathers:
        item.finish()
    for copy in sides:
        copy.wait()


def feed_gather(cot, gate_t, down, g_side, u_side, f_side):
    seq, wide = lax.axis_size("seq"), cot.shape[1]
    copies = RING_COPIES + 2 * Scatter.COPIES + 3 * PlaneGather.COPIES
    weight = jax.ShapeDtypeStruct((g_side.shape[0], wide), BF16)
    return pl.pallas_call(
        feed_kernel,
        out_shape=(jax.ShapeDtypeStruct((seq,) + cot.shape, BF16), weight, weight, weight),
        in_specs=[ANY] * 6,
        out_specs=(ANY,) * 4,
        scratch_shapes=sems(copies, 10),
        compiler_params=pltpu.CompilerParams(collective_id=1, has_side_effects=True),
        name="feed_gather",
    )(cot, gate_t, down, g_side, u_side, f_side)


ADD_ROWS = 16


def add_rows(dst, sources, first, count):
    def step(i, carry):
        rows = pl.ds(pl.multiple_of(first + i * ADD_ROWS, ADD_ROWS), ADD_ROWS)
        total = None
        for source, offset in sources:
            at = pl.ds(pl.multiple_of(first - offset + i * ADD_ROWS, ADD_ROWS), ADD_ROWS)
            item = source[at, :].astype(F32)
            total = item if total is None else total + item
        dst[rows, :] = total.astype(dst.dtype)
        return carry

    lax.fori_loop(0, count // ADD_ROWS, step, 0)


class RingSum:
    COPIES = 10

    def __init__(self, line, partial, buffers):
        self.line, self.partial = line, partial
        self.own, self.stage, self.relay, self.away, self.back = buffers
        self.rows = partial.shape[1]
        self.half = self.rows // 2
        self.low, self.high = pl.ds(0, self.half), pl.ds(self.half, self.half)

    def start(self):
        s, partner, right, left, far = seq_places()
        twin = lambda p: p + partner - s
        self.near, self.kept = [], []
        for k, p in enumerate((far, right, left, s)):
            self.near.append(
                self.line.send(self.partial.at[twin(p)], self.stage.at[k], {"seq": partner})
            )
            self.kept.append(self.line.local(self.partial.at[p], self.own.at[k]))

    def ready(self, k):
        self.near[k].wait_recv()
        self.kept[k].wait()

    def go(self, src, dst, peer):
        return self.line.send(src, dst, {"seq": peer})

    def middle(self):
        s, partner, right, left, far = seq_places()
        half = self.half
        pair = lambda k: [(self.own.at[k], 0), (self.stage.at[k], 0)]
        away, relay, back = self.away, self.relay, self.back
        self.ready(0)
        add_rows(away.at[0], pair(0), 0, half)
        self.r0 = self.go(away.at[0, self.low], relay.at[0], right)
        add_rows(away.at[0], pair(0), half, half)
        self.r1 = self.go(away.at[0, self.high], relay.at[1], left)
        self.ready(1)
        add_rows(away.at[1], pair(1), half, half)
        self.s0 = self.go(away.at[1, self.high], back.at[0, self.high], right)
        self.ready(2)
        add_rows(away.at[2], pair(2), 0, half)
        self.s1 = self.go(away.at[2, self.low], back.at[1, self.low], left)

    def last(self):
        s, partner, right, left, far = seq_places()
        half = self.half
        pair = lambda k: [(self.own.at[k], 0), (self.stage.at[k], 0)]
        away, relay, back = self.away, self.relay, self.back
        self.r0.wait_recv()
        add_rows(away.at[1], pair(1) + [(relay.at[0], 0)], 0, half)
        self.s2 = self.go(away.at[1, self.low], back.at[0, self.low], right)
        self.r1.wait_recv()
        add_rows(away.at[2], pair(2) + [(relay.at[1], half)], half, half)
        self.s3 = self.go(away.at[2, self.high], back.at[1, self.high], left)

    def finish(self, total):
        self.ready(3)
        for copy in (self.s0, self.s1, self.s2, self.s3):
            copy.wait_recv()
        add_rows(
            total,
            [(self.own.at[3], 0), (self.stage.at[3], 0), (self.back.at[0], 0), (self.back.at[1], 0)],
            0, self.rows,
        )
        for copy in self.near + [self.r0, self.r1, self.s0, self.s1, self.s2, self.s3]:
            copy.wait_send()


def sum_buffers(rows, width):
    return [
        pltpu.VMEM((4, rows, width), BF16),
        pltpu.VMEM((4, rows, width), BF16),
        pltpu.VMEM((2, rows // 2, width), BF16),
        pltpu.VMEM((3, rows, width), BF16),
        pltpu.VMEM((2, rows, width), BF16),
    ]


MID_ROWS = 32


def by_rows(rows, step):
    def run(i, carry):
        step(pl.ds(pl.multiple_of(i * MID_ROWS, MID_ROWS), MID_ROWS))
        return carry

    lax.fori_loop(0, rows // MID_ROWS, run, 0)


def norm_back_rows(values, gain, grad):
    scale = lax.rsqrt(jnp.mean(values * values, axis=-1, keepdims=True) + 1e-05)
    weighted = grad * gain
    return scale * weighted - values * (
        scale * scale * scale * jnp.mean(weighted * values, axis=-1, keepdims=True)
    )


def branch_kernel(
    partial, tokens, up, gain, down, middle, everyone,
    payload, total, own, stage, relay, away, back, send, recv, local,
):
    s, partner, right, left, far = seq_places()
    greet([partner, right, left], [])
    line = Line(send, recv, local)
    ring = RingSum(line, partial, (own, stage, relay, away, back))
    ring.start()
    ring.middle()
    ring.last()
    ring.finish(total)
    width = tokens.shape[1]

    def step(rows):
        inner = total[rows, width:].astype(BF16)
        value = tokens[rows, :].astype(F32) + (total[rows, :width] + mm(inner, up[...]))
        middle[rows, :] = value
        scale = lax.rsqrt(jnp.mean(value * value, axis=-1, keepdims=True) + 1e-05)
        normed = (value * scale * gain[...]).astype(BF16)
        payload[rows, :width] = normed
        payload[rows, width:] = (inner.astype(F32) + mm_nt(normed, down[...])).astype(BF16)

    by_rows(tokens.shape[0], step)
    gather = RingGather(line, payload, everyone)
    gather.start()
    gather.middle()
    gather.finish()


def back_kernel(
    partial, cot, values, down, gain, up, grad_middle, everyone,
    payload, total, own, stage, relay, away, back, send, recv, local,
):
    s, partner, right, left, far = seq_places()
    greet([partner, right, left], [])
    line = Line(send, recv, local)
    ring = RingSum(line, partial, (own, stage, relay, away, back))
    ring.start()
    ring.middle()
    ring.last()
    ring.finish(total)
    width = cot.shape[1]

    def step(rows):
        inner = total[rows, width:].astype(BF16)
        grad = total[rows, :width] + mm(inner, down[...])
        result = cot[rows, :].astype(F32) + norm_back_rows(values[rows, :], gain[...], grad)
        grad_middle[rows, :] = result
        low = result.astype(BF16)
        payload[rows, :width] = low
        payload[rows, width:] = (inner.astype(F32) + mm_nt(low, up[...])).astype(BF16)

    by_rows(cot.shape[0], step)
    gather = RingGather(line, payload, everyone)
    gather.start()
    gather.middle()
    gather.finish()


def sum_and_gather(kernel, cid, name, partial, operands):
    seq, rows, wide = partial.shape
    return pl.pallas_call(
        kernel,
        out_shape=(
            jax.ShapeDtypeStruct((rows, wide - SIDE), F32),
            jax.ShapeDtypeStruct((seq, rows, wide), BF16),
        ),
        in_specs=[ANY] + [VMEM] * len(operands),
        out_specs=(VMEM, ANY),
        scratch_shapes=[pltpu.VMEM((rows, wide), BF16), pltpu.VMEM((rows, wide), F32)]
        + sum_buffers(rows, wide)
        + sems(RingSum.COPIES + RING_COPIES, 5),
        compiler_params=pltpu.CompilerParams(
            collective_id=cid, has_side_effects=True, vmem_limit_bytes=48 << 20
        ),
        name=name,
    )(partial, *operands)


def layer_kernel(
    partial, values, up, layer_out, inner_out,
    total, own, stage, relay, away, back, send, recv, local,
):
    s, partner, right, left, far = seq_places()
    greet([partner, right, left], [])
    line = Line(send, recv, local)
    ring = RingSum(line, partial, (own, stage, relay, away, back))
    ring.start()
    ring.middle()
    ring.last()
    ring.finish(total)
    width = values.shape[1]

    def step(rows):
        inner = total[rows, width:].astype(BF16)
        inner_out[rows, :] = inner
        layer_out[rows, :] = (
            values[rows, :] + (total[rows, :width] + mm(inner, up[...]))
        ).astype(BF16)

    by_rows(values.shape[0], step)


def input_kernel(
    partial, tokens, grad_middle, down, gain, input_grad, inner_out,
    total, own, stage, relay, away, back, send, recv, local,
):
    s, partner, right, left, far = seq_places()
    greet([partner, right, left], [])
    line = Line(send, recv, local)
    ring = RingSum(line, partial, (own, stage, relay, away, back))
    ring.start()
    ring.middle()
    ring.last()
    ring.finish(total)
    width = tokens.shape[1]

    def step(rows):
        inner = total[rows, width:].astype(BF16)
        inner_out[rows, :] = inner
        grad = total[rows, :width] + mm(inner, down[...])
        input_grad[rows, :] = (
            grad_middle[rows, :]
            + norm_back_rows(tokens[rows, :].astype(F32), gain[...], grad)
        ).astype(BF16)

    by_rows(tokens.shape[0], step)


def sum_only(kernel, cid, name, partial, operands):
    seq, rows, wide = partial.shape
    return pl.pallas_call(
        kernel,
        out_shape=(
            jax.ShapeDtypeStruct((rows, wide - SIDE), BF16),
            jax.ShapeDtypeStruct((rows, SIDE), BF16),
        ),
        in_specs=[ANY] + [VMEM] * len(operands),
        out_specs=(VMEM, VMEM),
        scratch_shapes=[pltpu.VMEM((rows, wide), F32)]
        + sum_buffers(rows, wide)
        + sems(RingSum.COPIES, 4),
        compiler_params=pltpu.CompilerParams(
            collective_id=cid, has_side_effects=True, vmem_limit_bytes=48 << 20
        ),
        name=name,
    )(partial, *operands)


BOTH = ("fsdp", "seq")


def rms_scale(values, gain):
    return values * lax.rsqrt(jnp.mean(values * values, axis=-1, keepdims=True) + 1e-05) * gain


def norm_back(values, gain, grad):
    scale = lax.rsqrt(jnp.mean(values * values, axis=-1, keepdims=True) + 1e-05)
    weighted = grad * gain
    return scale * weighted - values * scale * scale * scale * jnp.mean(
        weighted * values, axis=-1, keepdims=True
    )


def dot(a, b):
    return jnp.dot(a, b, preferred_element_type=F32)


def dot_nt(a, b):
    return lax.dot_general(a, b, (((1,), (1,)), ((), ())), preferred_element_type=F32)


def dot_tn(a, b):
    return lax.dot_general(a, b, (((0,), (0,)), ((), ())), preferred_element_type=F32)


def body(
    tokens,
    segments,
    adapter_index,
    attn_gain,
    w_qkv,
    w_beta,
    conv_weight,
    head_gain,
    w_out,
    ffn_gain,
    w_gateup,
    w_down,
    qkv_down,
    qkv_up,
    mixout_down,
    mixout_up,
    gateup_down,
    gateup_up,
    ffnout_down,
    ffnout_up,
    cotangent,
):
    seq = lax.axis_size("seq")
    s = lax.axis_index("seq")
    width = tokens.shape[1]
    heads = w_beta.shape[1] // seq
    rank = qkv_down.shape[2]
    count = qkv_down.shape[0]
    hidden_width = w_down.shape[0]
    share = hidden_width // seq
    columns = heads * 3 * CH
    outs = heads * CH
    which = adapter_index[0]
    docs = segments[0]
    length = docs.shape[0]

    def pick(array):
        return lax.dynamic_index_in_dim(array, which, 0, keepdims=False)

    def mine(array, size, axis):
        return lax.dynamic_slice_in_dim(array, s * size, size, axis)

    def lanes(array, first=0):
        return jnp.pad(array, ((0, 0), (first, SIDE - first - array.shape[1])))

    def lines(array, first=0):
        return jnp.pad(array, ((first, SIDE - first - array.shape[0]), (0, 0)))

    q_down, q_up = pick(qkv_down), mine(pick(qkv_up), columns, 1)
    m_down, m_up = mine(pick(mixout_down), outs, 0), pick(mixout_up)
    g_down, g_up = pick(gateup_down), pick(gateup_up)
    gate_up = mine(g_up[:, :hidden_width], share, 1)
    upper_up = mine(g_up[:, hidden_width:], share, 1)
    f_down, f_up = mine(pick(ffnout_down), share, 0), pick(ffnout_up)
    beta_w = mine(w_beta, heads, 1)

    base = tokens.astype(F32)
    normed_own = rms_scale(base, attn_gain).astype(BF16)
    payload = jnp.concatenate([normed_own, dot(normed_own, lanes(q_down, rank)).astype(BF16)], axis=1)
    normed, wq, wo = start_gather(
        payload, w_qkv, w_out,
        jnp.pad(q_up, ((rank, SIDE - 2 * rank), (0, SIDE))), lanes(beta_w), lanes(m_down),
    )
    normed = normed.reshape(length, -1)
    joined = dot(normed, wq).astype(BF16)

    ids = jnp.pad(docs, (PAD, PAD), constant_values=-1)
    dcol = jnp.broadcast_to(ids[:, None], (length + 2 * PAD, CH))
    drow = docs.reshape(length // CH, CH)
    taps = mine(conv_weight, heads, 1).reshape(-1, columns)
    fixed = (joined, dcol, drow, taps, head_gain[None])
    mixed, o_kept, t_kept, d_kept, s_kept = mixer_fwd(*fixed)

    payload = jnp.concatenate([cotangent, dot_nt(cotangent, lines(f_up)).astype(BF16)], axis=1)
    cot, wg, wu, wd = feed_gather(
        payload, w_gateup.T, w_down,
        lanes(gate_up.T, rank), lanes(upper_up.T, rank), lanes(f_down),
    )
    cot = cot.reshape(length, -1)

    blocks = lambda partial: partial.astype(BF16).reshape(seq, -1, partial.shape[1])
    middle, normed2 = sum_and_gather(
        branch_kernel, 2, "branch", blocks(dot(mixed, wo)),
        (tokens, lines(m_up), ffn_gain[None], lines(g_down.T, rank)),
    )
    normed2 = normed2.reshape(length, -1)

    gate = dot_nt(normed2, wg)
    upper = dot_nt(normed2, wu)
    sigma = jax.nn.sigmoid(gate)
    hidden = (gate * sigma * upper).astype(BF16)
    layer_out, f_inner = sum_only(
        layer_kernel, 3, "layer", blocks(dot(hidden, wd)), (middle, lines(f_up))
    )

    grad_hidden = dot_nt(cot, wd)
    grad_gate = (grad_hidden * upper * sigma * (1.0 + gate * (1.0 - sigma))).astype(BF16)
    grad_upper = (grad_hidden * gate * sigma).astype(BF16)
    grad_middle, branch = sum_and_gather(
        back_kernel, 4, "back", blocks(dot(grad_gate, wg) + dot(grad_upper, wu)),
        (cotangent, middle, lines(g_down.T, rank), ffn_gain[None], lines(m_up)),
    )
    branch = branch.reshape(length, -1)

    grad_mixed = dot_nt(branch, wo).astype(BF16)
    grad_joined = mixer_bwd(*fixed, grad_mixed, o_kept, t_kept, d_kept, s_kept)
    input_grad, q_dinner = sum_only(
        input_kernel, 5, "input", blocks(dot_nt(grad_joined, wq)),
        (tokens, grad_middle, lines(q_down.T, rank), attn_gain[None]),
    )

    inner = lax.all_gather(
        jnp.concatenate([f_inner[:, :rank], q_dinner[:, rank : 2 * rank]], axis=1),
        "seq", axis=0, tiled=True,
    )
    low = lambda rows: rows[:, width : width + rank]
    high = lambda rows: rows[:, width + rank : width + 2 * rank]
    part = lambda rows: mine(rows, width // seq, 1)
    early = (
        dot_tn(high(normed2), grad_gate),
        dot_tn(high(normed2), grad_upper),
        dot_tn(low(cot), hidden),
        dot_tn(low(branch), mixed),
        dot_tn(low(normed2), part(branch)),
        dot_tn(high(branch), part(normed2)),
    )
    late = (
        dot_tn(high(normed), grad_joined[:, :columns]),
        dot_tn(inner[:, :rank], part(cot)),
        dot_tn(inner[:, rank:], part(normed)),
    )

    match = (lax.all_gather(adapter_index, "fsdp", axis=0, tiled=True)[None, :] == jnp.arange(count, dtype=jnp.int32)[:, None]).astype(F32)

    def total(pieces):
        sizes = [p.shape[1] for p in pieces]
        piece = jnp.concatenate(pieces, axis=1).astype(BF16)
        plane = lax.all_gather(piece, "fsdp", axis=0)
        by_adapter = jnp.einsum("af,frn->arn", match, plane.astype(F32)).astype(BF16)
        whole = lax.all_gather(by_adapter, "seq", axis=0)
        result, at = [], 0
        for size in sizes:
            item = whole[..., at : at + size].astype(F32)
            result.append(jnp.transpose(item, (1, 2, 0, 3)).reshape(count, rank, seq * size))
            at += size
        return result

    gate_g, upper_g, ffdown_g, mixdown_g, mixup_g, gudown_g = total(early)
    qkvup_g, ffup_g, qkvdown_g = total(late)
    flip = lambda v: jnp.swapaxes(v, 1, 2)
    return (
        layer_out,
        input_grad,
        flip(qkvdown_g),
        qkvup_g,
        flip(mixdown_g),
        mixup_g,
        flip(gudown_g),
        jnp.concatenate([gate_g, upper_g], axis=2),
        flip(ffdown_g),
        ffup_g,
    )


def solution(mesh):
    tokens, columns = P(BOTH, None), P(None, "fsdp")
    placed = (
        tokens, P("fsdp", None), P("fsdp"), P(), columns, P(), P(), P(), columns, P(), columns,
        columns, P(), P(), P(), P(), P(), P(), P(), P(), tokens,
    )
    return jax.shard_map(
        body,
        mesh=mesh,
        in_specs=placed,
        out_specs=(tokens, tokens) + (P(),) * 8,
        check_vma=False,
    )
```

time: 1580 us -> 635 us (0.40); the launches traced: 1560 us -> 630 us
  other arithmetic: 456 us -> 22.1 us
  Pallas kernels: 0 us -> 360 us
  matrix products: 426 us -> 83.6 us
  waiting for transfers between devices: 364 us -> 58.1 us
  local copies, waits for them, and re-layouts: 262 us -> 50.1 us
  blocking collectives: 0 us -> 41.1 us
  starting transfers between devices: 30.9 us -> 0.12 us
    another operation x161 -> x0, other arithmetic: 370 us -> none  [the longest x112 341 us: delta_block(): jax.scipy.linalg.solve_triangular(lower, target, lower=True, unit_diagona...]
    pallas_call x0 -> x8, Pallas kernels: none -> 360 us  [the longest x2 105 us: sum_and_gather(): pl.pallas_call(kernel, out_shape=(jax.ShapeDtypeStruct((rows, wide - SIDE...]
    dot_general x386 -> x23, matrix products: 384 us -> 83.6 us  [the longest x6 38.3 us: dot(): return jnp.dot(a, b, preferred_element_type=F32)]
    psum x1 -> x0, waiting for transfers between devices: 175 us -> none  [body(): lax.psum((spread * grad_qkvdown[None], spread * grad_qkvup[None], spread...]
    all_gather x4 -> x3, waiting for transfers between devices: 158 us -> 58.1 us  [the longest x2 58 us: total(): whole = lax.all_gather(by_adapter, 'seq', axis=0)]
    squeeze x96 -> x1, local copies, waits for them, and re-layouts: 87.5 us -> 0.88 us  [pick(): return lax.dynamic_index_in_dim(array, which, 0, keepdims=False)]
    another operation x64 -> x0, matrix products: 41.8 us -> none  [delta_block(): jax.scipy.linalg.solve_triangular(lower, target, lower=True, unit_diagona...]
    slice x66 -> x4, local copies, waits for them, and re-layouts: 39.1 us -> 2.2 us  [the longest x1 2 us: body(): upper_up = mine(g_up[:, hidden_width:], share, 1)]
  transfers between devices with their start and end apart: 11 -> 3, of which waited for: 6 -> 2; matrix products, arithmetic and copies ran while one was open for 35% -> 7% of each run, Pallas kernels for 0% -> 12%
where the time goes in v1:
time: 635 us; the launch traced here: 630 us
  Pallas kernels  360 us (57%)
  matrix products  83.6 us (13%)
  waiting for transfers between devices  58.1 us (9%)
  local copies, waits for them, and re-layouts  50.1 us (8%)
  blocking collectives  41.1 us (6%)
  other arithmetic  22.1 us (3%)
  between operations  15.4 us (2%)
    pallas_call x2, Pallas kernels, sum_and_gather(): pl.pallas_call(kernel, out_shape=(jax.ShapeDtypeStruct((rows, wide - SIDE...  105 us
    pallas_call x1, Pallas kernels, feed_gather(): pl.pallas_call(feed_kernel, out_shape=(jax.ShapeDtypeStruct((seq,) + cot....  82.8 us
    all_gather x2, waiting for transfers between devices, total(): whole = lax.all_gather(by_adapter, 'seq', axis=0)  58 us
    pallas_call x1, Pallas kernels, start_gather(): pl.pallas_call(start_kernel, out_shape=(jax.ShapeDtypeStruct((seq,) + pay...  57 us
    pallas_call x2, Pallas kernels, sum_only(): pl.pallas_call(kernel, out_shape=(jax.ShapeDtypeStruct((rows, wide - SIDE...  53.3 us
    pallas_call x1, Pallas kernels, mixer_fwd(): pl.pallas_call(functools.partial(mixer_fwd_kernel, heads, chunks), out_sh...  38.7 us
    dot_general x6, matrix products, dot(): return jnp.dot(a, b, preferred_element_type=F32)  38.3 us
    dot_general x6, matrix products, dot_nt(): lax.dot_general(a, b, (((1,), (1,)), ((), ())), preferred_element_type=F32)  29.2 us
  transfers between devices with their start and end apart: 3, of which 2 were waited for; matrix products, arithmetic and copies ran while one was open for 7% of the time, Pallas kernels for 12%

profile of v1, /device:TPU:1, one launch (start us, length us, event | category | flops | bytes accessed | tf_op | source)
XLA Modules:
  0.0 630.5 jit_solution(956502861857446728)
XLA Ops:
  23.8 2.8 copy.69
  30.3 57.0 %start_gather.1 = (bf16[8,128,2176]{2,1,0:T(8,128)(2,1)}, bf16[2176,896]{1,0:T(8,128)(2,1)}, bf16[256,2176]{1,0:T(8,128)(2,1)}) custom-call(bf16[128,2176]{1,0:T(8,128)(2,1)} %pad_maximum_fusion.payload, bf16[2048,384]{1,0:T(8,128)(2,1)} %w_qkv.1, bf16[2048,128]{1,0:T(8,128)(2,1)} %w_out.1, bf16[128,896]{1,0:T(8,128)(2,1)} %pad.49.q_side, ...), custom_call_target="tpu_custom_call" | custom-call | tf_op jit(solution)/shard_map/start_gather/pallas_call | solution.py:639
  87.3 8.8 %convolution_convert_fusion.5.source = bf16[1024,896]{1,0:T(8,128)(2,1)} fusion(bf16[1024,2176]{1,0:T(8,128)(2,1)} %bitcast.174, bf16[2176,896]{1,0:T(8,128)(2,1)} %get-tuple-element.31), kind=kOutput, calls=%fused_computation.13 | convolution fusion | flops 3993894912 | bytes 10190848 | tf_op jit(solution)/shard_map/dot_general | solution.py:987
  96.3 38.7 %mixer_fwd.1 = (bf16[1024,256]{1,0:T(8,128)(2,1)S(1)}, f32[2,1024,128]{2,1,0:T(8,128)S(1)}, f32[2,1024,128]{2,1,0:T(8,128)S(1)}, f32[2,1024,128]{2,1,0:T(8,128)S(1)}, f32[2,1024,128]{2,1,0:T(8,128)S(1)}) custom-call(bf16[1024,896]{1,0:T(8,128)(2,1)} %convolution_convert_fusion.5.source, s32[1056,128]{1,0:T(8,128)S(1)} %broadcast_in_dim.8.dcol, ...), custom_call_target="tpu_custom_call" | custom-call | tf_op jit(solution)/shard_map/mixer_fwd/pallas_call | solution.py:183
  135.1 3.6 convolution_convert_fusion.2
  138.7 49.7 %branch.1 = (f32[128,2048]{1,0:T(8,128)S(1)}, bf16[8,128,2176]{2,1,0:T(8,128)(2,1)}) custom-call(bf16[8,128,2176]{2,1,0:T(8,128)(2,1)} %bitcast.148, bf16[128,2048]{1,0:T(8,128)(2,1)S(1)} %copy-done.2, bf16[128,2048]{1,0:T(8,128)(2,1)S(1)} %pad.53.up, f32[1,2048]{1,0:T(1,128)S(1)} %bitcast.144, bf16[128,2048]{1,0:T(8,128)(2,1)S(1)} %pad.54.down), custom_call_target="tpu_custom_call" | custom-call | tf_op jit(solution)/shard_map/branch/pallas_call | solution.py:883
  188.5 82.8 %feed_gather.1 = (bf16[8,128,2176]{2,1,0:T(8,128)(2,1)}, bf16[704,2176]{1,0:T(8,128)(2,1)}, bf16[704,2176]{1,0:T(8,128)(2,1)}, bf16[704,2176]{1,0:T(8,128)(2,1)}) custom-call(bf16[128,2176]{1,0:T(8,128)(2,1)} %pad_maximum_fusion.1.cot, bf16[704,2048]{1,0:T(8,128)(2,1)} %bitcast.156, bf16[5632,128]{1,0:T(8,128)(2,1)} %down.1, bf16[704,128]{1,0:T(8,128)(2,1)} %pad.56.g_side, ...), custom_call_target="tpu_custom_call" | custom-call | tf_op jit(solution)/shard_map/feed_gather/pallas_call | solution.py:695
  271.3 6.6 %fusion.49 = f32[1024,704]{0,1:T(8,128)S(1)} fusion(bf16[1024,2176]{1,0:T(8,128)(2,1)} %bitcast.163, bf16[704,2176]{1,0:T(8,128)(2,1)} %get-tuple-element.35), kind=kOutput, calls=%fused_computation.96 | convolution fusion | flops 3137339392 | bytes 10403840 | tf_op jit(solution)/shard_map/dot_general | solution.py:991
  278.0 3.5 fusion.50
  281.5 5.9 multiply_convert_fusion
  288.0 6.3 %fusion.51 = f32[1024,2176]{1,0:T(8,128)} fusion(bf16[1024,704]{0,1:T(8,128)(2,1)S(1)} %get-tuple-element.57, bf16[704,2176]{1,0:T(8,128)(2,1)S(1)} %copy-done.36), kind=kOutput, calls=%fused_computation.98 | convolution fusion | flops 3137339392 | bytes 13418496 | tf_op jit(solution)/shard_map/dot_general | solution.py:987
  296.4 11.0 %add_convert_fusion = bf16[1024,2176]{1,0:T(8,128)(2,1)} fusion(f32[1024,2176]{1,0:T(8,128)} %fusion.51, bf16[1024,704]{0,1:T(8,128)(2,1)} %get-tuple-element.56, bf16[704,2176]{1,0:T(8,128)(2,1)} %get-tuple-element.36), kind=kOutput, calls=%fused_computation | convolution fusion | flops 3141795840 | bytes 17874944 | tf_op jit(solution)/shard_map/dot_general | solution.py:987
  307.4 54.9 %back.1 = (f32[128,2048]{1,0:T(8,128)S(1)}, bf16[8,128,2176]{2,1,0:T(8,128)(2,1)}) custom-call(bf16[8,128,2176]{2,1,0:T(8,128)(2,1)} %bitcast.154, bf16[128,2048]{1,0:T(8,128)(2,1)S(1)} %copy-done.6, f32[128,2048]{1,0:T(8,128)S(1)} %get-tuple-element.38.values, bf16[128,2048]{1,0:T(8,128)(2,1)S(1)} %pad.54.down, f32[1,2048]{1,0:T(1,128)S(1)} %bitcast.145, ...), custom_call_target="tpu_custom_call" | custom-call | tf_op jit(solution)/shard_map/back/pallas_call | solution.py:883
  370.9 8.3 %convolution_convert_fusion = bf16[1024,2176]{1,0:T(8,128)(2,1)} fusion(bf16[1024,704]{0,1:T(8,128)(2,1)} %get-tuple-element.58, bf16[704,2176]{1,0:T(8,128)(2,1)} %get-tuple-element.37), kind=kOutput, calls=%fused_computation.1 | convolution fusion | flops 3139567616 | bytes 8962048 | tf_op jit(solution)/shard_map/dot_general | solution.py:987
  379.3 9.6 %all-reduce.12 = s32[16]{0:T(128)S(1)} all-reduce(s32[16]{0:T(128)S(1)} %dynamic-update-slice), channel_id=1, replica_groups=mesh['fsdp'=16,'seq'=8] {'fsdp'}, use_global_device_ids=true, to_apply=%add.12 | all-reduce | flops 16 | bytes 128
  389.0 27.3 %layer.1 = (bf16[128,2048]{1,0:T(8,128)(2,1)S(1)}, bf16[128,128]{1,0:T(8,128)(2,1)S(1)}) custom-call(bf16[8,128,2176]{2,1,0:T(8,128)(2,1)} %bitcast.153, f32[128,2048]{1,0:T(8,128)S(1)} %get-tuple-element.38.values, bf16[128,2048]{1,0:T(8,128)(2,1)S(1)} %pad.55.up), custom_call_target="tpu_custom_call" | custom-call | tf_op jit(solution)/shard_map/layer/pallas_call | solution.py:953
  417.2 4.2 convolution_convert_fusion.6.grad
  421.4 23.6 %mixer_bwd.1 = bf16[1024,896]{1,0:T(8,128)(2,1)} custom-call(bf16[1024,896]{1,0:T(8,128)(2,1)} %convolution_convert_fusion.5.source, s32[1056,128]{1,0:T(8,128)S(1)} %broadcast_in_dim.8.dcol, s32[8,128]{1,0:T(8,128)S(1)} %bitcast.141, f32[4,768]{1,0:T(4,128)S(1)} %bitcast.138, f32[1,128]{1,0:T(1,128)S(1)} %bitcast.147, ...), custom_call_target="tpu_custom_call" | custom-call | tf_op jit(solution)/shard_map/mixer_bwd/pallas_call | solution.py:341
  445.1 8.7 %convolution_convert_fusion.1 = bf16[1024,2176]{1,0:T(8,128)(2,1)} fusion(bf16[1024,896]{1,0:T(8,128)(2,1)} %mixer_bwd.1, bf16[2176,896]{1,0:T(8,128)(2,1)S(1)} %copy-done.33), kind=kOutput, calls=%fused_computation.2 | convolution fusion | flops 3995205632 | bytes 10190848 | tf_op jit(solution)/shard_map/dot_general | solution.py:991
  453.7 26.0 %input.1 = (bf16[128,2048]{1,0:T(8,128)(2,1)S(1)}, bf16[128,128]{1,0:T(8,128)(2,1)S(1)}) custom-call(bf16[8,128,2176]{2,1,0:T(8,128)(2,1)} %bitcast.152, bf16[128,2048]{1,0:T(8,128)(2,1)S(1)} %copy-done.2, f32[128,2048]{1,0:T(8,128)S(1)} %copy-done.16, bf16[128,2048]{1,0:T(8,128)(2,1)S(1)} %pad.59.down, f32[1,2048]{1,0:T(1,128)S(1)} %bitcast.142), custom_call_target="tpu_custom_call" | custom-call | tf_op jit(solution)/shard_map/input/pallas_call | solution.py:953
  480.6 11.9 %all_gather.27 = bf16[1024,32]{0,1:T(8,128)(2,1)S(1)} all-gather(bf16[128,32]{0,1:T(8,128)(2,1)S(1)} %pad_maximum_fusion.3), channel_id=1, replica_groups=mesh['fsdp'=16,'seq'=8] {'seq'}, dimensions={0}, use_global_device_ids=true | all-gather | bytes 73728 | tf_op jit(solution)/shard_map/all_gather | solution.py:1110
  497.0 19.6 %all_gather.28 = bf16[16,16,1280]{2,1,0:T(8,128)(2,1)S(1)} all-gather(bf16[1,16,1280]{2,1,0:T(8,128)(2,1)S(1)} %pad_maximum_fusion.2), channel_id=1, replica_groups=mesh['fsdp'=16,'seq'=8] {'fsdp'}, dimensions={0}, use_global_device_ids=true | all-gather | bytes 696320 | tf_op jit(solution)/shard_map/all_gather | solution.py:1136
  517.7 2.6 convolution_convert_fusion.3
  520.4 26.7 %all-gather.8.cloned.1.call-done = bf16[64,16,1280]{2,0,1:T(8,128)(2,1)} async-done(((bf16[8,16,1280]{2,0,1:T(8,128)(2,1)}), bf16[64,16,1280]{2,0,1:T(8,128)(2,1)}) %all-gather.8.cloned.1.call-update) | async-done | bytes 2621456 | tf_op jit(solution)/shard_map/all_gather | solution.py:1138
  547.0 2.4 convert_bitcast_fusion.5
  558.3 31.4 %all-gather.10.cloned.1.call-done = bf16[64,16,2880]{2,0,1:T(8,128)(2,1)} async-done(((bf16[8,16,2880]{2,0,1:T(8,128)(2,1)}), bf16[64,16,2880]{2,0,1:T(8,128)(2,1)}) %all-gather.10.cloned.1.call-update) | async-done | bytes 5898256 | tf_op jit(solution)/shard_map/all_gather | solution.py:1138
  589.7 3.5 convert_bitcast_fusion.2
  593.2 6.0 convert_bitcast_fusion
  600.7 2.9 copy.82
  612.0 2.4 reshape.252
  614.7 2.4 reshape.251
  617.1 5.1 maximum_convert_fusion
  (158 shorter events, 58.9 us)
Async XLA Ops:
  7.2 10.3 %copy-start = (bf16[8,16,11264]{2,1,0:T(8,128)(2,1)S(1)}, bf16[8,16,11264]{2,1,0:T(8,128)(2,1)}, u32[]{:S(2)}) copy-start(bf16[8,16,11264]{2,1,0:T(8,128)(2,1)} %param.38) | copy-start | bytes 8650756
  7.2 14.1 %copy-start.2 = (bf16[128,2048]{1,0:T(8,128)(2,1)S(1)}, bf16[128,2048]{1,0:T(8,128)(2,1)}, u32[]{:S(2)}) copy-start(bf16[128,2048]{1,0:T(8,128)(2,1)} %tokens.3) | copy-start | bytes 1572868
  7.2 14.1 %copy-start.22 = (f32[2048]{0:T(1024)S(1)}, f32[2048]{0:T(1024)}, u32[]{:S(2)}) copy-start(f32[2048]{0:T(1024)} %param.24) | copy-start | bytes 24580
  7.2 510.5 %all-gather.6.cloned.1.call-start = ((), (), s32[]{:S(2)}) async-start(), calls=%async_computation | async-start | bytes 1601536 | tf_op jit(solution)/shard_map/all_gather | solution.py:1136
  26.6 3.6 copy-start.21
  87.3 9.1 %copy-start.24 = (f32[128]{0:T(128)S(1)}, f32[128]{0:T(128)}, u32[]{:S(2)}) copy-start(f32[128]{0:T(128)} %param.28) | copy-start | bytes 1540
  96.1 39.0 %copy-start.29 = (bf16[256,2176]{1,0:T(8,128)(2,1)S(1)}, bf16[256,2176]{1,0:T(8,128)(2,1)}, u32[]{:S(2)}) copy-start(bf16[256,2176]{1,0:T(8,128)(2,1)} %get-tuple-element.33) | copy-start | bytes 3342340
  135.0 3.7 copy-start.3
  135.0 3.6 copy-start.7
  135.0 3.6 copy-start.9
  135.1 3.6 copy-start.11
  271.2 6.7 %copy-start.30 = (bf16[8,128,2176]{2,1,0:T(8,128)(2,1)S(1)}, bf16[8,128,2176]{2,1,0:T(8,128)(2,1)}, u32[]{:S(2)}) copy-start(bf16[8,128,2176]{2,1,0:T(8,128)(2,1)} %get-tuple-element.34) | copy-start | bytes 13369348
  271.3 6.7 %copy-start.35 = (bf16[704,2176]{1,0:T(8,128)(2,1)S(1)}, bf16[704,2176]{1,0:T(8,128)(2,1)}, u32[]{:S(2)}) copy-start(bf16[704,2176]{1,0:T(8,128)(2,1)} %get-tuple-element.36) | copy-start | bytes 9191428
  271.3 10.2 %slice-start = ((s8[4456448]{0:T(1024)(128)(4,1)}), s8[4194304]{0:T(1024)(128)(4,1)S(1)}, s32[]{:S(2)}) async-start(s8[4456448]{0:T(1024)(128)(4,1)} %bitcast.179), calls=%async_computation.3 | async-start | bytes 8388608
  281.5 6.5 %copy-start.36 = (bf16[704,2176]{1,0:T(8,128)(2,1)S(1)}, bf16[704,2176]{1,0:T(8,128)(2,1)}, u32[]{:S(2)}) copy-start(bf16[704,2176]{1,0:T(8,128)(2,1)} %get-tuple-element.35) | copy-start | bytes 9191428
  296.4 11.0 %copy-start.6 = (bf16[128,2048]{1,0:T(8,128)(2,1)S(1)}, bf16[128,2048]{1,0:T(8,128)(2,1)}, u32[]{:S(2)}) copy-start(bf16[128,2048]{1,0:T(8,128)(2,1)} %cot.1) | copy-start | bytes 1572868
  307.4 55.9 %copy-start.4 = (bf16[1024,256]{1,0:T(8,128)(2,1)S(1)}, bf16[1024,256]{1,0:T(8,128)(2,1)}, u32[]{:S(2)}) copy-start(bf16[1024,256]{1,0:T(8,128)(2,1)} %copy-done.3) | copy-start | bytes 1572868
  307.4 59.9 %copy-start.28 = (bf16[1024,704]{0,1:T(8,128)(2,1)S(1)}, bf16[1024,704]{0,1:T(8,128)(2,1)}, u32[]{:S(2)}) copy-start(bf16[1024,704]{0,1:T(8,128)(2,1)} %get-tuple-element.58) | copy-start | bytes 4325380
  363.3 6.3 copy-start.37
  369.5 177.5 %all-gather.8.cloned.1.call-start = ((), (), s32[]{:S(2)}) async-start(), calls=%async_computation.1 | async-start | bytes 2949120 | tf_op jit(solution)/shard_map/all_gather | solution.py:1138
  370.9 17.9 %copy-start.32 = (bf16[16,2048]{1,0:T(8,128)(2,1)S(1)}, bf16[16,2048]{1,0:T(8,128)(2,1)}, u32[]{:S(2)}) copy-start(bf16[16,2048]{1,0:T(8,128)(2,1)} %copy-done.31) | copy-start | bytes 196612
  417.2 4.2 copy-start.8
  417.2 4.2 copy-start.10
  417.2 4.2 copy-start.12
  417.2 4.2 copy-start.14
  421.4 23.6 %copy-start.33 = (bf16[2176,896]{1,0:T(8,128)(2,1)S(1)}, bf16[2176,896]{1,0:T(8,128)(2,1)}, u32[]{:S(2)}) copy-start(bf16[2176,896]{1,0:T(8,128)(2,1)} %get-tuple-element.31) | copy-start | bytes 11698180
  445.0 8.7 %copy-start.16 = (f32[128,2048]{1,0:T(8,128)S(1)}, f32[128,2048]{1,0:T(8,128)}, u32[]{:S(2)}) copy-start(f32[128,2048]{1,0:T(8,128)} %copy-done.15) | copy-start | bytes 3145732
  517.6 72.0 %all-gather.10.cloned.1.call-start = ((), (), s32[]{:S(2)}) async-start(), calls=%async_computation.2 | async-start | bytes 6782976 | tf_op jit(solution)/shard_map/all_gather | solution.py:1138
  610.2 4.2 copy-start.25
  617.1 5.1 copy-start.18
  617.1 5.9 copy-start.20
  617.1 6.7 %copy-start.1 = (bf16[8,16,11264]{2,1,0:T(8,128)(2,1)S(1)}, bf16[8,16,11264]{2,1,0:T(8,128)(2,1)}, u32[]{:S(2)}) copy-start(bf16[8,16,11264]{2,1,0:T(8,128)(2,1)} %param.38) | copy-start | bytes 8650756
  (11 other events, 29.4 us)
Sparse Core Ops, SparseCore 0:
  369.6 40.4 all-gather.5
  517.8 29.2 all-gather.7
  549.3 40.3 all-gather.9

commit v2 on v1

v2 whole, which is shorter than its diff:
```python
import functools
import jax
import jax.numpy as jnp
from jax import lax
from jax.experimental import pallas as pl
from jax.experimental.pallas import tpu as pltpu
from jax.sharding import PartitionSpec as P

F32 = jnp.float32
BF16 = jnp.bfloat16
CH = 128
PAD = 16


def mm(a, b):
    return jnp.dot(a.astype(BF16), b.astype(BF16), preferred_element_type=F32)


def mm_nt(a, b):
    return lax.dot_general(
        a.astype(BF16), b.astype(BF16), (((1,), (1,)), ((), ())), preferred_element_type=F32
    )


def mm_tn(a, b):
    return lax.dot_general(
        a.astype(BF16), b.astype(BF16), (((0,), (0,)), ((), ())), preferred_element_type=F32
    )


def split(a):
    high = a.astype(BF16)
    return high, (a - high.astype(F32)).astype(BF16)


def mm_fine(a, b):
    ah, al = split(a)
    bh, bl = split(b)
    return jnp.dot(
        jnp.concatenate([ah, al, ah], axis=1),
        jnp.concatenate([bh, bh, bl], axis=0),
        preferred_element_type=F32,
    )


def unit_lower_inverse(lower, row, col, product):
    near = jnp.where((row >> 3) == (col >> 3), lower, 0.0)
    eye = (row == col).astype(F32)
    second = product(near, near)
    fourth = product(second, second)
    inverse = eye - near + second - product(near, second)
    inverse = inverse + product(inverse, fourth)
    for bits in (3, 4, 5, 6):
        joining = ((row >> (bits + 1)) == (col >> (bits + 1))) & ((row >> bits) != (col >> bits))
        below = jnp.where(joining, lower, 0.0)
        inverse = inverse - product(inverse, product(below, inverse))
    return inverse


def sigmoid(v):
    return 1.0 / (1.0 + jnp.exp(-v))


def chunk_masks(c, dcol, drow):
    start = pl.multiple_of(c * CH, CH)
    docs = dcol[pl.ds(start + PAD, CH), :]
    before = dcol[pl.ds(start + PAD - 8, 8), :][7:8, :]
    last = docs[CH - 1 :, :]
    same = docs == drow[pl.ds(c, 1), :]
    live = (docs == before).astype(F32)
    tail = (docs == last).astype(F32)
    live_last = (last == before).astype(F32)
    return docs, same, live, tail, live_last


def conv_chunk(c, joined, dcol, taps, docs):
    start = pl.multiple_of(c * CH, CH)
    window = joined[pl.ds(start, CH + PAD), : taps.shape[1]].astype(F32)
    ids = dcol[pl.ds(start, CH + PAD), :]
    total = window[PAD:, :] * taps[3:4, :]
    for lag in (1, 2, 3):
        keep = (ids[PAD - lag : PAD - lag + CH, :] == docs).astype(F32)
        keep = jnp.concatenate([keep] * (taps.shape[1] // CH), axis=1)
        total = total + window[PAD - lag : PAD - lag + CH, :] * keep * taps[3 - lag : 4 - lag, :]
    return total


def raw_chunk(c, joined, taps):
    rows = pl.ds(pl.multiple_of(c * CH + PAD, PAD), CH)
    return joined[rows, taps.shape[1] :].astype(F32)


def normal_parts(act):
    query, keys, values = act[:, :CH], act[:, CH : 2 * CH], act[:, 2 * CH :]
    q_scale = lax.rsqrt(jnp.sum(query * query, axis=-1, keepdims=True) + 1e-06)
    k_scale = lax.rsqrt(jnp.sum(keys * keys, axis=-1, keepdims=True) + 1e-06)
    return query * q_scale * CH**-0.5, keys * k_scale, values, q_scale, k_scale


def mixer_fwd_kernel(
    heads, chunks, normed, weight, cot, gate_t, w_out, g_side, out_side,
    dcol, drow, taps, gain,
    mixed, o_out, t_out, d_out, s_out, partial, joined_out, everyone, wg, upper, wo,
    joined, rows_v, weight_v, wo_v, q_s, k_s, u_s, w_s, p_s, sem, send, recv, local,
):
    loads = [
        pltpu.make_async_copy(weight, weight_v, sem.at[0]),
        pltpu.make_async_copy(normed, rows_v, sem.at[1]),
    ]
    for copy in loads:
        copy.start()
    greet(ring_peers(), all_plane())
    feed = Feed(
        Line(send, recv, local), cot, gate_t, w_out, (out_side, g_side), everyone, wg, wo, upper
    )
    feed.start()
    joined[pl.ds(0, PAD), :] = jnp.zeros((PAD, joined.shape[1]), BF16)
    for copy in loads:
        copy.wait()
    batch = 2 * CH

    def project(step):
        rows = pl.multiple_of(step * batch, batch)
        joined[pl.ds(rows + PAD, batch), :] = mm(
            rows_v[pl.ds(rows, batch), :], weight_v[...]
        ).astype(BF16)

    project(0)
    row = lax.broadcasted_iota(jnp.int32, (CH, CH), 0)
    col = lax.broadcasted_iota(jnp.int32, (CH, CH), 1)

    def prepare(c, h, docs, same, live, act, raws):
        start = pl.multiple_of(c * CH, CH)
        rows = pl.ds(start, CH)
        query, keys, values, _, _ = normal_parts(act[:, h * 3 * CH : (h + 1) * 3 * CH])
        beta = sigmoid(raws[:, h : h + 1])
        inner = mm_nt(keys, keys)
        lower = jnp.where(same & (row > col), inner * beta, 0.0)
        inverse = unit_lower_inverse(lower, row, col, mm_fine)
        t_out[h, rows, :] = inverse
        both = mm(inverse, jnp.concatenate([values * beta, keys * (beta * live)], axis=1))
        u_s[h, rows, :] = both[:, :CH]
        w_s[h, rows, :] = both[:, CH:].astype(BF16)
        scores = jnp.where(same & (row >= col), mm_nt(query, keys), 0.0)
        p_s[h, rows, :] = scores.astype(BF16)
        q_s[h, rows, :] = (query * live).astype(BF16)
        k_s[h, rows, :] = keys

    def first(step, carry):
        feed.stage(step)
        parts = []
        for part in range(2):
            c = step * 2 + part
            docs, same, live, tail, live_last = chunk_masks(c, dcol, drow)
            conv = conv_chunk(c, joined, dcol, taps, docs)
            act = conv * sigmoid(conv)
            parts.append((c, docs, same, live, act, raw_chunk(c, joined, taps)))
        project(jnp.minimum(step + 1, chunks // 2 - 1))
        for c, docs, same, live, act, raws in parts:
            for h in range(heads):
                prepare(c, h, docs, same, live, act, raws)
        return carry

    lax.fori_loop(0, chunks // 2, first, 0)
    kept = pltpu.make_async_copy(joined.at[pl.ds(PAD, chunks * CH), :], joined_out, sem.at[0])
    kept.start()
    feed.third()

    def second(c, states):
        rows = pl.ds(pl.multiple_of(c * CH, CH), CH)
        docs, same, live, tail, live_last = chunk_masks(c, dcol, drow)
        after = []
        for h in range(heads):
            state = states[h]
            s_out[h, rows, :] = state
            update = u_s[h, rows, :] - mm(w_s[h, rows, :], state)
            d_out[h, rows, :] = update
            after.append(state * live_last + mm_tn(k_s[h, rows, :] * tail, update))
        return tuple(after)

    zero = jnp.zeros((CH, CH), F32)
    lax.fori_loop(0, chunks, second, (zero,) * heads)
    feed.fourth()
    last = pltpu.make_async_copy(wo, wo_v, sem.at[1])
    last.start()
    last.wait()

    def third(c, carry):
        rows = pl.ds(pl.multiple_of(c * CH, CH), CH)
        for h in range(heads):
            out = mm(
                jnp.concatenate([q_s[h, rows, :], p_s[h, rows, :]], axis=1),
                jnp.concatenate(
                    [s_out[h, rows, :].astype(BF16), d_out[h, rows, :].astype(BF16)], axis=0
                ),
            )
            o_out[h, rows, :] = out
            scale = lax.rsqrt(jnp.mean(out * out, axis=-1, keepdims=True) + 1e-05)
            mixed[rows, h * CH : (h + 1) * CH] = (out * scale * gain[...]).astype(BF16)
        partial[c] = mm(mixed[rows, :], wo_v[...]).astype(BF16)
        return carry

    lax.fori_loop(0, chunks, third, 0)
    kept.wait()
    feed.finish()


def mixer_fwd(
    normed, weight, cot, gate_t, w_out, g_side, out_side, dcol, drow, taps, gain
):
    tokens, across = normed.shape
    wide = weight.shape[1]
    heads = wide // (3 * CH)
    chunks = tokens // CH
    seq = lax.axis_size("seq")
    square = jax.ShapeDtypeStruct((heads, tokens, CH), F32)
    out = lambda *shape: jax.ShapeDtypeStruct(shape, BF16)
    share, part = g_side.shape[0], out_side.shape[0]
    return pl.pallas_call(
        functools.partial(mixer_fwd_kernel, heads, chunks),
        out_shape=(
            out(tokens, heads * CH), square, square, square, square,
            out(chunks, CH, across), out(tokens, wide), out(seq, *cot.shape),
            out(share, across), out(share, 128), out(part, across),
        ),
        in_specs=[ANY] * 7 + [VMEM] * 4,
        out_specs=(VMEM,) * 6 + (ANY,) * 5,
        scratch_shapes=[
            pltpu.VMEM((tokens + PAD, wide), BF16),
            pltpu.VMEM((tokens, across), BF16),
            pltpu.VMEM((across, wide), BF16),
            pltpu.VMEM((part, across), BF16),
            pltpu.VMEM((heads, tokens, CH), BF16),
            pltpu.VMEM((heads, tokens, CH), F32),
            pltpu.VMEM((heads, tokens, CH), F32),
            pltpu.VMEM((heads, tokens, CH), BF16),
            pltpu.VMEM((heads, tokens, CH), BF16),
            pltpu.SemaphoreType.DMA((2,)),
        ]
        + sems(Feed.COPIES, Feed.LOCAL),
        compiler_params=comm_params(1, 56),
        name="mixer_fwd",
    )(normed, weight, cot, gate_t, w_out, g_side, out_side, dcol, drow, taps, gain)


def mixer_bwd_kernel(
    heads, chunks, source, partial, early, normed, weight, q_side, values, up,
    dcol, drow, taps, gain, grad, o_in, t_in, d_in, s_in,
    back_partial, up_out, layer_out, inner_out, early_out,
    joined, e_s, f_s, w_s, x_s, ds_s, go_s, dj_s, side_v, weight_v, sem,
    total, own, stage, relay, away, back, early_pieces, early_sum, send, recv, local,
):
    loads = [
        pltpu.make_async_copy(source, joined.at[pl.ds(PAD, source.shape[0]), :], sem.at[0]),
        pltpu.make_async_copy(weight, weight_v, sem.at[1]),
        pltpu.make_async_copy(
            normed.at[:, pl.ds(normed.shape[1] - SIDE, SIDE)], side_v, sem.at[2]
        ),
    ]
    for copy in loads:
        copy.start()
    greet(ring_peers(), line_peers())
    line = Line(send, recv, local)
    ring = RingSum(line, partial, (own, stage, relay, away, back))
    sums = EarlySum(line, early, early_pieces, early_sum, early_out)
    ring.start()
    sums.start()
    joined[pl.ds(0, PAD), :] = jnp.zeros((PAD, joined.shape[1]), BF16)
    dj_s[pl.ds((chunks - 1) * CH, CH), :] = jnp.zeros((CH, dj_s.shape[1]), BF16)
    for copy in loads:
        copy.wait()
    row = lax.broadcasted_iota(jnp.int32, (CH, CH), 0)
    col = lax.broadcasted_iota(jnp.int32, (CH, CH), 1)
    width = 3 * CH

    def revive(c):
        docs, same, live, tail, live_last = chunk_masks(c, dcol, drow)
        conv = conv_chunk(c, joined, dcol, taps, docs)
        raws = raw_chunk(c, joined, taps)
        return docs, same, live, tail, live_last, conv, raws

    def first(c, carry):
        pl.when(c == chunks // 2)(sums.plane.second)
        docs, same, live, tail, live_last, conv, raws = revive(c)
        act = conv * sigmoid(conv)
        rows = pl.ds(pl.multiple_of(c * CH, CH), CH)
        for h in range(heads):
            query, keys, values, _, _ = normal_parts(act[:, h * width : (h + 1) * width])
            beta = sigmoid(raws[:, h : h + 1])
            out = o_in[h, rows, :]
            weighted = grad[rows, h * CH : (h + 1) * CH].astype(F32) * gain[...]
            scale = lax.rsqrt(jnp.mean(out * out, axis=-1, keepdims=True) + 1e-05)
            grad_o = scale * weighted - out * (
                scale * scale * scale * jnp.mean(weighted * out, axis=-1, keepdims=True)
            )
            go_s[h, rows, :] = grad_o
            scores = jnp.where(same & (row >= col), mm_nt(query, keys), 0.0)
            ef = mm_tn(jnp.concatenate([scores, query * live], axis=1), grad_o)
            e_s[h, rows, :] = ef[:CH]
            f_s[h, rows, :] = ef[CH:]
            w_s[h, rows, :] = mm(t_in[h, rows, :], keys * (beta * live)).astype(BF16)
            x_s[h, rows, :] = keys * tail
        return carry

    lax.fori_loop(0, chunks, first, 0)
    ring.middle()
    sums.plane.third()

    def second(step, states):
        c = chunks - 1 - step
        rows = pl.ds(pl.multiple_of(c * CH, CH), CH)
        docs, same, live, tail, live_last = chunk_masks(c, dcol, drow)
        before = []
        for h in range(heads):
            state = states[h]
            ds_s[h, rows, :] = state
            grad_update = e_s[h, rows, :] + mm(x_s[h, rows, :], state)
            x_s[h, rows, :] = grad_update
            before.append(
                state * live_last + f_s[h, rows, :] - mm_tn(w_s[h, rows, :], grad_update)
            )
        return tuple(before)

    zero = jnp.zeros((CH, CH), F32)
    lax.fori_loop(0, chunks, second, (zero,) * heads)

    sums.plane.fourth()

    def project(c):
        rows = pl.ds(pl.multiple_of(c * CH, CH), CH)
        grads = dj_s[rows, :]
        back_partial[c] = mm_nt(grads, weight_v[...]).astype(BF16)

    def third(step, after):
        c = chunks - 1 - step
        pl.when(step == chunks // 4)(ring.last)
        pl.when(step == chunks // 4)(sums.add)
        pl.when(step == chunks - 1)(sums.ring.middle)
        project(jnp.minimum(c + 1, chunks - 1))
        docs, same, live, tail, live_last, conv, raws = revive(c)
        gate = sigmoid(conv)
        act = conv * gate
        slope = gate * (1.0 + conv * (1.0 - gate))
        rows = pl.ds(pl.multiple_of(c * CH, CH), CH)
        lane = lax.broadcasted_iota(jnp.int32, (CH, CH), 1)
        grad_raw = jnp.zeros((CH, CH), F32)
        grads = []
        for h in range(heads):
            part = act[:, h * width : (h + 1) * width]
            query, keys, values, q_scale, k_scale = normal_parts(part)
            beta = sigmoid(raws[:, h : h + 1])
            state, update, state_grad = s_in[h, rows, :], d_in[h, rows, :], ds_s[h, rows, :]
            grad_o = go_s[h, rows, :]
            grad_target = mm_tn(t_in[h, rows, :], x_s[h, rows, :])
            pair = mm_nt(jnp.concatenate([grad_target, grad_o], axis=0), update)
            grad_lower = jnp.where(same & (row > col), -pair[:CH], 0.0)
            grad_scores = jnp.where(same & (row >= col), pair[CH:], 0.0)
            inner = mm_nt(keys, keys)
            recalled = mm(keys, state)
            grad_beta = jnp.sum(
                grad_lower * inner + grad_target * (values - live * recalled),
                axis=-1,
                keepdims=True,
            )
            grad_inner = grad_lower * beta
            back = mm_nt(
                jnp.concatenate([grad_o * live, -grad_target * (beta * live)], axis=0), state
            )
            grad_query = back[:CH] + mm(grad_scores, keys)
            grad_keys = (
                back[CH:]
                + mm_tn(
                    jnp.concatenate([grad_scores, grad_inner], axis=0),
                    jnp.concatenate([query, keys], axis=0),
                )
                + mm(grad_inner, keys)
                + mm_nt(update * tail, state_grad)
            )
            grad_values = grad_target * beta
            raw_q, raw_k = part[:, :CH], part[:, CH : 2 * CH]
            grad_query = grad_query * CH**-0.5
            grad_q = q_scale * grad_query - raw_q * (
                q_scale * q_scale * q_scale * jnp.sum(grad_query * raw_q, axis=-1, keepdims=True)
            )
            grad_k = k_scale * grad_keys - raw_k * (
                k_scale * k_scale * k_scale * jnp.sum(grad_keys * raw_k, axis=-1, keepdims=True)
            )
            grads += [grad_q, grad_k, grad_values]
            grad_raw = jnp.where(lane == h, grad_beta * beta * (1.0 - beta), grad_raw)
        dj_s[rows, heads * width :] = grad_raw.astype(BF16)
        grads = jnp.concatenate(grads, axis=1) * slope
        window = jnp.concatenate([grads, after], axis=0)
        ids = dcol[pl.ds(pl.multiple_of(c * CH + PAD, PAD), CH + PAD), :]
        total_ = grads * taps[3:4, :]
        for lag in (1, 2, 3):
            keep = (ids[lag : lag + CH] == ids[:CH]).astype(F32)
            keep = jnp.concatenate([keep] * (heads * 3), axis=1)
            total_ = total_ + window[lag : lag + CH] * keep * taps[3 - lag : 4 - lag, :]
        dj_s[rows, : heads * width] = total_.astype(BF16)
        return grads[:8]

    lax.fori_loop(0, chunks, third, jnp.zeros((8, heads * width), F32))
    project(0)
    up_out[...] = mm_tn(side_v[...], dj_s[:, : heads * width])[
        up_out.shape[0] : 2 * up_out.shape[0]
    ].astype(BF16)
    sums.ring.finish()
    ring.finish(total)
    across = values.shape[1]
    rank, n = inner_out.shape[1:]
    q_inner = mm_nt(q_side[...], dj_s[...])[rank : 2 * rank].astype(BF16)
    f_inner = total[:, across:].T[:rank].astype(BF16)
    inner_out[0] = q_inner[:, :n]
    rest = 2 * n - q_inner.shape[1] - f_inner.shape[1]
    inner_out[1] = jnp.concatenate(
        [q_inner[:, n:], f_inner, jnp.zeros((rank, rest), BF16)], axis=1
    )

    def step(rows):
        inner = total[rows, across:].astype(BF16)
        layer_out[rows, :] = (
            values[rows, :] + (total[rows, :across] + mm(inner, up[...]))
        ).astype(BF16)

    by_rows(values.shape[0], step)


def mixer_bwd(
    joined, partial, early, normed, weight, q_side, values, up, dcol, drow, taps, gain,
    grad, o, t, d, s,
):
    tokens, wide = joined.shape
    heads = wide // (3 * CH)
    chunks = tokens // CH
    square = (heads, tokens, CH)
    rows, across = values.shape
    seq, rank = lax.axis_size("seq"), early.shape[2]
    out = lambda *shape: jax.ShapeDtypeStruct(shape, BF16)
    return pl.pallas_call(
        functools.partial(mixer_bwd_kernel, heads, chunks),
        out_shape=(
            out(chunks, CH, across + SIDE), out(rank, heads * 3 * CH),
            out(rows, across), out(2, rank, 640), out(seq, *early.shape[1:]),
        ),
        in_specs=[ANY] * 5 + [VMEM] * 12,
        out_specs=(VMEM,) * 4 + (ANY,),
        scratch_shapes=[
            pltpu.VMEM((tokens + PAD, wide), BF16),
            pltpu.VMEM(square, F32),
            pltpu.VMEM(square, F32),
            pltpu.VMEM(square, BF16),
            pltpu.VMEM(square, F32),
            pltpu.VMEM(square, F32),
            pltpu.VMEM(square, F32),
            pltpu.VMEM((tokens, wide), BF16),
            pltpu.VMEM((tokens, SIDE), BF16),
            pltpu.VMEM(weight.shape, BF16),
            pltpu.SemaphoreType.DMA((3,)),
            pltpu.VMEM((rows, across + SIDE), F32),
        ]
        + sum_buffers(rows, across + SIDE)
        + [pltpu.VMEM((16,) + early.shape, BF16), pltpu.VMEM(early.shape[1:], BF16)]
        + sems(RingSum.COPIES + EarlySum.COPIES, RingSum.LOCAL + EarlySum.LOCAL),
        compiler_params=comm_params(5, 60),
        name="mixer_bwd",
    )(
        joined, partial, early, normed, weight, q_side, values, up, dcol, drow, taps, gain,
        grad, o, t, d, s,
    )

MESH = pl.DeviceIdType.MESH
SIDE = 128
ANY = pl.BlockSpec(memory_space=pl.ANY)
VMEM = pl.BlockSpec(memory_space=pltpu.VMEM)
SMEM = pl.BlockSpec(memory_space=pltpu.SMEM)


class Line:
    def __init__(self, send_sems, recv_sems, local_sems):
        self.send_sems, self.recv_sems, self.local_sems = send_sems, recv_sems, local_sems
        self.used, self.used_local = 0, 0

    def take(self, copies, local=0):
        at = self.used, self.used_local
        self.used += copies
        self.used_local += local
        return at

    def copy(self, at, src, dst, device):
        return pltpu.make_async_remote_copy(
            src_ref=src, dst_ref=dst, send_sem=self.send_sems.at[at],
            recv_sem=self.recv_sems.at[at], device_id=device, device_id_type=MESH,
        )

    def local(self, at, src, dst):
        return pltpu.make_async_copy(src, dst, self.local_sems.at[at])


def sems(copies, local):
    return [
        pltpu.SemaphoreType.DMA((copies,)),
        pltpu.SemaphoreType.DMA((copies,)),
        pltpu.SemaphoreType.DMA((local,)),
    ]


def seq_places():
    s = lax.axis_index("seq")
    x, core = s // 2, lax.rem(s, 2)
    there = lambda d: lax.rem(x + d, 4) * 2 + core
    return s, x * 2 + 1 - core, there(1), there(3), there(2)


def plane_places():
    f = lax.axis_index("fsdp")
    return f, f // 4, lax.rem(f, 4)


def ring_peers():
    s, partner, right, left, far = seq_places()
    return [partner, right, left]


def all_plane():
    f = lax.axis_index("fsdp")
    return [lax.rem(f + d, 16) for d in range(1, 16)]


def line_peers():
    f, y, z = plane_places()
    return [y * 4 + lax.rem(z + d, 4) for d in (1, 3)] + [
        lax.rem(y + d, 4) * 4 + z for d in (1, 3)
    ]


def greet(seq_peers, plane_peers):
    barrier = pltpu.get_barrier_semaphore()
    for p in seq_peers:
        pl.semaphore_signal(barrier, inc=1, device_id={"seq": p}, device_id_type=MESH)
    for p in plane_peers:
        pl.semaphore_signal(barrier, inc=1, device_id={"fsdp": p}, device_id_type=MESH)
    pl.semaphore_wait(barrier, len(seq_peers) + len(plane_peers))


class RingGather:
    COPIES, LOCAL = 13, 1

    def __init__(self, line, block, out, first=0, rows=None):
        self.line, self.placed, self.out = line, block is None, out
        self.block = out.at[lax.axis_index("seq")] if self.placed else block
        rows = rows or self.block.shape[0]
        half = rows // 2
        self.low, self.high = pl.ds(first, half), pl.ds(first + half, half)
        self.all = pl.ds(first, rows)
        self.at, self.local_at = line.take(self.COPIES, self.LOCAL)

    def mine(self, i, rows, peer):
        s = lax.axis_index("seq")
        return self.line.copy(
            self.at + i, self.block.at[rows], self.out.at[s, rows], {"seq": peer}
        )

    def pass_on(self, i, s, rows, peer):
        ref = self.out.at[s, rows]
        return self.line.copy(self.at + i, ref, ref, {"seq": peer})

    def copy(self, i):
        s, partner, right, left, far = seq_places()
        low, high = self.low, self.high
        if i < 4:
            return self.mine(i, *((low, right), (high, left), (high, right), (low, left))[i])
        if i == 4:
            return self.mine(4, self.all, partner)
        return self.pass_on(
            i,
            *(
                (left, low, right), (left, low, partner), (right, high, left),
                (right, high, partner), (left, high, partner), (right, low, partner),
                (far, low, partner), (far, high, partner),
            )[i - 5],
        )

    def own(self):
        s = lax.axis_index("seq")
        return self.line.local(self.local_at, self.block, self.out.at[s])

    def start(self):
        for i in range(5):
            self.copy(i).start()
        if not self.placed:
            self.own().start()

    def middle(self):
        for arrived, onward in ((0, (5, 6)), (1, (7, 8)), (2, (9,)), (3, (10,))):
            self.copy(arrived).wait_recv()
            for i in onward:
                self.copy(i).start()

    def finish(self):
        self.copy(5).wait_recv()
        self.copy(11).start()
        self.copy(7).wait_recv()
        self.copy(12).start()
        for i in (0, 1, 2, 3, 5, 7):
            self.copy(i).wait_send()
        for i in (4, 6, 8, 9, 10, 11, 12):
            self.copy(i).wait()
        if not self.placed:
            self.own().wait()

    def reach(self, step):
        @pl.when(step == 0)
        def _():
            self.copy(4).wait_recv()

        @pl.when(step == 1)
        def _():
            self.middle()
            self.copy(8).wait_recv()
            self.copy(10).wait_recv()

        @pl.when(step == 2)
        def _():
            self.copy(6).wait_recv()
            self.copy(9).wait_recv()

        @pl.when(step == 3)
        def _():
            self.copy(5).wait_recv()
            self.copy(11).start()
            self.copy(7).wait_recv()
            self.copy(12).start()
            self.copy(11).wait_recv()
            self.copy(12).wait_recv()

    def sent(self):
        for i in range(self.COPIES):
            self.copy(i).wait_send()


class PlaneGather:
    COPIES, LOCAL = 40, 0

    def __init__(self, line, place):
        self.line, self.place = line, place
        self.at, _ = line.take(self.COPIES)

    def by(self, half, along, across):
        f, y, z = plane_places()
        dy, dz = (across, along) if half == 0 else (along, across)
        return lax.rem(y + dy + 4, 4) * 4 + lax.rem(z + dz + 4, 4)

    def send(self, at, ref, peer):
        return self.line.copy(self.at + at, ref, ref, {"fsdp": peer})

    def one(self, half, i):
        ref = self.place(lax.axis_index("fsdp"), half, None)
        return self.send(half * 20 + i, ref, self.by(half, (1, -1)[i], 0))

    def one_on(self, half, i):
        d = (1, -1)[i]
        ref = self.place(self.by(half, -d, 0), half, i)
        return self.send(half * 20 + 2 + i, ref, self.by(half, d, 0))

    def two(self, half, k, i):
        ref = self.place(self.by(half, (0, -1, 1, 2)[k], 0), half, None)
        return self.send(half * 20 + 4 + k * 2 + i, ref, self.by(half, 0, (1, -1)[i]))

    def two_on(self, half, k, i):
        d = (1, -1)[i]
        ref = self.place(self.by(half, (0, -1, 1, 2)[k], -d), half, i)
        return self.send(half * 20 + 12 + k * 2 + i, ref, self.by(half, 0, d))

    def first(self):
        for half in (0, 1):
            for i in (0, 1):
                self.one(half, i).start()

    def second(self):
        for half in (0, 1):
            for i in (0, 1):
                self.two(half, 0, i).start()
        for half in (0, 1):
            for i in (0, 1):
                self.one(half, i).wait_recv()
                self.one_on(half, i).start()
                for j in (0, 1):
                    self.two(half, 1 + i, j).start()

    def third(self):
        for half in (0, 1):
            for i in (0, 1):
                self.one_on(half, i).wait_recv()
            for i in (0, 1):
                self.two(half, 3, i).start()
        for k in range(3):
            for half in (0, 1):
                self.cross(half, k)

    def cross(self, half, k):
        for i in (0, 1):
            self.two(half, k, i).wait_recv()
            self.two_on(half, k, i).start()

    def fourth(self):
        for half in (0, 1):
            self.cross(half, 3)

    def finish(self):
        for half in (0, 1):
            for i in (0, 1):
                self.one(half, i).wait_send()
                self.one_on(half, i).wait_send()
                for k in range(4):
                    self.two(half, k, i).wait_send()
                    self.two_on(half, k, i).wait()


class Scatter:
    COPIES, LOCAL = 17, 2

    def __init__(self, line, sources, source_block, into):
        self.line, self.sources = line, sources
        self.source_block, self.into = source_block, into
        self.at, self.local_at = line.take(self.COPIES, self.LOCAL)

    def copy(self, j, d):
        f, _, _ = plane_places()
        t = lax.rem(f + d, 16)
        line = self.line
        return pltpu.make_async_remote_copy(
            src_ref=self.source_block(t), dst_ref=self.into(t, j),
            send_sem=line.send_sems.at[self.at + d], recv_sem=line.recv_sems.at[self.at + j],
            device_id={"fsdp": t}, device_id_type=MESH,
        )

    def keep(self, j):
        f, _, _ = plane_places()
        return self.line.local(self.local_at + j, self.source_block(f), self.into(f, j))

    def start(self):
        f, _, _ = plane_places()
        for j, source in enumerate(self.sources):
            @pl.when(f == source)
            def _():
                for d in range(1, 16):
                    self.copy(j, d).start()
                self.keep(j).start()

    def arrive(self):
        f, _, _ = plane_places()
        for j, source in enumerate(self.sources):
            @pl.when(f == source)
            def _():
                self.keep(j).wait()

            @pl.when(f != source)
            def _():
                ref = self.into(f, j)
                pltpu.make_async_remote_copy(
                    src_ref=ref, dst_ref=ref, send_sem=self.line.send_sems.at[self.at],
                    recv_sem=self.line.recv_sems.at[self.at + j],
                    device_id={"fsdp": lax.rem(f + 1, 16)}, device_id_type=MESH,
                ).wait_recv()

    def finish(self):
        f, _, _ = plane_places()
        for j, source in enumerate(self.sources):
            @pl.when(f == source)
            def _():
                for d in range(1, 16):
                    self.copy(j, d).wait_send()


def rows_of(total, half, quarter):
    if quarter is None:
        return pl.ds(half * (total // 2), total // 2)
    return pl.ds(half * (total // 2) + quarter * (total // 4), total // 4)


def columns_place(out):
    return lambda f, half, quarter: out.at[
        rows_of(out.shape[0], half, quarter), pl.ds(pl.multiple_of(f * 128, 128), 128)
    ]


def block_of(ref, t):
    return ref.at[:, pl.ds(pl.multiple_of(t * 128, 128), 128)]


ADD_ROWS = 16


def add_rows(dst, sources, first, count):
    def step(i, carry):
        rows = pl.ds(pl.multiple_of(first + i * ADD_ROWS, ADD_ROWS), ADD_ROWS)
        total = None
        for source, offset in sources:
            at = pl.ds(pl.multiple_of(first - offset + i * ADD_ROWS, ADD_ROWS), ADD_ROWS)
            item = source[at, :].astype(F32)
            total = item if total is None else total + item
        dst[rows, :] = total.astype(dst.dtype)
        return carry

    lax.fori_loop(0, count // ADD_ROWS, step, 0)


class RingSum:
    COPIES, LOCAL = 10, 4

    def __init__(self, line, partial, buffers, first=0):
        self.line, self.partial, self.first = line, partial, first
        self.own, self.stage, self.relay, self.away, self.back = buffers
        self.rows = self.stage.shape[1]
        self.block = pl.ds(first, self.rows)
        self.half = self.rows // 2
        self.low, self.high = pl.ds(0, self.half), pl.ds(self.half, self.half)
        self.at, self.local_at = line.take(self.COPIES, self.LOCAL)

    def near(self, k):
        s, partner, right, left, far = seq_places()
        p = (far, right, left, s)[k]
        return self.line.copy(
            self.at + k, self.partial.at[p + partner - s, self.block], self.stage.at[k],
            {"seq": partner},
        )

    def kept(self, k):
        s, partner, right, left, far = seq_places()
        p = (far, right, left, s)[k]
        return self.line.local(self.local_at + k, self.partial.at[p, self.block], self.own.at[k])

    def go(self, i):
        s, partner, right, left, far = seq_places()
        away, relay, back, low, high = self.away, self.relay, self.back, self.low, self.high
        src, dst, peer = (
            (away.at[0, low], relay.at[0], right),
            (away.at[0, high], relay.at[1], left),
            (away.at[1, high], back.at[0, high], right),
            (away.at[2, low], back.at[1, low], left),
            (away.at[1, low], back.at[0, low], right),
            (away.at[2, high], back.at[1, high], left),
        )[i]
        return self.line.copy(self.at + 4 + i, src, dst, {"seq": peer})

    def start(self):
        for k in range(4):
            self.near(k).start()
            if self.own is not None:
                self.kept(k).start()

    def ready(self, k):
        self.near(k).wait_recv()
        if self.own is not None:
            self.kept(k).wait()

    def pair(self, k):
        if self.own is not None:
            return [(self.own.at[k], 0), (self.stage.at[k], 0)]
        s, partner, right, left, far = seq_places()
        return [(self.partial.at[(far, right, left, s)[k]], -self.first), (self.stage.at[k], 0)]

    def far(self):
        half, away = self.half, self.away
        self.ready(0)
        add_rows(away.at[0], self.pair(0), 0, half)
        self.go(0).start()
        add_rows(away.at[0], self.pair(0), half, half)
        self.go(1).start()

    def beside(self, k):
        half = self.half
        self.ready(k)
        add_rows(self.away.at[k], self.pair(k), half if k == 1 else 0, half)
        self.go(1 + k).start()

    def middle(self):
        self.far()
        self.beside(1)
        self.beside(2)

    def send_step(self, step):
        @pl.when(step == 0)
        def _():
            self.near(3).start()

        @pl.when(step == 1)
        def _():
            self.near(1).start()

        @pl.when(step == 2)
        def _():
            self.near(2).start()
            self.beside(1)

        @pl.when(step == 3)
        def _():
            self.near(0).start()
            self.beside(2)

    def last(self):
        half, away, relay = self.half, self.away, self.relay
        self.go(0).wait_recv()
        add_rows(away.at[1], self.pair(1) + [(relay.at[0], 0)], 0, half)
        self.go(4).start()
        self.go(1).wait_recv()
        add_rows(away.at[2], self.pair(2) + [(relay.at[1], half)], half, half)
        self.go(5).start()

    def finish(self, total):
        self.ready(3)
        for i in (2, 3, 4, 5):
            self.go(i).wait_recv()
        sources = self.pair(3) + [(self.back.at[0], 0), (self.back.at[1], 0)]
        add_rows(total.at[self.block], sources, 0, self.rows)
        for k in range(4):
            self.near(k).wait_send()
        for i in range(6):
            self.go(i).wait_send()


def sum_buffers(rows, width):
    return [
        pltpu.VMEM((4, rows, width), BF16),
        pltpu.VMEM((4, rows, width), BF16),
        pltpu.VMEM((2, rows // 2, width), BF16),
        pltpu.VMEM((3, rows, width), BF16),
        pltpu.VMEM((2, rows, width), BF16),
    ]


MID_ROWS = 32


def by_rows(rows, step, first=0):
    def run(i, carry):
        step(pl.ds(pl.multiple_of(first + i * MID_ROWS, MID_ROWS), MID_ROWS))
        return carry

    lax.fori_loop(0, rows // MID_ROWS, run, 0)


def norm_back_rows(values, gain, grad):
    scale = lax.rsqrt(jnp.mean(values * values, axis=-1, keepdims=True) + 1e-05)
    weighted = grad * gain
    return scale * weighted - values * (
        scale * scale * scale * jnp.mean(weighted * values, axis=-1, keepdims=True)
    )


def comm_params(cid, limit=48):
    return pltpu.CompilerParams(
        collective_id=cid, has_side_effects=True, vmem_limit_bytes=limit << 20
    )


def start_kernel(payload, w_qkv, q_side, beta_side, everyone, wq, send, recv, local):
    s = lax.axis_index("seq")
    greet(ring_peers(), all_plane())
    line = Line(send, recv, local)
    depth, width = w_qkv.shape
    scatter = Scatter(
        line, (2 * s, 2 * s + 1),
        lambda t: w_qkv.at[pl.ds(t * 128, 128), :],
        lambda t, j: wq.at[pl.ds(t * 128, 128), pl.ds(j * width, width)],
    )
    ring = RingGather(line, payload, everyone)
    _, at = line.take(0, 2)
    sides = [
        line.local(at, q_side, wq.at[pl.ds(depth, SIDE), :]),
        line.local(at + 1, beta_side, wq.at[pl.ds(0, depth), pl.ds(2 * width, SIDE)]),
    ]

    def place(t, half, quarter):
        size = 64 if quarter is None else 32
        return wq.at[
            pl.ds(t * 128 + half * 64 + (quarter or 0) * 32, size), pl.ds(0, 2 * width)
        ]

    qkv = PlaneGather(line, place)
    scatter.start()
    ring.start()
    for copy in sides:
        copy.start()
    scatter.arrive()
    qkv.first()
    qkv.second()
    ring.middle()
    qkv.third()
    qkv.fourth()
    ring.finish()
    scatter.finish()
    qkv.finish()
    for copy in sides:
        copy.wait()


def start_gather(payload, w_qkv, q_side, beta_side):
    seq, wide = lax.axis_size("seq"), payload.shape[1]
    copies = RingGather.COPIES + Scatter.COPIES + PlaneGather.COPIES
    return pl.pallas_call(
        start_kernel,
        out_shape=(
            jax.ShapeDtypeStruct((seq,) + payload.shape, BF16),
            jax.ShapeDtypeStruct((wide, q_side.shape[1]), BF16),
        ),
        in_specs=[ANY] * 4,
        out_specs=(ANY,) * 2,
        scratch_shapes=sems(copies, 10),
        compiler_params=comm_params(0),
        name="start_gather",
    )(payload, w_qkv, q_side, beta_side)


class Feed:
    COPIES = RingGather.COPIES + 2 * Scatter.COPIES + 2 * PlaneGather.COPIES
    LOCAL = RingGather.LOCAL + 2 * Scatter.LOCAL + 3

    def __init__(self, line, cot, gate_t, w_out, sides, everyone, wg, wo, upper):
        s = lax.axis_index("seq")
        self.line, self.w_out, self.sides = line, w_out, sides
        self.outs = (wo, wg)
        self.ring = RingGather(line, cot, everyone)
        self.scatters = [
            Scatter(line, (source,), lambda t: block_of(gate_t, t), into)
            for source, into in ((s, lambda t, j: block_of(wg, t)), (s + 8, lambda t, j: upper))
        ]
        self.out, self.gate = [PlaneGather(line, columns_place(o)) for o in self.outs]
        _, self.at = line.take(0, 3)

    def place(self, i):
        s, f = lax.axis_index("seq"), lax.axis_index("fsdp")
        if i == 2:
            wo = self.outs[0]
            share = wo.shape[0]
            src = self.w_out.at[pl.ds(pl.multiple_of(s * share, 16), share), :]
            dst = block_of(wo, f)
        else:
            src, out = self.sides[i], self.outs[i]
            dst = out.at[:, pl.ds(out.shape[1] - SIDE, SIDE)]
        return self.line.local(self.at + i, src, dst)

    def start(self):
        for item in self.scatters:
            item.start()
        for i in range(3):
            self.place(i).start()
        self.ring.start()
        self.place(2).wait()
        self.out.first()

    def stage(self, step):
        @pl.when(step == 2)
        def _():
            self.out.second()
            self.scatters[0].arrive()
            self.gate.first()

        @pl.when(step == 3)
        def _():
            self.out.third()
            self.ring.middle()
            self.gate.second()

    def third(self):
        self.out.fourth()
        self.gate.third()

    def fourth(self):
        self.out.finish()
        self.place(0).wait()
        self.gate.fourth()

    def finish(self):
        self.ring.finish()
        self.gate.finish()
        self.place(1).wait()
        self.scatters[1].arrive()
        for item in self.scatters:
            item.finish()


def chip_at(step):
    x = lax.axis_index("seq") // 2
    d = jnp.where(step == 2, 3, jnp.where(step == 3, 2, step))
    return lax.rem(x + d, 4)


def feed_forward_kernel(
    partial, down_w, f_side, u_side, upper_block, wg_in, cot_in,
    tokens, cot, mixed, wo, up, gain, down, chosen,
    middle, grad_middle, partial_down, grad_mixed, early,
    rows2, rows3, cots, wg, wu, wd, partial2, total,
    gate_s, upper_s, hidden_s, gg_s, gu_s, gate_e, upper_e, down_e, *rest,
):
    greet(ring_peers(), line_peers())
    buffers, (send, recv, local) = rest[:-3], rest[-3:]
    line = Line(send, recv, local)
    s = lax.axis_index("seq")
    f = lax.axis_index("fsdp")
    rows = tokens.shape[0]
    firsts = (0, rows // 2)
    first_sum = [
        RingSum(line, partial, buffers[5 * i : 5 * i + 5], first)
        for i, first in enumerate(firsts)
    ]
    second_sum = [
        RingSum(line, partial2, (None,) + buffers[10 + 4 * i : 14 + 4 * i], first)
        for i, first in enumerate(firsts)
    ]
    first_gather = [RingGather(line, None, rows2, first, rows // 2) for first in firsts]
    second_gather = [RingGather(line, None, rows3, first, rows // 2) for first in firsts]
    weights = [PlaneGather(line, columns_place(o)) for o in (wu, wd)]
    share = wd.shape[0]
    width = tokens.shape[1]
    _, at = line.take(0, 6)
    mine = [
        line.local(at, upper_block, block_of(wu, f)),
        line.local(
            at + 1, down_w.at[pl.ds(pl.multiple_of(s * share, 16), share), :], block_of(wd, f)
        ),
    ]
    others = [
        line.local(at + 2, u_side, wu.at[:, pl.ds(width, SIDE)]),
        line.local(at + 3, f_side, wd.at[:, pl.ds(width, SIDE)]),
        line.local(at + 4, wg_in, wg),
        line.local(at + 5, cot_in, cots),
    ]
    for copy in mine:
        copy.start()
    for item in first_sum:
        item.start()
    for copy, item in zip(mine, weights):
        copy.wait()
        item.first()
    for copy in others:
        copy.start()
    for item in first_sum:
        item.middle()
    for item in weights:
        item.second()
    for item in first_sum:
        item.last()

    def norm_rows(rows):
        inner = total[rows, width:].astype(BF16)
        value = tokens[rows, :].astype(F32) + (total[rows, :width] + mm(inner, up[...]))
        middle[rows, :] = value
        scale = lax.rsqrt(jnp.mean(value * value, axis=-1, keepdims=True) + 1e-05)
        normed = (value * scale * gain[...]).astype(BF16)
        rows2[s, rows, :width] = normed
        rows2[s, rows, width:] = (inner.astype(F32) + mm_nt(normed, down[...])).astype(BF16)

    first_sum[0].finish(total)
    by_rows(rows // 2, norm_rows)
    first_gather[0].start()
    for item in weights:
        item.third()
    first_sum[1].finish(total)
    by_rows(rows // 2, norm_rows, rows // 2)
    first_gather[1].start()
    for item in weights:
        item.fourth()
    for item in weights:
        item.finish()
    for copy in others:
        copy.wait()
    gate_e[...] = jnp.zeros_like(gate_e)
    upper_e[...] = jnp.zeros_like(upper_e)
    down_e[...] = jnp.zeros_like(down_e)
    pair = 2 * rows

    def chip(step, carry):
        for item in first_gather:
            item.reach(step)
        k = chip_at(step)
        both = pl.ds(k * 2, 2)
        normed = rows2[both].reshape(pair, width + SIDE)
        grads = cots[both].reshape(pair, width + SIDE)
        gate_s[...] = mm_nt(normed, wg[...])
        upper_s[...] = mm_nt(normed, wu[...])
        hidden = mm_nt(grads, wd[...])
        gate, upper = gate_s[...], upper_s[...]
        sigma = sigmoid(gate)
        silu = gate * sigma
        hidden_s[...] = (silu * upper).astype(BF16)
        gg_s[...] = (hidden * upper * sigma * (1.0 + gate * (1.0 - sigma))).astype(BF16)
        gu_s[...] = (hidden * silu).astype(BF16)
        partial2[both] = (
            (mm(gg_s[...], wg[...]) + mm(gu_s[...], wu[...]))
            .astype(BF16)
            .reshape(2, pair // 2, width + SIDE)
        )
        for item in second_sum:
            item.send_step(step)
        partial_down[both] = (
            mm(hidden_s[...], wd[...]).astype(BF16).reshape(2, pair // 2, width + SIDE)
        )
        side = normed[:, width:]
        gate_e[...] += mm_tn(side, gg_s[...])
        upper_e[...] += mm_tn(side, gu_s[...])
        down_e[...] += mm_tn(grads[:, width:], hidden_s[...])
        return carry

    lax.fori_loop(0, 4, chip, 0)
    for item in second_sum:
        item.far()
    for item in second_sum:
        item.last()

    def back_rows(rows):
        inner = total[rows, width:].astype(BF16)
        grad = total[rows, :width] + mm(inner, down[...])
        result = cot[rows, :].astype(F32) + norm_back_rows(middle[rows, :], gain[...], grad)
        grad_middle[rows, :] = result
        low = result.astype(BF16)
        rows3[s, rows, :width] = low
        rows3[s, rows, width:] = (inner.astype(F32) + mm_nt(low, up[...])).astype(BF16)

    second_sum[0].finish(total)
    by_rows(rows // 2, back_rows)
    second_gather[0].start()
    second_sum[1].finish(total)
    by_rows(rows // 2, back_rows, rows // 2)
    second_gather[1].start()
    for item in first_gather:
        item.sent()

    def out_back(step, carry):
        for item in second_gather:
            item.reach(step)
        k = chip_at(step)
        grads = rows3[pl.ds(k * 2, 2)].reshape(pair, width + SIDE)
        grad_mixed[pl.ds(pl.multiple_of(k * pair, pair), pair), :] = mm_nt(grads, wo[...]).astype(
            BF16
        )
        return carry

    lax.fori_loop(0, 4, out_back, 0)
    rank = early.shape[2]
    part = mixed.shape[1]
    own_part = pl.ds(pl.multiple_of(s * part, 128), part)
    flat = lambda v: v.reshape(-1, v.shape[-1])
    side2, side3 = flat(rows2[:, :, width:]), flat(rows3[:, :, width:])
    first = [
        gate_e[rank : 2 * rank, :].astype(BF16),
        upper_e[rank : 2 * rank, :].astype(BF16),
        chosen[...],
    ]
    second = [
        mm_tn(side3, mixed[...])[:rank].astype(BF16),
        mm_tn(side2, flat(rows3[:, :, own_part]))[:rank].astype(BF16),
        mm_tn(side3, flat(rows2[:, :, own_part]))[rank : 2 * rank].astype(BF16),
        down_e[:rank, :].astype(BF16),
        chosen[:, : SIDE // 2],
    ]
    n = early.shape[3]
    for half, parts in enumerate((first, second)):
        piece = jnp.concatenate(parts, axis=1)
        early[half, 0] = piece[:, :n]
        early[half, 1] = piece[:, n:]
    for item in second_gather:
        item.sent()


def feed_forward(
    partial, down_w, f_side, u_side, upper, wg, cots,
    tokens, cot, mixed, wo, up, gain, down, chosen,
):
    seq, rows, wide = partial.shape
    share = f_side.shape[0]
    rank, part = chosen.shape[0], mixed.shape[1]
    whole = pltpu.VMEM((seq, rows, wide), BF16)
    weight = pltpu.VMEM((share, wide), BF16)
    buffers = sum_buffers(rows // 2, wide)
    f32_rows = pltpu.VMEM((2 * rows, share), F32)
    bf16_rows = pltpu.VMEM((2 * rows, share), BF16)
    extra = pltpu.VMEM((SIDE, share), F32)
    return pl.pallas_call(
        feed_forward_kernel,
        out_shape=(
            jax.ShapeDtypeStruct((rows, wide - SIDE), F32),
            jax.ShapeDtypeStruct((rows, wide - SIDE), F32),
            jax.ShapeDtypeStruct((seq, rows, wide), BF16),
            jax.ShapeDtypeStruct((seq * rows, part), BF16),
            jax.ShapeDtypeStruct((2, 2, rank, share + SIDE // 2), BF16),
        ),
        in_specs=[ANY] * 7 + [VMEM] * 8,
        out_specs=(VMEM,) * 5,
        scratch_shapes=[whole, whole, whole, weight, weight, weight, whole]
        + [pltpu.VMEM((rows, wide), F32)]
        + [f32_rows, f32_rows, bf16_rows, bf16_rows, bf16_rows, extra, extra, extra]
        + buffers * 2
        + buffers[1:] * 2
        + sems(4 * RingSum.COPIES + 4 * RingGather.COPIES + 2 * PlaneGather.COPIES, 26),
        compiler_params=comm_params(2, 63),
        name="feed_forward",
    )(
        partial, down_w, f_side, u_side, upper, wg, cots,
        tokens, cot, mixed, wo, up, gain, down, chosen,
    )


class EarlySum:
    COPIES, LOCAL = PlaneGather.COPIES + RingGather.COPIES, 1 + RingGather.LOCAL

    def __init__(self, line, early, pieces, total, out):
        self.line, self.early, self.pieces, self.total = line, early, pieces, total
        _, self.local_at = line.take(0, 1)
        self.ring = RingGather(line, total, out)

        def place(f, half, quarter):
            return pieces.at[f, half] if quarter is None else pieces.at[f, half, quarter]

        self.plane = PlaneGather(line, place)

    def start(self):
        own = self.line.local(
            self.local_at, self.early, self.pieces.at[lax.axis_index("fsdp")]
        )
        own.start()
        own.wait()
        self.plane.first()

    def add(self):
        self.plane.finish()
        f = lax.axis_index("fsdp")
        half = lax.rem(f, 2)
        lane = lax.broadcasted_iota(jnp.int32, (1, SIDE), 1)
        mark = jnp.where(half == 0, 0, SIDE // 2) + f // 2
        totals = [None, None]
        for t in range(16):
            pair = [self.pieces[t, half, q].astype(F32) for q in (0, 1)]
            marks = pair[1][:1, -SIDE:]
            uses = jnp.sum(jnp.where(lane == mark, marks, 0.0), axis=1, keepdims=True)
            totals = [
                p * uses if total is None else total + p * uses for p, total in zip(pair, totals)
            ]
        self.total[0] = totals[0].astype(BF16)
        self.total[1] = totals[1].astype(BF16)
        self.ring.start()


def by_adapter(plane, out):
    count, wide = out.shape[0], out.shape[2]
    parts, n = plane.shape[1], plane.shape[3]
    for q in range(parts):
        cut = min(n, wide - q * n)
        for a in range(count):
            total = None
            for f in range(plane.shape[0]):
                at = wide - (parts - 1) * n + a
                uses = plane[f, parts - 1].astype(F32)[:1, at : at + 1]
                item = plane[f, q].astype(F32)[:, :cut] * uses
                total = item if total is None else total + item
            out[a, :, q * n : q * n + cut] = total.astype(BF16)


def finale_kernel(
    partial, normed, cot, early, up, inner, tokens, grad_middle, down, gain, chosen,
    input_grad, early_whole, late_whole,
    total, own, stage, relay, away, back, inners, sides, pieces, late, send, recv, local,
):
    greet(ring_peers(), line_peers())
    line = Line(send, recv, local)
    s, partner, _, _, _ = seq_places()
    f = lax.axis_index("fsdp")
    core = lax.rem(s, 2)
    rank, columns = up.shape
    ring = RingSum(line, partial, (own, stage, relay, away, back))
    inner_ring = RingGather(line, inner, inners)
    late_ring = RingGather(line, late, late_whole)

    def early_place(t, half, quarter):
        first = core * 4 + half * 2 + (quarter or 0)
        return early_whole.at[t, pl.ds(first, 2 if quarter is None else 1)]

    def late_place(t, half, quarter):
        first = half * 2 + (quarter or 0)
        return pieces.at[t, pl.ds(first, 2 if quarter is None else 1)]

    early_plane, late_plane = PlaneGather(line, early_place), PlaneGather(line, late_place)
    at, local_at = line.take(1, 3)
    half_slices = pl.ds(core * 4, 4)
    keep = line.local(local_at, early.at[half_slices], early_whole.at[f, half_slices])
    share = line.copy(
        at, early_whole.at[:, half_slices], early_whole.at[:, half_slices], {"seq": partner}
    )
    part = sides.shape[1] // 2
    mine = pl.ds(pl.multiple_of(s * part, 128), part)
    fetch = [
        line.local(local_at + 1, normed.at[:, mine], sides.at[:, pl.ds(0, part)]),
        line.local(local_at + 2, cot.at[:, mine], sides.at[:, pl.ds(part, part)]),
    ]
    inner_ring.start()
    ring.start()
    keep.start()
    for copy in fetch:
        copy.start()
    keep.wait()
    early_plane.first()
    inner_ring.middle()
    ring.middle()
    inner_ring.finish()
    tokens_here = tokens.shape[0]
    n = inners.shape[3]
    ahead = sides.shape[0] - n
    sums, beside = [None, None], []
    for t in range(inners.shape[0]):
        parts = inners[t, 0].astype(F32), inners[t, 1].astype(F32)[:, :ahead]
        sums = [p if total_ is None else total_ + p for p, total_ in zip(parts, sums)]
        beside.append(inners[t, 1][:, ahead : ahead + tokens_here])
    for copy in fetch:
        copy.wait()
    down_piece = mm(jnp.concatenate(sums, axis=1), sides[:, :part])
    up_piece = mm(jnp.concatenate(beside, axis=1), sides[:, part:])
    piece = jnp.concatenate(
        [up[...], down_piece.astype(BF16), up_piece.astype(BF16), chosen[...], chosen[...]], axis=1
    )
    wide = pieces.shape[3]
    for q in range(4):
        pieces[f, q] = piece[:, q * wide : (q + 1) * wide]
    late_plane.first()
    early_plane.second()
    ring.last()
    late_plane.second()
    late_plane.third()
    early_plane.third()
    late_plane.fourth()
    late_plane.finish()
    by_adapter(pieces, late)
    late_ring.start()
    early_plane.fourth()
    ring.finish(total)
    width = tokens.shape[1]

    def step(rows):
        grad = total[rows, :width] + mm(total[rows, width:], down[...])
        input_grad[rows, :] = (
            grad_middle[rows, :]
            + norm_back_rows(tokens[rows, :].astype(F32), gain[...], grad)
        ).astype(BF16)

    by_rows(tokens_here, step)
    early_plane.finish()
    share.start()
    late_ring.middle()
    late_ring.finish()
    share.wait()


def finale_call(
    partial, normed, cot, early, up, inner, tokens, grad_middle, down, gain, chosen, count
):
    seq, rows, wide = partial.shape
    fsdp = 16
    rank, columns = up.shape
    part = (wide - SIDE) // seq
    bf16 = lambda *shape: pltpu.VMEM(shape, BF16)
    out = lambda *shape: jax.ShapeDtypeStruct(shape, BF16)
    late = columns + 2 * part
    copies = RingSum.COPIES + 2 * RingGather.COPIES + 2 * PlaneGather.COPIES + 1
    return pl.pallas_call(
        finale_kernel,
        out_shape=(
            out(rows, wide - SIDE), out(fsdp, *early.shape), out(seq, count, rank, late),
        ),
        in_specs=[ANY] * 4 + [VMEM, ANY] + [VMEM] * 5,
        out_specs=(VMEM, ANY, ANY),
        scratch_shapes=[pltpu.VMEM((rows, wide), F32)]
        + sum_buffers(rows, wide)
        + [
            bf16(seq, *inner.shape), bf16(seq * rows, 2 * part),
            bf16(fsdp, 4, rank, (late + 2 * SIDE) // 4), bf16(count, rank, late),
        ]
        + sems(copies, 4 + 2 + 3),
        compiler_params=comm_params(4),
        name="finale",
    )(partial, normed, cot, early, up, inner, tokens, grad_middle, down, gain, chosen)


def lay_out_early(whole, share, part):
    fsdp, seq, _, rank, n = whole.shape
    count = fsdp // 2

    def kernel(whole, gateup, mix_down, mix_up, gu_down, ff_down):
        for t in range(seq):
            first = jnp.concatenate([whole[0, t, 0], whole[0, t, 1]], axis=1).astype(F32)
            gateup[0, :, t * share : (t + 1) * share] = first[:, :share]
            at = (seq + t) * share
            gateup[0, :, at : at + share] = first[:, share : 2 * share]
            second = jnp.concatenate([whole[1, t, 0], whole[1, t, 1]], axis=1).astype(F32)
            for i, out in enumerate((mix_down, mix_up, gu_down)):
                out[0, :, t * part : (t + 1) * part] = second[:, i * part : (i + 1) * part]
            ff_down[0, :, t * share : (t + 1) * share] = second[:, 3 * part : 3 * part + share]

    widths = (2 * share * seq,) + (part * seq,) * 3 + (share * seq,)
    return pl.pallas_call(
        kernel,
        grid=(count,),
        out_shape=tuple(jax.ShapeDtypeStruct((count, rank, w), F32) for w in widths),
        in_specs=[pl.BlockSpec((2, seq, 2, rank, n), lambda a: (a, 0, 0, 0, 0))],
        out_specs=tuple(pl.BlockSpec((1, rank, w), lambda a: (a, 0, 0)) for w in widths),
        compiler_params=pltpu.CompilerParams(vmem_limit_bytes=32 << 20),
        name="lay_out_early",
    )(whole)


def lay_out_late(whole, columns, part):
    seq, count, rank, wide = whole.shape

    def kernel(whole, qkv_up, qkv_down, ff_up):
        for t in range(seq):
            qkv_up[0, :, t * columns : (t + 1) * columns] = whole[t, 0, :, :columns].astype(F32)
            for i, out in enumerate((qkv_down, ff_up)):
                at = columns + i * part
                out[0, :, t * part : (t + 1) * part] = whole[t, 0, :, at : at + part].astype(F32)

    widths = (columns * seq, part * seq, part * seq)
    return pl.pallas_call(
        kernel,
        grid=(count,),
        out_shape=tuple(jax.ShapeDtypeStruct((count, rank, w), F32) for w in widths),
        in_specs=[pl.BlockSpec((seq, 1, rank, wide), lambda a: (0, a, 0, 0))],
        out_specs=tuple(pl.BlockSpec((1, rank, w), lambda a: (a, 0, 0)) for w in widths),
        compiler_params=pltpu.CompilerParams(vmem_limit_bytes=32 << 20),
        name="lay_out_late",
    )(whole)


def prepare_kernel(
    places, tokens, cot, gain, q_down, q_up, m_down, m_up, g_down, gu_up, f_down, f_up, w_beta,
    conv, docs,
    payload, cots, q_side, beta_side, out_side, g_side, u_side, f_side,
    m_lines, g_lines, f_lines, q_lines, dcol, drow, taps, chosen,
):
    which, s = places[0], places[1]
    rank, width = q_down.shape[1], tokens.shape[1]
    share = g_side.shape[0]

    def lines(out, block, first):
        parts = [jnp.zeros((first, width), BF16)] if first else []
        parts += [block, jnp.zeros((SIDE - first - rank, width), BF16)]
        out[...] = jnp.concatenate(parts, axis=0)

    lines(m_lines, m_up[0], 0)
    lines(g_lines, g_down[0], rank)
    lines(f_lines, f_up[0], 0)
    lines(q_lines, q_down[0], rank)

    def turned(block, first):
        n = block.shape[1]
        parts = [jnp.zeros((first, n), F32)] if first else []
        parts += [block.astype(F32), jnp.zeros((SIDE - first - block.shape[0], n), F32)]
        return jnp.concatenate(parts, axis=0).T.astype(BF16)

    def window(ref, base):
        size = -(-share // 128) * 128
        tile = base // 128 + (s * share) // 128
        wide = ref[0, :, pl.ds(pl.multiple_of(tile * 128, 128), size)].astype(F32)
        late = jnp.concatenate([wide[:, 64:], wide[:, :64]], axis=1)
        return jnp.where(lax.rem(s, 2) == 1, late, wide)

    g_side[...] = turned(window(gu_up, 0), rank)[:share]
    u_side[...] = turned(window(gu_up, f_down.shape[2]), rank)[:share]
    f_side[...] = turned(window(f_down, 0), 0)[:share]
    out_side[...] = turned(m_down[0], 0)
    heads = taps.shape[1] // conv.shape[2]
    row = lax.broadcasted_iota(jnp.int32, w_beta.shape, 0)
    beta = w_beta[...].astype(F32)
    rows = [
        jnp.sum(jnp.where(row == s * heads + h, beta, 0.0), axis=0, keepdims=True)
        for h in range(heads)
    ]
    beta_side[...] = turned(jnp.concatenate(rows, axis=0), 0)
    q_side[...] = jnp.zeros_like(q_side)
    q_side[rank : 2 * rank, : q_up.shape[2]] = q_up[0]

    value = tokens[...].astype(F32)
    scale = lax.rsqrt(jnp.mean(value * value, axis=-1, keepdims=True) + 1e-05)
    normed = (value * scale * gain[...]).astype(BF16)
    payload[:, :width] = normed
    payload[:, width:] = mm_nt(normed, q_lines[...]).astype(BF16)
    cots[:, :width] = cot[...]
    cots[:, width:] = mm_nt(cot[...], f_lines[...]).astype(BF16)

    chunks = drow.shape[0]
    dcol[:PAD, :] = jnp.full((PAD, CH), -1, jnp.int32)
    dcol[PAD + chunks * CH :, :] = jnp.full((PAD, CH), -1, jnp.int32)
    for c in range(chunks):
        line = docs[:, c * CH : (c + 1) * CH]
        drow[c : c + 1, :] = line
        square = jnp.broadcast_to(line.astype(F32), (CH, CH)).T
        dcol[PAD + c * CH : PAD + (c + 1) * CH, :] = square.astype(jnp.int32)
    third = conv.shape[2]
    for t in range(conv.shape[0]):
        for h in range(heads):
            taps[t : t + 1, h * third : (h + 1) * third] = conv[t, pl.ds(s * heads + h, 1), :]
    lane = lax.broadcasted_iota(jnp.int32, chosen.shape, 1)
    chosen[...] = (lane == which).astype(F32).astype(BF16)


def prepare(
    places, tokens, cot, gain, q_down, q_up, m_down, m_up, g_down, gu_up, f_down, f_up, w_beta,
    conv, docs, seq,
):
    rows, width = tokens.shape
    rank = q_down.shape[1]
    columns, part, share = q_up.shape[2] // seq, width // seq, f_down.shape[2] // seq
    length = docs.shape[1]
    one = lambda n: pl.BlockSpec((1, rank, n), lambda i, p: (p[0], 0, 0))
    mine = lambda n: pl.BlockSpec((1, rank, n), lambda i, p: (p[0], 0, p[1]))
    full = lambda a: pl.BlockSpec(a.shape, lambda i, p, a=a: (0,) * a.ndim)
    S = jax.ShapeDtypeStruct
    outs = (
        S((rows, width + SIDE), BF16), S((rows, width + SIDE), BF16),
        S((SIDE, columns + SIDE), BF16), S((width, SIDE), BF16), S((part, SIDE), BF16),
        S((share, SIDE), BF16), S((share, SIDE), BF16), S((share, SIDE), BF16),
        S((SIDE, width), BF16), S((SIDE, width), BF16), S((SIDE, width), BF16),
        S((SIDE, width), BF16),
        S((length + 2 * PAD, CH), jnp.int32), S((length // CH, CH), jnp.int32),
        S((conv.shape[0], columns), F32), S((rank, SIDE), BF16),
    )
    return pl.pallas_call(
        prepare_kernel,
        out_shape=outs,
        grid_spec=pltpu.PrefetchScalarGridSpec(
            num_scalar_prefetch=1,
            grid=(1,),
            in_specs=[
                full(tokens), full(cot), full(gain), one(width), mine(columns), mine(part),
                one(width), one(width), one(gu_up.shape[2]), one(f_down.shape[2]), one(width),
                full(w_beta), full(conv), full(docs),
            ],
            out_specs=[pl.BlockSpec(o.shape, lambda i, p, o=o: (0,) * len(o.shape)) for o in outs],
        ),
        compiler_params=pltpu.CompilerParams(vmem_limit_bytes=62 << 20),
        name="prepare",
    )(places, tokens, cot, gain, q_down, q_up, m_down, m_up, g_down, gu_up, f_down, f_up, w_beta,
      conv, docs)


BOTH = ("fsdp", "seq")


def body(
    tokens,
    segments,
    adapter_index,
    attn_gain,
    w_qkv,
    w_beta,
    conv_weight,
    head_gain,
    w_out,
    ffn_gain,
    w_gateup,
    w_down,
    qkv_down,
    qkv_up,
    mixout_down,
    mixout_up,
    gateup_down,
    gateup_up,
    ffnout_down,
    ffnout_up,
    cotangent,
):
    seq = lax.axis_size("seq")
    s = lax.axis_index("seq")
    width = tokens.shape[1]
    heads = w_beta.shape[1] // seq
    count = qkv_down.shape[0]
    columns = heads * 3 * CH
    which = adapter_index[0]
    length = segments.shape[1]

    turn = lambda v: jnp.swapaxes(v, 1, 2)
    (
        payload, cots, q_side, beta_side, out_side, g_side, u_side, f_side,
        m_lines, g_lines, f_lines, q_lines, dcol, drow, taps, chosen,
    ) = prepare(
        jnp.stack([which, s]), tokens, cotangent, attn_gain[None],
        turn(qkv_down), qkv_up, turn(mixout_down), mixout_up, turn(gateup_down), gateup_up,
        turn(ffnout_down), ffnout_up, w_beta.T, conv_weight, segments, seq,
    )

    normed, wq = start_gather(payload, w_qkv, q_side, beta_side)
    normed = normed.reshape(length, -1)
    fixed = (dcol, drow, taps, head_gain[None])
    mixed, o_kept, t_kept, d_kept, s_kept, partial, joined, cot, wg, upper, wo = mixer_fwd(
        normed, wq, cots, w_gateup.T, w_out, g_side, out_side, *fixed
    )

    middle, grad_middle, partial_down, grad_mixed, early = feed_forward(
        partial, w_down, f_side, u_side, upper, wg, cot, tokens, cotangent, mixed, wo,
        m_lines, ffn_gain[None], g_lines, chosen,
    )

    partial, up, layer_out, inner, early = mixer_bwd(
        joined, partial_down, early, normed, wq, q_side, middle, f_lines, *fixed,
        grad_mixed, o_kept, t_kept, d_kept, s_kept,
    )
    input_grad, early, late = finale_call(
        partial, normed, cot.reshape(length, -1), early, up, inner,
        tokens, grad_middle, q_lines, attn_gain[None], chosen, count,
    )
    gateup_g, mixdown_g, mixup_g, gudown_g, ffdown_g = lay_out_early(
        early, w_down.shape[0] // seq, width // seq
    )
    qkvup_g, qkvdown_g, ffup_g = lay_out_late(late, columns, width // seq)
    return (
        layer_out,
        input_grad,
        turn(qkvdown_g),
        qkvup_g,
        turn(mixdown_g),
        mixup_g,
        turn(gudown_g),
        gateup_g,
        turn(ffdown_g),
        ffup_g,
    )


def solution(mesh):
    tokens, columns = P(BOTH, None), P(None, "fsdp")
    placed = (
        tokens, P("fsdp", None), P("fsdp"), P(), columns, P(), P(), P(), columns, P(), columns,
        columns, P(), P(), P(), P(), P(), P(), P(), P(), tokens,
    )
    return jax.shard_map(
        body,
        mesh=mesh,
        in_specs=placed,
        out_specs=(tokens, tokens) + (P(),) * 8,
        check_vma=False,
    )
```

time: 635 us -> 367 us (0.58)
  matrix products: 83.6 us -> 0 us
  waiting for transfers between devices: 58.1 us -> 0 us
  blocking collectives: 41.1 us -> 0 us
  local copies, waits for them, and re-layouts: 50.1 us -> 9.94 us
  other arithmetic: 22.1 us -> 0.65 us
  between operations: 15.4 us -> 1.45 us
    dot_general x23 -> x0, matrix products: 83.6 us -> none  [the longest x6 38.3 us: dot(): return jnp.dot(a, b, preferred_element_type=F32)]
    all_gather x3 -> x0, waiting for transfers between devices: 58.1 us -> none  [the longest x2 58 us: total(): whole = lax.all_gather(by_adapter, 'seq', axis=0)]
    pallas_call x5, Pallas kernels: 241 us -> 183 us  [the longest x1 120 us: feed_forward(): pl.pallas_call(feed_forward_kernel, out_shape=(jax.ShapeDtypeStruct((rows...]
    pallas_call x1, Pallas kernels: 38.7 us -> 78.9 us  [mixer_fwd(): pl.pallas_call(functools.partial(mixer_fwd_kernel, heads, chunks), out_sh...]
    all_gather x2 -> x0, blocking collectives: 31.5 us -> none  [the longest x1 19.6 us: total(): plane = lax.all_gather(piece, 'fsdp', axis=0)]
    pallas_call x1, Pallas kernels: 23.6 us -> 49.1 us  [mixer_bwd(): pl.pallas_call(functools.partial(mixer_bwd_kernel, heads, chunks), out_sh...]
    pallas_call x1, Pallas kernels: 57 us -> 42.8 us  [start_gather(): pl.pallas_call(start_kernel, out_shape=(jax.ShapeDtypeStruct((seq,) + pay...]
    transpose x12 -> x0, local copies, waits for them, and re-layouts: 13.9 us -> none  [the longest x8 10.9 us: body(): flip = lambda v: jnp.swapaxes(v, 1, 2)]
  transfers between devices with their start and end apart: 3 -> 0, of which waited for: 2 -> 0; matrix products, arithmetic and copies ran while one was open for 7% -> 0% of each run, Pallas kernels for 12% -> 0%
where the time goes in v2:
time: 367 us; the launch traced here: 366 us
  Pallas kernels  354 us (96%)
  local copies, waits for them, and re-layouts  9.94 us (3%)
    pallas_call x1, Pallas kernels, feed_forward(): pl.pallas_call(feed_forward_kernel, out_shape=(jax.ShapeDtypeStruct((rows...  120 us
    pallas_call x1, Pallas kernels, mixer_fwd(): pl.pallas_call(functools.partial(mixer_fwd_kernel, heads, chunks), out_sh...  78.9 us
    pallas_call x1, Pallas kernels, mixer_bwd(): pl.pallas_call(functools.partial(mixer_bwd_kernel, heads, chunks), out_sh...  49.1 us
    pallas_call x1, Pallas kernels, finale_call(): pl.pallas_call(finale_kernel, out_shape=(out(rows, wide - SIDE), out(fsdp...  49 us
    pallas_call x1, Pallas kernels, start_gather(): pl.pallas_call(start_kernel, out_shape=(jax.ShapeDtypeStruct((seq,) + pay...  42.8 us
    unnamed x30, local copies, waits for them, and re-layouts  9.94 us

profile of v2, /device:TPU:1, one launch (start us, length us, event | category | flops | bytes accessed | tf_op | source)
XLA Modules:
  0.0 366.2 jit_solution(9657323562209857368)
XLA Ops:
  1.3 0.7 pad_add_fusion.places
  1.9 5.1 %prepare.1 = (bf16[128,2176]{1,0:T(8,128)(2,1)}, bf16[128,2176]{1,0:T(8,128)(2,1)}, bf16[128,896]{1,0:T(8,128)(2,1)}, bf16[2048,128]{1,0:T(8,128)(2,1)}, bf16[25...) custom-call(s32[2]{0:T(128)} %pad_add_fusion.places, ...), custom_call_target="tpu_custom_call" | custom-call | tf_op jit(solution)/shard_map/prepare/pallas_call | solution.py:1624
  7.0 0.0 copy-done.2
  7.0 0.0 copy-start.4
  7.0 0.9 copy-done.4
  8.0 1.1 copy-done.5
  9.0 1.0 copy-done.7
  10.1 42.8 %start_gather.1 = (bf16[8,128,2176]{2,1,0:T(8,128)(2,1)}, bf16[2176,896]{1,0:T(8,128)(2,1)}) custom-call(bf16[128,2176]{1,0:T(8,128)(2,1)S(1)} %copy-done.5, bf16[2048,384]{1,0:T(8,128)(2,1)S(1)} %copy-done.2, bf16[128,896]{1,0:T(8,128)(2,1)S(1)} %copy-done.4, bf16[2048,128]{1,0:T(8,128)(2,1)S(1)} %copy-done.7), custom_call_target="tpu_custom_call" | custom-call | tf_op jit(solution)/shard_map/start_gather/pallas_call | solution.py:1001
  52.8 78.9 %mixer_fwd.1 = (bf16[1024,256]{1,0:T(8,128)(2,1)}, f32[2,1024,128]{2,1,0:T(8,128)}, f32[2,1024,128]{2,1,0:T(8,128)}, f32[2,1024,128]{2,1,0:T(8,128)}, f32[2,1024...) custom-call(bf16[1024,2176]{1,0:T(8,128)(2,1)} %bitcast.18, ...), custom_call_target="tpu_custom_call" | custom-call | tf_op jit(solution)/shard_map/mixer_fwd/pallas_call | solution.py:219
  131.7 120.5 %feed_forward.1 = (f32[128,2048]{1,0:T(8,128)}, f32[128,2048]{1,0:T(8,128)}, bf16[8,128,2176]{2,1,0:T(8,128)(2,1)}, bf16[1024,256]{1,0:T(8,128)(2,1)}, bf16[2,2,16,768]{3,2,1,0:T(8,128)(2,1)}) custom-call(bf16[8,128,2176]{2,1,0:T(8,128)(2,1)} %get-tuple-element.72.partial, bf16[5632,128]{1,0:T(8,128)(2,1)} %down_w.1, ...), custom_call_target="tpu_custom_call" | custom-call | tf_op jit(solution)/shard_map/feed_forward/pallas_call | solution.py:1279
  252.2 0.0 copy-start.1
  252.2 0.0 copy-start.3
  252.2 0.0 copy-start.6
  252.2 0.0 copy-start.10
  252.2 0.0 copy-start.12
  252.2 49.1 %mixer_bwd.1 = (bf16[8,128,2176]{2,1,0:T(8,128)(2,1)}, bf16[16,768]{1,0:T(8,128)(2,1)}, bf16[128,2048]{1,0:T(8,128)(2,1)}, bf16[2,16,640]{2,1,0:T(8,128)(2,1)}, bf16[8,2,16,768]{3,2,1,0:T(8,128)(2,1)}) custom-call(bf16[1024,896]{1,0:T(8,128)(2,1)} %get-tuple-element.71.source, bf16[8,128,2176]{2,1,0:T(8,128)(2,1)} %get-tuple-element.83.partial, ...), custom_call_target="tpu_custom_call" | custom-call | tf_op jit(solution)/shard_map/mixer_bwd/pallas_call | solution.py:439
  301.3 0.0 copy-done.1
  301.3 0.0 copy-done.3
  301.4 0.0 copy-done.6
  301.4 0.0 copy-done.10
  301.4 0.0 copy-done.12
  301.4 0.0 copy-start.8
  301.4 1.0 copy-done.8
  302.4 0.8 copy-done.9
  303.2 0.7 copy-done.11
  303.9 49.0 %finale.1 = (bf16[128,2048]{1,0:T(8,128)(2,1)S(1)}, bf16[16,8,2,16,768]{4,3,2,1,0:T(8,128)(2,1)}, bf16[8,8,16,1280]{3,2,1,0:T(8,128)(2,1)S(1)}) custom-call(bf16[8,128,2176]{2,1,0:T(8,128)(2,1)} %get-tuple-element.93.partial, bf16[1024,2176]{1,0:T(8,128)(2,1)} %bitcast.20, bf16[1024,2176]{1,0:T(8,128)(2,1)} %bitcast.21, ...), custom_call_target="tpu_custom_call" | custom-call | tf_op jit(solution)/shard_map/finale/pallas_call | solution.py:1463
  352.9 3.8 %lay_out_late.1 = (f32[8,16,6144]{2,1,0:T(8,128)}, f32[8,16,2048]{2,1,0:T(8,128)}, f32[8,16,2048]{2,1,0:T(8,128)}) custom-call(bf16[8,8,16,1280]{3,2,1,0:T(8,128)(2,1)S(1)} %get-tuple-element.100.whole), custom_call_target="tpu_custom_call" | custom-call | tf_op jit(solution)/shard_map/lay_out_late/pallas_call | solution.py:1520
  356.6 2.8 copy-done
  359.4 5.1 %lay_out_early.1 = (f32[8,16,11264]{2,1,0:T(8,128)}, f32[8,16,2048]{2,1,0:T(8,128)}, f32[8,16,2048]{2,1,0:T(8,128)}, f32[8,16,2048]{2,1,0:T(8,128)}, f32[8,16,5632]{2,1,0:T(8,128)}) custom-call(bf16[16,8,2,16,768]{4,3,2,1,0:T(8,128)(2,1)S(1)} %copy-done), custom_call_target="tpu_custom_call" | custom-call | tf_op jit(solution)/shard_map/lay_out_early/pallas_call | solution.py:1498
  364.6 0.0 copy-done.13
  364.6 0.8 copy.34
  365.4 0.8 copy.35
  (7 shorter events, 0.0 us)
Async XLA Ops:
  1.9 5.1 %copy-start.2 = (bf16[2048,384]{1,0:T(8,128)(2,1)S(1)}, bf16[2048,384]{1,0:T(8,128)(2,1)}, u32[]{:S(2)}) copy-start(bf16[2048,384]{1,0:T(8,128)(2,1)} %w_qkv.1) | copy-start | bytes 4718596
  7.0 0.9 copy-start.4
  8.0 1.1 copy-start.5
  9.0 1.0 copy-start.7
  252.2 49.2 %copy-start.1 = (bf16[128,2048]{1,0:T(8,128)(2,1)S(1)}, bf16[128,2048]{1,0:T(8,128)(2,1)}, u32[]{:S(2)}) copy-start(bf16[128,2048]{1,0:T(8,128)(2,1)} %tokens.5) | copy-start | bytes 1572868
  252.2 49.2 %copy-start.3 = (f32[128,2048]{1,0:T(8,128)S(1)}, f32[128,2048]{1,0:T(8,128)}, u32[]{:S(2)}) copy-start(f32[128,2048]{1,0:T(8,128)} %get-tuple-element.97.grad_middle) | copy-start | bytes 3145732
  252.2 49.2 %copy-start.6 = (bf16[128,2048]{1,0:T(8,128)(2,1)S(1)}, bf16[128,2048]{1,0:T(8,128)(2,1)}, u32[]{:S(2)}) copy-start(bf16[128,2048]{1,0:T(8,128)(2,1)} %get-tuple-element.98.down) | copy-start | bytes 1572868
  252.2 49.2 %copy-start.10 = (f32[2048]{0:T(1024)S(1)}, f32[2048]{0:T(1024)}, u32[]{:S(2)}) copy-start(f32[2048]{0:T(1024)} %param.24) | copy-start | bytes 24580
  252.2 49.2 %copy-start.12 = (bf16[16,128]{1,0:T(8,128)(2,1)S(1)}, bf16[16,128]{1,0:T(8,128)(2,1)}, u32[]{:S(2)}) copy-start(bf16[16,128]{1,0:T(8,128)(2,1)} %get-tuple-element.82.chosen) | copy-start | bytes 12292
  301.4 1.0 copy-start.8
  302.4 0.8 copy-start.9
  303.2 0.7 copy-start.11
  356.6 2.8 copy-start
  359.4 5.1 %copy-start.13 = (bf16[128,2048]{1,0:T(8,128)(2,1)S(1)}, bf16[128,2048]{1,0:T(8,128)(2,1)}, u32[]{:S(2)}) copy-start(bf16[128,2048]{1,0:T(8,128)(2,1)} %get-tuple-element.120) | copy-start | bytes 1572868

commit v3 on v2

--- a/solution.py
+++ b/solution.py
@@ -43,18 +43,24 @@
     )
 
 
-def unit_lower_inverse(lower, row, col, product):
-    near = jnp.where((row >> 3) == (col >> 3), lower, 0.0)
+def unit_lower_inverses(lowers, row, col, product):
+    each = lambda f, *lists: [f(*items) for items in zip(*lists)]
+    near = (row >> 3) == (col >> 3)
     eye = (row == col).astype(F32)
-    second = product(near, near)
-    fourth = product(second, second)
-    inverse = eye - near + second - product(near, second)
-    inverse = inverse + product(inverse, fourth)
+    first = [jnp.where(near, lower, 0.0) for lower in lowers]
+    second = each(product, first, first)
+    fourth = each(product, second, second)
+    third = each(product, first, second)
+    inverses = each(lambda a, b, c: eye - a + b - c, first, second, third)
+    last = each(product, inverses, fourth)
+    inverses = each(lambda a, b: a + b, inverses, last)
     for bits in (3, 4, 5, 6):
         joining = ((row >> (bits + 1)) == (col >> (bits + 1))) & ((row >> bits) != (col >> bits))
-        below = jnp.where(joining, lower, 0.0)
-        inverse = inverse - product(inverse, product(below, inverse))
-    return inverse
+        below = [jnp.where(joining, lower, 0.0) for lower in lowers]
+        below = each(product, below, inverses)
+        below = each(product, inverses, below)
+        inverses = each(lambda a, b: a - b, inverses, below)
+    return inverses
 
 
 def sigmoid(v):
@@ -98,9 +104,9 @@
 
 
 def mixer_fwd_kernel(
-    heads, chunks, normed, weight, cot, gate_t, w_out, g_side, out_side,
+    heads, chunks, normed, weight, cot, w_out, w_down, out_side, f_side,
     dcol, drow, taps, gain,
-    mixed, o_out, t_out, d_out, s_out, partial, joined_out, everyone, wg, upper, wo,
+    mixed, o_out, t_out, d_out, s_out, partial, joined_out, everyone, wo, wd,
     joined, rows_v, weight_v, wo_v, q_s, k_s, u_s, w_s, p_s, sem, send, recv, local,
 ):
     loads = [
@@ -109,9 +115,9 @@
     ]
     for copy in loads:
         copy.start()
-    greet(ring_peers(), all_plane())
+    greet(ring_peers(), line_peers())
     feed = Feed(
-        Line(send, recv, local), cot, gate_t, w_out, (out_side, g_side), everyone, wg, wo, upper
+        Line(send, recv, local), cot, (w_out, w_down), (out_side, f_side), everyone, (wo, wd)
     )
     feed.start()
     joined[pl.ds(0, PAD), :] = jnp.zeros((PAD, joined.shape[1]), BF16)
@@ -129,22 +135,28 @@
     row = lax.broadcasted_iota(jnp.int32, (CH, CH), 0)
     col = lax.broadcasted_iota(jnp.int32, (CH, CH), 1)
 
-    def prepare(c, h, docs, same, live, act, raws):
-        start = pl.multiple_of(c * CH, CH)
-        rows = pl.ds(start, CH)
-        query, keys, values, _, _ = normal_parts(act[:, h * 3 * CH : (h + 1) * 3 * CH])
-        beta = sigmoid(raws[:, h : h + 1])
-        inner = mm_nt(keys, keys)
-        lower = jnp.where(same & (row > col), inner * beta, 0.0)
-        inverse = unit_lower_inverse(lower, row, col, mm_fine)
-        t_out[h, rows, :] = inverse
-        both = mm(inverse, jnp.concatenate([values * beta, keys * (beta * live)], axis=1))
-        u_s[h, rows, :] = both[:, :CH]
-        w_s[h, rows, :] = both[:, CH:].astype(BF16)
-        scores = jnp.where(same & (row >= col), mm_nt(query, keys), 0.0)
-        p_s[h, rows, :] = scores.astype(BF16)
-        q_s[h, rows, :] = (query * live).astype(BF16)
-        k_s[h, rows, :] = keys
+    def prepare(items):
+        lowers, parts = [], []
+        for c, docs, same, live, act, raws in items:
+            for h in range(heads):
+                query, keys, values, _, _ = normal_parts(act[:, h * 3 * CH : (h + 1) * 3 * CH])
+                beta = sigmoid(raws[:, h : h + 1])
+                inner = mm_nt(keys, keys)
+                lowers.append(jnp.where(same & (row > col), inner * beta, 0.0))
+                rows = pl.ds(pl.multiple_of(c * CH, CH), CH)
+                scores = jnp.where(same & (row >= col), mm_nt(query, keys), 0.0)
+                p_s[h, rows, :] = scores.astype(BF16)
+                q_s[h, rows, :] = (query * live).astype(BF16)
+                k_s[h, rows, :] = keys
+                targets = jnp.concatenate([values * beta, keys * (beta * live)], axis=1)
+                parts.append((h, rows, targets.astype(BF16)))
+        inverses = unit_lower_inverses(lowers, row, col, mm_fine)
+        for inverse, (h, rows, targets) in zip(inverses, parts):
+            inverse = inverse.astype(BF16)
+            t_out[h, rows, :] = inverse
+            both = mm(inverse, targets)
+            u_s[h, rows, :] = both[:, :CH]
+            w_s[h, rows, :] = both[:, CH:].astype(BF16)
 
     def first(step, carry):
         feed.stage(step)
@@ -156,9 +168,7 @@
             act = conv * sigmoid(conv)
             parts.append((c, docs, same, live, act, raw_chunk(c, joined, taps)))
         project(jnp.minimum(step + 1, chunks // 2 - 1))
-        for c, docs, same, live, act, raws in parts:
-            for h in range(heads):
-                prepare(c, h, docs, same, live, act, raws)
+        prepare(parts)
         return carry
 
     lax.fori_loop(0, chunks // 2, first, 0)
@@ -169,14 +179,14 @@
     def second(c, states):
         rows = pl.ds(pl.multiple_of(c * CH, CH), CH)
         docs, same, live, tail, live_last = chunk_masks(c, dcol, drow)
-        after = []
         for h in range(heads):
-            state = states[h]
-            s_out[h, rows, :] = state
-            update = u_s[h, rows, :] - mm(w_s[h, rows, :], state)
-            d_out[h, rows, :] = update
-            after.append(state * live_last + mm_tn(k_s[h, rows, :] * tail, update))
-        return tuple(after)
+            s_out[h, rows, :] = states[h].astype(BF16)
+        recalled = [mm(w_s[h, rows, :], states[h]) for h in range(heads)]
+        updates = [u_s[h, rows, :] - recalled[h] for h in range(heads)]
+        added = [mm_tn(k_s[h, rows, :] * tail, updates[h]) for h in range(heads)]
+        for h in range(heads):
+            d_out[h, rows, :] = updates[h].astype(BF16)
+        return tuple(states[h] * live_last + added[h] for h in range(heads))
 
     zero = jnp.zeros((CH, CH), F32)
     lax.fori_loop(0, chunks, second, (zero,) * heads)
@@ -187,13 +197,16 @@
 
     def third(c, carry):
         rows = pl.ds(pl.multiple_of(c * CH, CH), CH)
-        for h in range(heads):
-            out = mm(
+        outs = [
+            mm(
                 jnp.concatenate([q_s[h, rows, :], p_s[h, rows, :]], axis=1),
                 jnp.concatenate(
-                    [s_out[h, rows, :].astype(BF16), d_out[h, rows, :].astype(BF16)], axis=0
+                    [s_out[h, rows, :], d_out[h, rows, :]], axis=0
                 ),
             )
+            for h in range(heads)
+        ]
+        for h, out in enumerate(outs):
             o_out[h, rows, :] = out
             scale = lax.rsqrt(jnp.mean(out * out, axis=-1, keepdims=True) + 1e-05)
             mixed[rows, h * CH : (h + 1) * CH] = (out * scale * gain[...]).astype(BF16)
@@ -206,25 +219,25 @@
 
 
 def mixer_fwd(
-    normed, weight, cot, gate_t, w_out, g_side, out_side, dcol, drow, taps, gain
+    normed, weight, cot, w_out, w_down, out_side, f_side, dcol, drow, taps, gain
 ):
     tokens, across = normed.shape
     wide = weight.shape[1]
     heads = wide // (3 * CH)
     chunks = tokens // CH
     seq = lax.axis_size("seq")
-    square = jax.ShapeDtypeStruct((heads, tokens, CH), F32)
     out = lambda *shape: jax.ShapeDtypeStruct(shape, BF16)
-    share, part = g_side.shape[0], out_side.shape[0]
+    square = out(heads, tokens, CH)
+    share, part = f_side.shape[0], out_side.shape[0]
     return pl.pallas_call(
         functools.partial(mixer_fwd_kernel, heads, chunks),
         out_shape=(
-            out(tokens, heads * CH), square, square, square, square,
+            out(tokens, heads * CH), jax.ShapeDtypeStruct(square.shape, F32), square, square, square,
             out(chunks, CH, across), out(tokens, wide), out(seq, *cot.shape),
-            out(share, across), out(share, 128), out(part, across),
+            out(part, across), out(share, across),
         ),
         in_specs=[ANY] * 7 + [VMEM] * 4,
-        out_specs=(VMEM,) * 6 + (ANY,) * 5,
+        out_specs=(VMEM,) * 6 + (ANY,) * 4,
         scratch_shapes=[
             pltpu.VMEM((tokens + PAD, wide), BF16),
             pltpu.VMEM((tokens, across), BF16),
@@ -238,17 +251,20 @@
             pltpu.SemaphoreType.DMA((2,)),
         ]
         + sems(Feed.COPIES, Feed.LOCAL),
-        compiler_params=comm_params(1, 56),
+        compiler_params=comm_params(1, 62),
         name="mixer_fwd",
-    )(normed, weight, cot, gate_t, w_out, g_side, out_side, dcol, drow, taps, gain)
+    )(normed, weight, cot, w_out, w_down, out_side, f_side, dcol, drow, taps, gain)
 
 
 def mixer_bwd_kernel(
-    heads, chunks, source, partial, early, normed, weight, q_side, values, up,
-    dcol, drow, taps, gain, grad, o_in, t_in, d_in, s_in,
-    back_partial, up_out, layer_out, inner_out, early_out,
+    heads, chunks, source, partial, early, normed, weight, cot, q_side, values, up,
+    dcol, drow, taps, gain, grad, o_in, t_in, d_in, s_in, tokens, grad_middle, down, attn_gain,
+    chosen, layer_out, input_grad, early_whole, up_whole, low_whole,
     joined, e_s, f_s, w_s, x_s, ds_s, go_s, dj_s, side_v, weight_v, sem,
-    total, own, stage, relay, away, back, early_pieces, early_sum, send, recv, local,
+    total, own, stage, relay, away, back, early_pieces, early_sum, early_ring,
+    back_partial, stage2, relay2, away2, back2, inner, inners, sides,
+    up_pieces, up_sum, low_pieces, low_sum,
+    send, recv, local,
 ):
     loads = [
         pltpu.make_async_copy(source, joined.at[pl.ds(PAD, source.shape[0]), :], sem.at[0]),
@@ -259,14 +275,50 @@
     ]
     for copy in loads:
         copy.start()
-    greet(ring_peers(), line_peers())
+    greet(all_seq(), line_peers())
     line = Line(send, recv, local)
     ring = RingSum(line, partial, (own, stage, relay, away, back))
-    sums = EarlySum(line, early, early_pieces, early_sum, early_out)
+    sums = EarlySum(line, early, early_pieces, early_sum, early_ring)
+    second_sum = RingSum(line, back_partial, (None, stage2, relay2, away2, back2))
+    s, partner, _, _, _ = seq_places()
+    f = lax.axis_index("fsdp")
+    core = lax.rem(s, 2)
+    inner_spread = Spread(line, "seq", 8, inner, lambda t: inners.at[t])
+    up_ring = RingGather(line, up_sum, up_whole)
+    low_ring = RingGather(line, low_sum, low_whole)
+
+    def early_place(t, half, quarter):
+        first = core * 4 + half * 2 + (quarter or 0)
+        return early_whole.at[t, pl.ds(first, 2 if quarter is None else 1)]
+
+    def piece_place(pieces):
+        def place(t, half, quarter):
+            first = half * 2 + (quarter or 0)
+            return pieces.at[t, pl.ds(first, 2 if quarter is None else 1)]
+
+        return place
+
+    early_plane = PlaneGather(line, early_place)
+    up_plane = PlaneGather(line, piece_place(up_pieces))
+    low_plane = PlaneGather(line, piece_place(low_pieces))
+    at, local_at = line.take(1, 3)
+    half_slices = pl.ds(core * 4, 4)
+    retain = line.local(local_at, early_ring.at[half_slices], early_whole.at[f, half_slices])
+    share = line.copy(
+        at, early_whole.at[:, half_slices], early_whole.at[:, half_slices], {"seq": partner}
+    )
+    part = sides.shape[1] // 2
+    mine = pl.ds(pl.multiple_of(s * part, 128), part)
+    fetch = [
+        line.local(local_at + 1, normed.at[:, mine], sides.at[:, pl.ds(0, part)]),
+        line.local(local_at + 2, cot.at[:, mine], sides.at[:, pl.ds(part, part)]),
+    ]
+    for copy in fetch:
+        copy.start()
     ring.start()
     sums.start()
     joined[pl.ds(0, PAD), :] = jnp.zeros((PAD, joined.shape[1]), BF16)
-    dj_s[pl.ds((chunks - 1) * CH, CH), :] = jnp.zeros((CH, dj_s.shape[1]), BF16)
+    dj_s[pl.ds((chunks - 2) * CH, 2 * CH), :] = jnp.zeros((2 * CH, dj_s.shape[1]), BF16)
     for copy in loads:
         copy.wait()
     row = lax.broadcasted_iota(jnp.int32, (CH, CH), 0)
@@ -279,30 +331,43 @@
         raws = raw_chunk(c, joined, taps)
         return docs, same, live, tail, live_last, conv, raws
 
-    def first(c, carry):
-        pl.when(c == chunks // 2)(sums.plane.second)
-        docs, same, live, tail, live_last, conv, raws = revive(c)
-        act = conv * sigmoid(conv)
-        rows = pl.ds(pl.multiple_of(c * CH, CH), CH)
-        for h in range(heads):
-            query, keys, values, _, _ = normal_parts(act[:, h * width : (h + 1) * width])
-            beta = sigmoid(raws[:, h : h + 1])
-            out = o_in[h, rows, :]
-            weighted = grad[rows, h * CH : (h + 1) * CH].astype(F32) * gain[...]
-            scale = lax.rsqrt(jnp.mean(out * out, axis=-1, keepdims=True) + 1e-05)
-            grad_o = scale * weighted - out * (
-                scale * scale * scale * jnp.mean(weighted * out, axis=-1, keepdims=True)
-            )
-            go_s[h, rows, :] = grad_o
-            scores = jnp.where(same & (row >= col), mm_nt(query, keys), 0.0)
-            ef = mm_tn(jnp.concatenate([scores, query * live], axis=1), grad_o)
+    def first(step, carry):
+        pl.when(step == 2)(sums.plane.second)
+        items = []
+        for part in range(2):
+            c = step * 2 + part
+            docs, same, live, tail, live_last, conv, raws = revive(c)
+            act = conv * sigmoid(conv)
+            rows = pl.ds(pl.multiple_of(c * CH, CH), CH)
+            for h in range(heads):
+                query, keys, values, _, _ = normal_parts(act[:, h * width : (h + 1) * width])
+                beta = sigmoid(raws[:, h : h + 1])
+                out = o_in[h, rows, :]
+                weighted = grad[rows, h * CH : (h + 1) * CH].astype(F32) * gain[...]
+                scale = lax.rsqrt(jnp.mean(out * out, axis=-1, keepdims=True) + 1e-05)
+                grad_o = scale * weighted - out * (
+                    scale * scale * scale * jnp.mean(weighted * out, axis=-1, keepdims=True)
+                )
+                go_s[h, rows, :] = grad_o
+                x_s[h, rows, :] = keys * tail
+                known = (keys * (beta * live)).astype(BF16)
+                items.append((h, rows, same, query, keys, (query * live), grad_o, known))
+        scores = [mm_nt(query, keys) for _, _, _, query, keys, _, _, _ in items]
+        recalls = [mm(t_in[h, rows, :], known) for h, rows, _, _, _, _, _, known in items]
+        scores = [
+            jnp.where(item[2] & (row >= col), score, 0.0) for item, score in zip(items, scores)
+        ]
+        both = [
+            mm_tn(jnp.concatenate([score, item[5]], axis=1), item[6])
+            for item, score in zip(items, scores)
+        ]
+        for (h, rows, *_), ef, recall in zip(items, both, recalls):
             e_s[h, rows, :] = ef[:CH]
             f_s[h, rows, :] = ef[CH:]
-            w_s[h, rows, :] = mm(t_in[h, rows, :], keys * (beta * live)).astype(BF16)
-            x_s[h, rows, :] = keys * tail
+            w_s[h, rows, :] = recall.astype(BF16)
         return carry
 
-    lax.fori_loop(0, chunks, first, 0)
+    lax.fori_loop(0, chunks // 2, first, 0)
     ring.middle()
     sums.plane.third()
 
@@ -310,16 +375,16 @@
         c = chunks - 1 - step
         rows = pl.ds(pl.multiple_of(c * CH, CH), CH)
         docs, same, live, tail, live_last = chunk_masks(c, dcol, drow)
-        before = []
         for h in range(heads):
-            state = states[h]
-            ds_s[h, rows, :] = state
-            grad_update = e_s[h, rows, :] + mm(x_s[h, rows, :], state)
-            x_s[h, rows, :] = grad_update
-            before.append(
-                state * live_last + f_s[h, rows, :] - mm_tn(w_s[h, rows, :], grad_update)
-            )
-        return tuple(before)
+            ds_s[h, rows, :] = states[h]
+        passed = [mm(x_s[h, rows, :], states[h]) for h in range(heads)]
+        grads = [e_s[h, rows, :] + passed[h] for h in range(heads)]
+        taken = [mm_tn(w_s[h, rows, :], grads[h]) for h in range(heads)]
+        for h in range(heads):
+            x_s[h, rows, :] = grads[h]
+        return tuple(
+            states[h] * live_last + f_s[h, rows, :] - taken[h] for h in range(heads)
+        )
 
     zero = jnp.zeros((CH, CH), F32)
     lax.fori_loop(0, chunks, second, (zero,) * heads)
@@ -331,141 +396,244 @@
         grads = dj_s[rows, :]
         back_partial[c] = mm_nt(grads, weight_v[...]).astype(BF16)
 
+    def send_near(chip, ready):
+        for k, d in enumerate((2, 1, 3, 0)):
+            here = ready & (lax.rem(s // 2 + d, 4) == chip)
+            pl.when(here)(lambda: second_sum.near(k).start())
+
     def third(step, after):
-        c = chunks - 1 - step
-        pl.when(step == chunks // 4)(ring.last)
-        pl.when(step == chunks // 4)(sums.add)
-        pl.when(step == chunks - 1)(sums.ring.middle)
-        project(jnp.minimum(c + 1, chunks - 1))
-        docs, same, live, tail, live_last, conv, raws = revive(c)
-        gate = sigmoid(conv)
-        act = conv * gate
-        slope = gate * (1.0 + conv * (1.0 - gate))
-        rows = pl.ds(pl.multiple_of(c * CH, CH), CH)
+        pl.when(step == 0)(sums.add)
+        pl.when(step == 1)(ring.last)
+        pl.when(step == 1)(sums.ring.middle)
+
+        @pl.when(step == 2)
+        def _():
+            sums.ring.finish()
+            retain.start()
+            retain.wait()
+            early_plane.first()
+
+        pl.when(step == 3)(early_plane.second)
+        later = chunks - 1 - 2 * step
+        for part in range(2):
+            project(jnp.minimum(later + 2 - part, chunks - 1 - part))
+        send_near(jnp.minimum(later + 1, chunks) // 2, step > 0)
+        chunk_items, items = [], []
+        for part in range(2):
+            c = later - part
+            docs, same, live, tail, live_last, conv, raws = revive(c)
+            gate = sigmoid(conv)
+            act = conv * gate
+            slope = gate * (1.0 + conv * (1.0 - gate))
+            rows = pl.ds(pl.multiple_of(c * CH, CH), CH)
+            chunk_items.append((c, rows, slope))
+            for h in range(heads):
+                cut = act[:, h * width : (h + 1) * width]
+                beta = sigmoid(raws[:, h : h + 1])
+                items.append((h, rows, same, live, tail, beta, cut) + normal_parts(cut))
+        targets = [mm_tn(t_in[h, rows, :], x_s[h, rows, :]) for h, rows, *_ in items]
+        pairs = [
+            mm_nt(jnp.concatenate([target, go_s[h, rows, :]], axis=0), d_in[h, rows, :])
+            for (h, rows, *_), target in zip(items, targets)
+        ]
+        backs = [
+            mm_nt(
+                jnp.concatenate([go_s[h, rows, :] * live, -target * (beta * live)], axis=0),
+                s_in[h, rows, :],
+            )
+            for (h, rows, _, live, _, beta, *_), target in zip(items, targets)
+        ]
+        inners = [mm_nt(item[8], item[8]) for item in items]
+        recalls = [mm(item[8], s_in[item[0], item[1], :]) for item in items]
+        ends = [
+            mm_nt(d_in[h, rows, :].astype(F32) * tail, ds_s[h, rows, :])
+            for h, rows, _, _, tail, *_ in items
+        ]
+        lowers = [
+            jnp.where(item[2] & (row > col), -pair[:CH], 0.0) for item, pair in zip(items, pairs)
+        ]
+        scores = [
+            jnp.where(item[2] & (row >= col), pair[CH:], 0.0) for item, pair in zip(items, pairs)
+        ]
+        grad_inners = [lower * item[5] for item, lower in zip(items, lowers)]
+        turned = [
+            mm_tn(
+                jnp.concatenate([score, grad_inner], axis=0),
+                jnp.concatenate([item[7], item[8]], axis=0),
+            )
+            for item, score, grad_inner in zip(items, scores, grad_inners)
+        ]
+        straight = [
+            mm(jnp.concatenate([score, grad_inner], axis=0), item[8])
+            for item, score, grad_inner in zip(items, scores, grad_inners)
+        ]
         lane = lax.broadcasted_iota(jnp.int32, (CH, CH), 1)
-        grad_raw = jnp.zeros((CH, CH), F32)
-        grads = []
-        for h in range(heads):
-            part = act[:, h * width : (h + 1) * width]
-            query, keys, values, q_scale, k_scale = normal_parts(part)
-            beta = sigmoid(raws[:, h : h + 1])
-            state, update, state_grad = s_in[h, rows, :], d_in[h, rows, :], ds_s[h, rows, :]
-            grad_o = go_s[h, rows, :]
-            grad_target = mm_tn(t_in[h, rows, :], x_s[h, rows, :])
-            pair = mm_nt(jnp.concatenate([grad_target, grad_o], axis=0), update)
-            grad_lower = jnp.where(same & (row > col), -pair[:CH], 0.0)
-            grad_scores = jnp.where(same & (row >= col), pair[CH:], 0.0)
-            inner = mm_nt(keys, keys)
-            recalled = mm(keys, state)
-            grad_beta = jnp.sum(
-                grad_lower * inner + grad_target * (values - live * recalled),
-                axis=-1,
-                keepdims=True,
-            )
-            grad_inner = grad_lower * beta
-            back = mm_nt(
-                jnp.concatenate([grad_o * live, -grad_target * (beta * live)], axis=0), state
-            )
-            grad_query = back[:CH] + mm(grad_scores, keys)
-            grad_keys = (
-                back[CH:]
-                + mm_tn(
-                    jnp.concatenate([grad_scores, grad_inner], axis=0),
-                    jnp.concatenate([query, keys], axis=0),
+        for part, (c, rows, slope) in enumerate(chunk_items):
+            grads, grad_raw = [], jnp.zeros((CH, CH), F32)
+            for h in range(heads):
+                k = part * heads + h
+                _, _, _, live, _, beta, cut, query, keys, values, q_scale, k_scale = items[k]
+                target, back = targets[k], backs[k]
+                grad_beta = jnp.sum(
+                    lowers[k] * inners[k] + target * (values - live * recalls[k]),
+                    axis=-1,
+                    keepdims=True,
                 )
-                + mm(grad_inner, keys)
-                + mm_nt(update * tail, state_grad)
-            )
-            grad_values = grad_target * beta
-            raw_q, raw_k = part[:, :CH], part[:, CH : 2 * CH]
-            grad_query = grad_query * CH**-0.5
-            grad_q = q_scale * grad_query - raw_q * (
-                q_scale * q_scale * q_scale * jnp.sum(grad_query * raw_q, axis=-1, keepdims=True)
-            )
-            grad_k = k_scale * grad_keys - raw_k * (
-                k_scale * k_scale * k_scale * jnp.sum(grad_keys * raw_k, axis=-1, keepdims=True)
-            )
-            grads += [grad_q, grad_k, grad_values]
-            grad_raw = jnp.where(lane == h, grad_beta * beta * (1.0 - beta), grad_raw)
-        dj_s[rows, heads * width :] = grad_raw.astype(BF16)
-        grads = jnp.concatenate(grads, axis=1) * slope
-        window = jnp.concatenate([grads, after], axis=0)
-        ids = dcol[pl.ds(pl.multiple_of(c * CH + PAD, PAD), CH + PAD), :]
-        total_ = grads * taps[3:4, :]
-        for lag in (1, 2, 3):
-            keep = (ids[lag : lag + CH] == ids[:CH]).astype(F32)
-            keep = jnp.concatenate([keep] * (heads * 3), axis=1)
-            total_ = total_ + window[lag : lag + CH] * keep * taps[3 - lag : 4 - lag, :]
-        dj_s[rows, : heads * width] = total_.astype(BF16)
-        return grads[:8]
-
-    lax.fori_loop(0, chunks, third, jnp.zeros((8, heads * width), F32))
+                grad_query = (back[:CH] + straight[k][:CH]) * CH**-0.5
+                grad_keys = back[CH:] + turned[k] + straight[k][CH:] + ends[k]
+                raw_q, raw_k = cut[:, :CH], cut[:, CH : 2 * CH]
+                grad_q = q_scale * grad_query - raw_q * (
+                    q_scale * q_scale * q_scale
+                    * jnp.sum(grad_query * raw_q, axis=-1, keepdims=True)
+                )
+                grad_k = k_scale * grad_keys - raw_k * (
+                    k_scale * k_scale * k_scale
+                    * jnp.sum(grad_keys * raw_k, axis=-1, keepdims=True)
+                )
+                grads += [grad_q, grad_k, target * beta]
+                grad_raw = jnp.where(lane == h, grad_beta * beta * (1.0 - beta), grad_raw)
+            dj_s[rows, heads * width :] = grad_raw.astype(BF16)
+            grads = jnp.concatenate(grads, axis=1) * slope
+            window = jnp.concatenate([grads, after], axis=0)
+            ids = dcol[pl.ds(pl.multiple_of(c * CH + PAD, PAD), CH + PAD), :]
+            total_ = grads * taps[3:4, :]
+            for lag in (1, 2, 3):
+                keep = (ids[lag : lag + CH] == ids[:CH]).astype(F32)
+                keep = jnp.concatenate([keep] * (heads * 3), axis=1)
+                total_ = total_ + window[lag : lag + CH] * keep * taps[3 - lag : 4 - lag, :]
+            dj_s[rows, : heads * width] = total_.astype(BF16)
+            after = grads[:8]
+        return after
+
+    lax.fori_loop(0, chunks // 2, third, jnp.zeros((8, heads * width), F32))
+    project(1)
     project(0)
-    up_out[...] = mm_tn(side_v[...], dj_s[:, : heads * width])[
-        up_out.shape[0] : 2 * up_out.shape[0]
-    ].astype(BF16)
-    sums.ring.finish()
+    send_near(0, s >= 0)
+    rank, n = inner.shape[1:]
+
+    def put(pieces, piece):
+        size = pieces.shape[3]
+        for q in range(4):
+            pieces[f, q] = piece[:, q * size : (q + 1) * size]
+
+    up_piece = mm_tn(side_v[...], dj_s[:, : heads * width])[rank : 2 * rank].astype(BF16)
+    put(up_pieces, jnp.concatenate([up_piece, chosen[...], chosen[...]], axis=1))
+    up_plane.first()
     ring.finish(total)
     across = values.shape[1]
-    rank, n = inner_out.shape[1:]
     q_inner = mm_nt(q_side[...], dj_s[...])[rank : 2 * rank].astype(BF16)
     f_inner = total[:, across:].T[:rank].astype(BF16)
-    inner_out[0] = q_inner[:, :n]
+    inner[0] = q_inner[:, :n]
     rest = 2 * n - q_inner.shape[1] - f_inner.shape[1]
-    inner_out[1] = jnp.concatenate(
-        [q_inner[:, n:], f_inner, jnp.zeros((rank, rest), BF16)], axis=1
-    )
-
-    def step(rows):
+    inner[1] = jnp.concatenate([q_inner[:, n:], f_inner, jnp.zeros((rank, rest), BF16)], axis=1)
+    inner_spread.start()
+    second_sum.middle()
+    early_plane.third()
+    up_plane.second()
+
+    def layer_rows(rows):
         inner = total[rows, across:].astype(BF16)
         layer_out[rows, :] = (
             values[rows, :] + (total[rows, :across] + mm(inner, up[...]))
         ).astype(BF16)
 
-    by_rows(values.shape[0], step)
+    by_rows(values.shape[0], layer_rows)
+    for copy in fetch:
+        copy.wait()
+    inner_spread.arrive()
+    tokens_here = tokens.shape[0]
+    ahead = sides.shape[0] - n
+    added, beside = [None, None], []
+    for t in range(inners.shape[0]):
+        parts = inners[t, 0].astype(F32), inners[t, 1].astype(F32)[:, :ahead]
+        added = [p if sum_ is None else sum_ + p for p, sum_ in zip(parts, added)]
+        beside.append(inners[t, 1][:, ahead : ahead + tokens_here])
+    down_piece = mm(jnp.concatenate(added, axis=1), sides[:, :part])
+    ff_piece = mm(jnp.concatenate(beside, axis=1), sides[:, part:])
+    put(low_pieces, jnp.concatenate([down_piece, ff_piece], axis=1).astype(BF16))
+    low_plane.first()
+    up_plane.third()
+    second_sum.last()
+    low_plane.second()
+    up_plane.fourth()
+    early_plane.fourth()
+    up_plane.finish()
+    marks = up_pieces.at[:, 3]
+    by_adapter(up_pieces, marks, 0, up_sum)
+    up_ring.start()
+    low_plane.third()
+    low_plane.fourth()
+    early_plane.finish()
+    share.start()
+    low_plane.finish()
+    by_adapter(low_pieces, marks, 0, low_sum)
+    low_ring.start()
+    second_sum.finish(total)
+
+    def input_rows(rows):
+        grad_normed = total[rows, :across] + mm(total[rows, across:], down[...])
+        input_grad[rows, :] = (
+            grad_middle[rows, :]
+            + norm_back_rows(tokens[rows, :].astype(F32), attn_gain[...], grad_normed)
+        ).astype(BF16)
+
+    by_rows(tokens_here, input_rows)
+    up_ring.middle()
+    low_ring.middle()
+    up_ring.finish()
+    low_ring.finish()
+    share.wait()
+    inner_spread.finish()
 
 
 def mixer_bwd(
-    joined, partial, early, normed, weight, q_side, values, up, dcol, drow, taps, gain,
-    grad, o, t, d, s,
+    joined, partial, early, normed, weight, cot, q_side, values, up, dcol, drow, taps, gain,
+    grad, o, t, d, s, tokens, grad_middle, down, attn_gain, chosen, count,
 ):
-    tokens, wide = joined.shape
+    length, wide = joined.shape
     heads = wide // (3 * CH)
-    chunks = tokens // CH
-    square = (heads, tokens, CH)
+    chunks = length // CH
+    square = (heads, length, CH)
     rows, across = values.shape
-    seq, rank = lax.axis_size("seq"), early.shape[2]
+    seq, fsdp, rank = lax.axis_size("seq"), 16, early.shape[2]
+    part = across // seq
+    columns = heads * 3 * CH
     out = lambda *shape: jax.ShapeDtypeStruct(shape, BF16)
+    bf16 = lambda *shape: pltpu.VMEM(shape, BF16)
+    f32 = lambda *shape: pltpu.VMEM(shape, F32)
+    buffers = sum_buffers(rows, across + SIDE)
+    copies = 2 * RingSum.COPIES + EarlySum.COPIES + 2 * RingGather.COPIES + 3 * PlaneGather.COPIES
     return pl.pallas_call(
         functools.partial(mixer_bwd_kernel, heads, chunks),
         out_shape=(
-            out(chunks, CH, across + SIDE), out(rank, heads * 3 * CH),
-            out(rows, across), out(2, rank, 640), out(seq, *early.shape[1:]),
+            out(rows, across), out(rows, across),
+            out(fsdp, seq, *early.shape[1:]),
+            out(seq, count, rank, columns), out(seq, count, rank, 2 * part),
         ),
-        in_specs=[ANY] * 5 + [VMEM] * 12,
-        out_specs=(VMEM,) * 4 + (ANY,),
+        in_specs=[ANY] * 6 + [VMEM] * 17,
+        out_specs=(VMEM, VMEM, ANY, ANY, ANY),
         scratch_shapes=[
-            pltpu.VMEM((tokens + PAD, wide), BF16),
-            pltpu.VMEM(square, F32),
-            pltpu.VMEM(square, F32),
-            pltpu.VMEM(square, BF16),
-            pltpu.VMEM(square, F32),
-            pltpu.VMEM(square, F32),
-            pltpu.VMEM(square, F32),
-            pltpu.VMEM((tokens, wide), BF16),
-            pltpu.VMEM((tokens, SIDE), BF16),
-            pltpu.VMEM(weight.shape, BF16),
-            pltpu.SemaphoreType.DMA((3,)),
-            pltpu.VMEM((rows, across + SIDE), F32),
+            bf16(length + PAD, wide), f32(*square), f32(*square), bf16(*square), f32(*square),
+            f32(*square), f32(*square), bf16(length, wide), bf16(length, SIDE),
+            bf16(*weight.shape), pltpu.SemaphoreType.DMA((3,)), f32(rows, across + SIDE),
         ]
-        + sum_buffers(rows, across + SIDE)
-        + [pltpu.VMEM((16,) + early.shape, BF16), pltpu.VMEM(early.shape[1:], BF16)]
-        + sems(RingSum.COPIES + EarlySum.COPIES, RingSum.LOCAL + EarlySum.LOCAL),
-        compiler_params=comm_params(5, 60),
+        + buffers
+        + [
+            bf16(fsdp, *early.shape), bf16(*early.shape[1:]), bf16(seq, *early.shape[1:]),
+            bf16(seq, rows, across + SIDE),
+        ]
+        + buffers[1:]
+        + [
+            bf16(2, rank, 640), bf16(seq, 2, rank, 640), bf16(length, 2 * part),
+            bf16(fsdp, 4, rank, (columns + 2 * SIDE) // 4), bf16(count, rank, columns),
+            bf16(fsdp, 4, rank, part // 2), bf16(count, rank, 2 * part),
+        ]
+        + sems(copies + 7 + 1, 2 * RingSum.LOCAL + EarlySum.LOCAL + 3 + 3),
+        compiler_params=comm_params(4, 60),
         name="mixer_bwd",
     )(
-        joined, partial, early, normed, weight, q_side, values, up, dcol, drow, taps, gain,
-        grad, o, t, d, s,
+        joined, partial, early, normed, weight, cot, q_side, values, up, dcol, drow, taps, gain,
+        grad, o, t, d, s, tokens, grad_middle, down, attn_gain, chosen,
     )
 
 MESH = pl.DeviceIdType.MESH
@@ -519,6 +687,11 @@
 def ring_peers():
     s, partner, right, left, far = seq_places()
     return [partner, right, left]
+
+
+def all_seq():
+    s = lax.axis_index("seq")
+    return [lax.rem(s + d, 8) for d in range(1, 8)]
 
 
 def all_plane():
@@ -772,6 +945,35 @@
                     self.copy(j, d).wait_send()
 
 
+class Spread:
+    def __init__(self, line, axis, count, block, slot):
+        self.line, self.axis, self.count, self.block, self.slot = line, axis, count, block, slot
+        self.at, self.local_at = line.take(count - 1, 1)
+
+    def copy(self, d):
+        me = lax.axis_index(self.axis)
+        return self.line.copy(
+            self.at + d - 1, self.block, self.slot(me), {self.axis: lax.rem(me + d, self.count)}
+        )
+
+    def own(self):
+        return self.line.local(self.local_at, self.block, self.slot(lax.axis_index(self.axis)))
+
+    def start(self):
+        for d in range(1, self.count):
+            self.copy(d).start()
+        self.own().start()
+
+    def arrive(self):
+        for d in range(1, self.count):
+            self.copy(d).wait_recv()
+        self.own().wait()
+
+    def finish(self):
+        for d in range(1, self.count):
+            self.copy(d).wait_send()
+
+
 def rows_of(total, half, quarter):
     if quarter is None:
         return pl.ds(half * (total // 2), total // 2)
@@ -954,7 +1156,9 @@
     )
 
 
-def start_kernel(payload, w_qkv, q_side, beta_side, everyone, wq, send, recv, local):
+def start_kernel(
+    payload, w_qkv, gate_t, q_side, beta_side, everyone, wq, blocks, send, recv, local
+):
     s = lax.axis_index("seq")
     greet(ring_peers(), all_plane())
     line = Line(send, recv, local)
@@ -964,6 +1168,10 @@
         lambda t: w_qkv.at[pl.ds(t * 128, 128), :],
         lambda t, j: wq.at[pl.ds(t * 128, 128), pl.ds(j * width, width)],
     )
+    others = [
+        Scatter(line, (s + 8 * i,), lambda t: block_of(gate_t, t), lambda t, j, i=i: blocks.at[i])
+        for i in (0, 1)
+    ]
     ring = RingGather(line, payload, everyone)
     _, at = line.take(0, 2)
     sides = [
@@ -987,97 +1195,90 @@
     qkv.second()
     ring.middle()
     qkv.third()
+    for item in others:
+        item.start()
     qkv.fourth()
     ring.finish()
-    scatter.finish()
     qkv.finish()
+    for item in others:
+        item.arrive()
+    for item in [scatter] + others:
+        item.finish()
     for copy in sides:
         copy.wait()
 
 
-def start_gather(payload, w_qkv, q_side, beta_side):
+def start_gather(payload, w_qkv, gate_t, q_side, beta_side):
     seq, wide = lax.axis_size("seq"), payload.shape[1]
-    copies = RingGather.COPIES + Scatter.COPIES + PlaneGather.COPIES
+    copies = RingGather.COPIES + 3 * Scatter.COPIES + PlaneGather.COPIES
     return pl.pallas_call(
         start_kernel,
         out_shape=(
             jax.ShapeDtypeStruct((seq,) + payload.shape, BF16),
             jax.ShapeDtypeStruct((wide, q_side.shape[1]), BF16),
+            jax.ShapeDtypeStruct((2, gate_t.shape[0], 128), BF16),
         ),
-        in_specs=[ANY] * 4,
-        out_specs=(ANY,) * 2,
+        in_specs=[ANY] * 5,
+        out_specs=(ANY,) * 3,
         scratch_shapes=sems(copies, 10),
-        compiler_params=comm_params(0),
+        compiler_params=comm_params(0, 62),
         name="start_gather",
-    )(payload, w_qkv, q_side, beta_side)
+    )(payload, w_qkv, gate_t, q_side, beta_side)
 
 
 class Feed:
-    COPIES = RingGather.COPIES + 2 * Scatter.COPIES + 2 * PlaneGather.COPIES
-    LOCAL = RingGather.LOCAL + 2 * Scatter.LOCAL + 3
-
-    def __init__(self, line, cot, gate_t, w_out, sides, everyone, wg, wo, upper):
-        s = lax.axis_index("seq")
-        self.line, self.w_out, self.sides = line, w_out, sides
-        self.outs = (wo, wg)
+    COPIES = RingGather.COPIES + 2 * PlaneGather.COPIES
+    LOCAL = RingGather.LOCAL + 4
+
+    def __init__(self, line, cot, sources, sides, everyone, outs):
+        self.line, self.sources, self.sides, self.outs = line, sources, sides, outs
         self.ring = RingGather(line, cot, everyone)
-        self.scatters = [
-            Scatter(line, (source,), lambda t: block_of(gate_t, t), into)
-            for source, into in ((s, lambda t, j: block_of(wg, t)), (s + 8, lambda t, j: upper))
-        ]
-        self.out, self.gate = [PlaneGather(line, columns_place(o)) for o in self.outs]
-        _, self.at = line.take(0, 3)
+        self.gathers = [PlaneGather(line, columns_place(o)) for o in outs]
+        _, self.at = line.take(0, 4)
 
     def place(self, i):
         s, f = lax.axis_index("seq"), lax.axis_index("fsdp")
-        if i == 2:
-            wo = self.outs[0]
-            share = wo.shape[0]
-            src = self.w_out.at[pl.ds(pl.multiple_of(s * share, 16), share), :]
-            dst = block_of(wo, f)
+        out = self.outs[i % 2]
+        if i < 2:
+            share = out.shape[0]
+            src = self.sources[i].at[pl.ds(pl.multiple_of(s * share, 16), share), :]
+            dst = block_of(out, f)
         else:
-            src, out = self.sides[i], self.outs[i]
-            dst = out.at[:, pl.ds(out.shape[1] - SIDE, SIDE)]
+            src, dst = self.sides[i - 2], out.at[:, pl.ds(out.shape[1] - SIDE, SIDE)]
         return self.line.local(self.at + i, src, dst)
 
     def start(self):
-        for item in self.scatters:
-            item.start()
-        for i in range(3):
+        for i in range(4):
             self.place(i).start()
         self.ring.start()
-        self.place(2).wait()
-        self.out.first()
+        for i, gather in enumerate(self.gathers):
+            self.place(i).wait()
+            gather.first()
 
     def stage(self, step):
-        @pl.when(step == 2)
+        @pl.when(step == 1)
         def _():
-            self.out.second()
-            self.scatters[0].arrive()
-            self.gate.first()
+            for gather in self.gathers:
+                gather.second()
 
         @pl.when(step == 3)
         def _():
-            self.out.third()
+            for gather in self.gathers:
+                gather.third()
             self.ring.middle()
-            self.gate.second()
 
     def third(self):
-        self.out.fourth()
-        self.gate.third()
+        for gather in self.gathers:
+            gather.fourth()
 
     def fourth(self):
-        self.out.finish()
-        self.place(0).wait()
-        self.gate.fourth()
+        self.gathers[0].finish()
+        self.place(2).wait()
 
     def finish(self):
         self.ring.finish()
-        self.gate.finish()
-        self.place(1).wait()
-        self.scatters[1].arrive()
-        for item in self.scatters:
-            item.finish()
+        self.gathers[1].finish()
+        self.place(3).wait()
 
 
 def chip_at(step):
@@ -1087,7 +1288,7 @@
 
 
 def feed_forward_kernel(
-    partial, down_w, f_side, u_side, upper_block, wg_in, cot_in,
+    partial, blocks, g_side, u_side, wd_in, cot_in,
     tokens, cot, mixed, wo, up, gain, down, chosen,
     middle, grad_middle, partial_down, grad_mixed, early,
     rows2, rows3, cots, wg, wu, wd, partial2, total,
@@ -1110,20 +1311,14 @@
     ]
     first_gather = [RingGather(line, None, rows2, first, rows // 2) for first in firsts]
     second_gather = [RingGather(line, None, rows3, first, rows // 2) for first in firsts]
-    weights = [PlaneGather(line, columns_place(o)) for o in (wu, wd)]
-    share = wd.shape[0]
+    weights = [PlaneGather(line, columns_place(o)) for o in (wg, wu)]
     width = tokens.shape[1]
     _, at = line.take(0, 6)
-    mine = [
-        line.local(at, upper_block, block_of(wu, f)),
-        line.local(
-            at + 1, down_w.at[pl.ds(pl.multiple_of(s * share, 16), share), :], block_of(wd, f)
-        ),
-    ]
+    mine = [line.local(at + i, blocks.at[i], block_of(o, f)) for i, o in enumerate((wg, wu))]
     others = [
-        line.local(at + 2, u_side, wu.at[:, pl.ds(width, SIDE)]),
-        line.local(at + 3, f_side, wd.at[:, pl.ds(width, SIDE)]),
-        line.local(at + 4, wg_in, wg),
+        line.local(at + 2, g_side, wg.at[:, pl.ds(width, SIDE)]),
+        line.local(at + 3, u_side, wu.at[:, pl.ds(width, SIDE)]),
+        line.local(at + 4, wd_in, wd),
         line.local(at + 5, cot_in, cots),
     ]
     for copy in mine:
@@ -1165,9 +1360,6 @@
         item.finish()
     for copy in others:
         copy.wait()
-    gate_e[...] = jnp.zeros_like(gate_e)
-    upper_e[...] = jnp.zeros_like(upper_e)
-    down_e[...] = jnp.zeros_like(down_e)
     pair = 2 * rows
 
     def chip(step, carry):
@@ -1183,23 +1375,16 @@
         gate, upper = gate_s[...], upper_s[...]
         sigma = sigmoid(gate)
         silu = gate * sigma
-        hidden_s[...] = (silu * upper).astype(BF16)
-        gg_s[...] = (hidden * upper * sigma * (1.0 + gate * (1.0 - sigma))).astype(BF16)
-        gu_s[...] = (hidden * silu).astype(BF16)
+        hidden_s[k] = (silu * upper).astype(BF16)
+        gg_s[k] = (hidden * upper * sigma * (1.0 + gate * (1.0 - sigma))).astype(BF16)
+        gu_s[k] = (hidden * silu).astype(BF16)
         partial2[both] = (
-            (mm(gg_s[...], wg[...]) + mm(gu_s[...], wu[...]))
+            (mm(gg_s[k], wg[...]) + mm(gu_s[k], wu[...]))
             .astype(BF16)
             .reshape(2, pair // 2, width + SIDE)
         )
         for item in second_sum:
             item.send_step(step)
-        partial_down[both] = (
-            mm(hidden_s[...], wd[...]).astype(BF16).reshape(2, pair // 2, width + SIDE)
-        )
-        side = normed[:, width:]
-        gate_e[...] += mm_tn(side, gg_s[...])
-        upper_e[...] += mm_tn(side, gu_s[...])
-        down_e[...] += mm_tn(grads[:, width:], hidden_s[...])
         return carry
 
     lax.fori_loop(0, 4, chip, 0)
@@ -1223,6 +1408,22 @@
     second_sum[1].finish(total)
     by_rows(rows // 2, back_rows, rows // 2)
     second_gather[1].start()
+    gate_e[...] = jnp.zeros_like(gate_e)
+    upper_e[...] = jnp.zeros_like(upper_e)
+    down_e[...] = jnp.zeros_like(down_e)
+
+    def down_project(k, carry):
+        both = pl.ds(k * 2, 2)
+        partial_down[both] = (
+            mm(hidden_s[k], wd[...]).astype(BF16).reshape(2, rows, width + SIDE)
+        )
+        side = rows2[both, :, width:].reshape(pair, SIDE)
+        gate_e[...] += mm_tn(side, gg_s[k])
+        upper_e[...] += mm_tn(side, gu_s[k])
+        down_e[...] += mm_tn(cots[both, :, width:].reshape(pair, SIDE), hidden_s[k])
+        return carry
+
+    lax.fori_loop(0, 4, down_project, 0)
     for item in first_gather:
         item.sent()
 
@@ -1264,17 +1465,16 @@
 
 
 def feed_forward(
-    partial, down_w, f_side, u_side, upper, wg, cots,
-    tokens, cot, mixed, wo, up, gain, down, chosen,
+    partial, blocks, g_side, u_side, wd, cots, tokens, cot, mixed, wo, up, gain, down, chosen
 ):
     seq, rows, wide = partial.shape
-    share = f_side.shape[0]
+    share = g_side.shape[0]
     rank, part = chosen.shape[0], mixed.shape[1]
     whole = pltpu.VMEM((seq, rows, wide), BF16)
     weight = pltpu.VMEM((share, wide), BF16)
     buffers = sum_buffers(rows // 2, wide)
     f32_rows = pltpu.VMEM((2 * rows, share), F32)
-    bf16_rows = pltpu.VMEM((2 * rows, share), BF16)
+    bf16_rows = pltpu.VMEM((seq // 2, 2 * rows, share), BF16)
     extra = pltpu.VMEM((SIDE, share), F32)
     return pl.pallas_call(
         feed_forward_kernel,
@@ -1285,7 +1485,7 @@
             jax.ShapeDtypeStruct((seq * rows, part), BF16),
             jax.ShapeDtypeStruct((2, 2, rank, share + SIDE // 2), BF16),
         ),
-        in_specs=[ANY] * 7 + [VMEM] * 8,
+        in_specs=[ANY] * 6 + [VMEM] * 8,
         out_specs=(VMEM,) * 5,
         scratch_shapes=[whole, whole, whole, weight, weight, weight, whole]
         + [pltpu.VMEM((rows, wide), F32)]
@@ -1295,10 +1495,7 @@
         + sems(4 * RingSum.COPIES + 4 * RingGather.COPIES + 2 * PlaneGather.COPIES, 26),
         compiler_params=comm_params(2, 63),
         name="feed_forward",
-    )(
-        partial, down_w, f_side, u_side, upper, wg, cots,
-        tokens, cot, mixed, wo, up, gain, down, chosen,
-    )
+    )(partial, blocks, g_side, u_side, wd, cots, tokens, cot, mixed, wo, up, gain, down, chosen)
 
 
 class EarlySum:
@@ -1341,142 +1538,21 @@
         self.ring.start()
 
 
-def by_adapter(plane, out):
+def by_adapter(plane, marks, first, out):
     count, wide = out.shape[0], out.shape[2]
-    parts, n = plane.shape[1], plane.shape[3]
+    fsdp, parts, _, n = plane.shape
+    uses = [marks[f].astype(F32)[:1] for f in range(fsdp)]
     for q in range(parts):
         cut = min(n, wide - q * n)
+        if cut <= 0:
+            continue
+        items = [plane[f, q].astype(F32)[:, :cut] for f in range(fsdp)]
         for a in range(count):
             total = None
-            for f in range(plane.shape[0]):
-                at = wide - (parts - 1) * n + a
-                uses = plane[f, parts - 1].astype(F32)[:1, at : at + 1]
-                item = plane[f, q].astype(F32)[:, :cut] * uses
+            for f in range(fsdp):
+                item = items[f] * uses[f][:, first + a : first + a + 1]
                 total = item if total is None else total + item
             out[a, :, q * n : q * n + cut] = total.astype(BF16)
-
-
-def finale_kernel(
-    partial, normed, cot, early, up, inner, tokens, grad_middle, down, gain, chosen,
-    input_grad, early_whole, late_whole,
-    total, own, stage, relay, away, back, inners, sides, pieces, late, send, recv, local,
-):
-    greet(ring_peers(), line_peers())
-    line = Line(send, recv, local)
-    s, partner, _, _, _ = seq_places()
-    f = lax.axis_index("fsdp")
-    core = lax.rem(s, 2)
-    rank, columns = up.shape
-    ring = RingSum(line, partial, (own, stage, relay, away, back))
-    inner_ring = RingGather(line, inner, inners)
-    late_ring = RingGather(line, late, late_whole)
-
-    def early_place(t, half, quarter):
-        first = core * 4 + half * 2 + (quarter or 0)
-        return early_whole.at[t, pl.ds(first, 2 if quarter is None else 1)]
-
-    def late_place(t, half, quarter):
-        first = half * 2 + (quarter or 0)
-        return pieces.at[t, pl.ds(first, 2 if quarter is None else 1)]
-
-    early_plane, late_plane = PlaneGather(line, early_place), PlaneGather(line, late_place)
-    at, local_at = line.take(1, 3)
-    half_slices = pl.ds(core * 4, 4)
-    keep = line.local(local_at, early.at[half_slices], early_whole.at[f, half_slices])
-    share = line.copy(
-        at, early_whole.at[:, half_slices], early_whole.at[:, half_slices], {"seq": partner}
-    )
-    part = sides.shape[1] // 2
-    mine = pl.ds(pl.multiple_of(s * part, 128), part)
-    fetch = [
-        line.local(local_at + 1, normed.at[:, mine], sides.at[:, pl.ds(0, part)]),
-        line.local(local_at + 2, cot.at[:, mine], sides.at[:, pl.ds(part, part)]),
-    ]
-    inner_ring.start()
-    ring.start()
-    keep.start()
-    for copy in fetch:
-        copy.start()
-    keep.wait()
-    early_plane.first()
-    inner_ring.middle()
-    ring.middle()
-    inner_ring.finish()
-    tokens_here = tokens.shape[0]
-    n = inners.shape[3]
-    ahead = sides.shape[0] - n
-    sums, beside = [None, None], []
-    for t in range(inners.shape[0]):
-        parts = inners[t, 0].astype(F32), inners[t, 1].astype(F32)[:, :ahead]
-        sums = [p if total_ is None else total_ + p for p, total_ in zip(parts, sums)]
-        beside.append(inners[t, 1][:, ahead : ahead + tokens_here])
-    for copy in fetch:
-        copy.wait()
-    down_piece = mm(jnp.concatenate(sums, axis=1), sides[:, :part])
-    up_piece = mm(jnp.concatenate(beside, axis=1), sides[:, part:])
-    piece = jnp.concatenate(
-        [up[...], down_piece.astype(BF16), up_piece.astype(BF16), chosen[...], chosen[...]], axis=1
-    )
-    wide = pieces.shape[3]
-    for q in range(4):
-        pieces[f, q] = piece[:, q * wide : (q + 1) * wide]
-    late_plane.first()
-    early_plane.second()
-    ring.last()
-    late_plane.second()
-    late_plane.third()
-    early_plane.third()
-    late_plane.fourth()
-    late_plane.finish()
-    by_adapter(pieces, late)
-    late_ring.start()
-    early_plane.fourth()
-    ring.finish(total)
-    width = tokens.shape[1]
-
-    def step(rows):
-        grad = total[rows, :width] + mm(total[rows, width:], down[...])
-        input_grad[rows, :] = (
-            grad_middle[rows, :]
-            + norm_back_rows(tokens[rows, :].astype(F32), gain[...], grad)
-        ).astype(BF16)
-
-    by_rows(tokens_here, step)
-    early_plane.finish()
-    share.start()
-    late_ring.middle()
-    late_ring.finish()
-    share.wait()
-
-
-def finale_call(
-    partial, normed, cot, early, up, inner, tokens, grad_middle, down, gain, chosen, count
-):
-    seq, rows, wide = partial.shape
-    fsdp = 16
-    rank, columns = up.shape
-    part = (wide - SIDE) // seq
-    bf16 = lambda *shape: pltpu.VMEM(shape, BF16)
-    out = lambda *shape: jax.ShapeDtypeStruct(shape, BF16)
-    late = columns + 2 * part
-    copies = RingSum.COPIES + 2 * RingGather.COPIES + 2 * PlaneGather.COPIES + 1
-    return pl.pallas_call(
-        finale_kernel,
-        out_shape=(
-            out(rows, wide - SIDE), out(fsdp, *early.shape), out(seq, count, rank, late),
-        ),
-        in_specs=[ANY] * 4 + [VMEM, ANY] + [VMEM] * 5,
-        out_specs=(VMEM, ANY, ANY),
-        scratch_shapes=[pltpu.VMEM((rows, wide), F32)]
-        + sum_buffers(rows, wide)
-        + [
-            bf16(seq, *inner.shape), bf16(seq * rows, 2 * part),
-            bf16(fsdp, 4, rank, (late + 2 * SIDE) // 4), bf16(count, rank, late),
-        ]
-        + sems(copies, 4 + 2 + 3),
-        compiler_params=comm_params(4),
-        name="finale",
-    )(partial, normed, cot, early, up, inner, tokens, grad_middle, down, gain, chosen)
 
 
 def lay_out_early(whole, share, part):
@@ -1506,26 +1582,26 @@
     )(whole)
 
 
-def lay_out_late(whole, columns, part):
-    seq, count, rank, wide = whole.shape
-
-    def kernel(whole, qkv_up, qkv_down, ff_up):
+def lay_out_late(up, low, part):
+    seq, count, rank, columns = up.shape
+
+    def kernel(up, low, qkv_up, qkv_down, ff_up):
         for t in range(seq):
-            qkv_up[0, :, t * columns : (t + 1) * columns] = whole[t, 0, :, :columns].astype(F32)
-            for i, out in enumerate((qkv_down, ff_up)):
-                at = columns + i * part
-                out[0, :, t * part : (t + 1) * part] = whole[t, 0, :, at : at + part].astype(F32)
+            qkv_up[0, :, t * columns : (t + 1) * columns] = up[t, 0].astype(F32)
+            qkv_down[0, :, t * part : (t + 1) * part] = low[t, 0, :, :part].astype(F32)
+            ff_up[0, :, t * part : (t + 1) * part] = low[t, 0, :, part:].astype(F32)
 
     widths = (columns * seq, part * seq, part * seq)
+    cut = lambda n: pl.BlockSpec((seq, 1, rank, n), lambda a: (0, a, 0, 0))
     return pl.pallas_call(
         kernel,
         grid=(count,),
         out_shape=tuple(jax.ShapeDtypeStruct((count, rank, w), F32) for w in widths),
-        in_specs=[pl.BlockSpec((seq, 1, rank, wide), lambda a: (0, a, 0, 0))],
+        in_specs=[cut(columns), cut(2 * part)],
         out_specs=tuple(pl.BlockSpec((1, rank, w), lambda a: (a, 0, 0)) for w in widths),
         compiler_params=pltpu.CompilerParams(vmem_limit_bytes=32 << 20),
         name="lay_out_late",
-    )(whole)
+    )(up, low)
 
 
 def prepare_kernel(
@@ -1669,9 +1745,7 @@
     seq = lax.axis_size("seq")
     s = lax.axis_index("seq")
     width = tokens.shape[1]
-    heads = w_beta.shape[1] // seq
     count = qkv_down.shape[0]
-    columns = heads * 3 * CH
     which = adapter_index[0]
     length = segments.shape[1]
 
@@ -1685,30 +1759,27 @@
         turn(ffnout_down), ffnout_up, w_beta.T, conv_weight, segments, seq,
     )
 
-    normed, wq = start_gather(payload, w_qkv, q_side, beta_side)
+    normed, wq, blocks = start_gather(payload, w_qkv, w_gateup.T, q_side, beta_side)
     normed = normed.reshape(length, -1)
     fixed = (dcol, drow, taps, head_gain[None])
-    mixed, o_kept, t_kept, d_kept, s_kept, partial, joined, cot, wg, upper, wo = mixer_fwd(
-        normed, wq, cots, w_gateup.T, w_out, g_side, out_side, *fixed
+    mixed, o_kept, t_kept, d_kept, s_kept, partial, joined, cot, wo, wd = mixer_fwd(
+        normed, wq, cots, w_out, w_down, out_side, f_side, *fixed
     )
 
     middle, grad_middle, partial_down, grad_mixed, early = feed_forward(
-        partial, w_down, f_side, u_side, upper, wg, cot, tokens, cotangent, mixed, wo,
+        partial, blocks, g_side, u_side, wd, cot, tokens, cotangent, mixed, wo,
         m_lines, ffn_gain[None], g_lines, chosen,
     )
 
-    partial, up, layer_out, inner, early = mixer_bwd(
-        joined, partial_down, early, normed, wq, q_side, middle, f_lines, *fixed,
-        grad_mixed, o_kept, t_kept, d_kept, s_kept,
-    )
-    input_grad, early, late = finale_call(
-        partial, normed, cot.reshape(length, -1), early, up, inner,
+    layer_out, input_grad, early, up, low = mixer_bwd(
+        joined, partial_down, early, normed, wq, cot.reshape(length, -1), q_side, middle, f_lines,
+        *fixed, grad_mixed, o_kept, t_kept, d_kept, s_kept,
         tokens, grad_middle, q_lines, attn_gain[None], chosen, count,
     )
     gateup_g, mixdown_g, mixup_g, gudown_g, ffdown_g = lay_out_early(
         early, w_down.shape[0] // seq, width // seq
     )
-    qkvup_g, qkvdown_g, ffup_g = lay_out_late(late, columns, width // seq)
+    qkvup_g, qkvdown_g, ffup_g = lay_out_late(up, low, width // seq)
     return (
         layer_out,
         input_grad,

time: 367 us -> 342 us (0.932)
  Pallas kernels: 354 us -> 333 us
    pallas_call x1 -> x0, Pallas kernels: 49 us -> none  [finale_call(): pl.pallas_call(finale_kernel, out_shape=(out(rows, wide - SIDE), out(fsdp...]
    pallas_call x1, Pallas kernels: 49.1 us -> 93.1 us  [mixer_bwd(): pl.pallas_call(functools.partial(mixer_bwd_kernel, heads, chunks), out_sh...]
    pallas_call x1, Pallas kernels: 78.9 us -> 58.7 us  [mixer_fwd(): pl.pallas_call(functools.partial(mixer_fwd_kernel, heads, chunks), out_sh...]
    pallas_call x1, Pallas kernels: 42.8 us -> 50.2 us  [start_gather(): pl.pallas_call(start_kernel, out_shape=(jax.ShapeDtypeStruct((seq,) + pay...]
    unnamed x30 -> x12, local copies, waits for them, and re-layouts: 9.94 us -> 7 us
where the time goes in v3:
time: 342 us
  Pallas kernels  333 us (97%)
  local copies, waits for them, and re-layouts  7 us (2%)
    pallas_call x1, Pallas kernels, feed_forward(): pl.pallas_call(feed_forward_kernel, out_shape=(jax.ShapeDtypeStruct((rows...  117 us
    pallas_call x1, Pallas kernels, mixer_bwd(): pl.pallas_call(functools.partial(mixer_bwd_kernel, heads, chunks), out_sh...  93.1 us
    pallas_call x1, Pallas kernels, mixer_fwd(): pl.pallas_call(functools.partial(mixer_fwd_kernel, heads, chunks), out_sh...  58.7 us
    pallas_call x1, Pallas kernels, start_gather(): pl.pallas_call(start_kernel, out_shape=(jax.ShapeDtypeStruct((seq,) + pay...  50.2 us
    unnamed x12, local copies, waits for them, and re-layouts  7 us

profile of v3, /device:TPU:1, one launch (start us, length us, event | category | flops | bytes accessed | tf_op | source)
XLA Modules:
  0.0 342.0 jit_solution(17735199833344543765)
XLA Ops:
  1.3 0.6 pad_add_fusion.places
  1.8 4.9 %prepare.1 = (bf16[128,2176]{1,0:T(8,128)(2,1)}, bf16[128,2176]{1,0:T(8,128)(2,1)}, bf16[128,896]{1,0:T(8,128)(2,1)}, bf16[2048,128]{1,0:T(8,128)(2,1)}, bf16[25...) custom-call(s32[2]{0:T(128)} %pad_add_fusion.places, ...), custom_call_target="tpu_custom_call" | custom-call | tf_op jit(solution)/shard_map/prepare/pallas_call | solution.py:1700
  6.8 50.2 %start_gather.1 = (bf16[8,128,2176]{2,1,0:T(8,128)(2,1)}, bf16[2176,896]{1,0:T(8,128)(2,1)}, bf16[2,704,128]{2,1,0:T(8,128)(2,1)}) custom-call(bf16[128,2176]{1,0:T(8,128)(2,1)} %get-tuple-element.57.payload, bf16[2048,384]{1,0:T(8,128)(2,1)} %w_qkv.1, bf16[704,2048]{1,0:T(8,128)(2,1)} %bitcast.19, bf16[128,896]{1,0:T(8,128)(2,1)} %get-tuple-element.58.q_side, ...), custom_call_target="tpu_custom_call" | custom-call | tf_op jit(solution)/shard_map/start_gather/pallas_call | solution.py:1214
  56.9 58.7 %mixer_fwd.1 = (bf16[1024,256]{1,0:T(8,128)(2,1)}, f32[2,1024,128]{2,1,0:T(8,128)}, bf16[2,1024,128]{2,1,0:T(8,128)(2,1)}, bf16[2,1024,128]{2,1,0:T(8,128)(2,1)}...) custom-call(bf16[1024,2176]{1,0:T(8,128)(2,1)} %bitcast.16, ...), custom_call_target="tpu_custom_call" | custom-call | tf_op jit(solution)/shard_map/mixer_fwd/pallas_call | solution.py:232
  115.6 117.4 %feed_forward.1 = (f32[128,2048]{1,0:T(8,128)}, f32[128,2048]{1,0:T(8,128)}, bf16[8,128,2176]{2,1,0:T(8,128)(2,1)}, bf16[1024,256]{1,0:T(8,128)(2,1)}, bf16[2,2,16,768]{3,2,1,0:T(8,128)(2,1)}) custom-call(bf16[8,128,2176]{2,1,0:T(8,128)(2,1)} %get-tuple-element.69.partial, bf16[2,704,128]{2,1,0:T(8,128)(2,1)} %get-tuple-element.70.blocks, ...), custom_call_target="tpu_custom_call" | custom-call | tf_op jit(solution)/shard_map/feed_forward/pallas_call | solution.py:1479
  233.0 93.1 %mixer_bwd.1 = (bf16[128,2048]{1,0:T(8,128)(2,1)}, bf16[128,2048]{1,0:T(8,128)(2,1)}, bf16[16,8,2,16,768]{4,3,2,1,0:T(8,128)(2,1)}, bf16[8,8,16,768]{3,2,1,0:T(8,128)(2,1)}, bf16[8,8,16,512]{3,2,1,0:T(8,128)(2,1)}) custom-call(bf16[1024,896]{1,0:T(8,128)(2,1)} %get-tuple-element.68.source, bf16[8,128,2176]{2,1,0:T(8,128)(2,1)} %get-tuple-element.80.partial, ...), custom_call_target="tpu_custom_call" | custom-call | tf_op jit(solution)/shard_map/mixer_bwd/pallas_call | solution.py:606
  326.1 0.0 copy-start.1
  326.1 1.4 copy-done.1
  327.5 0.0 copy-start.2
  327.5 1.2 copy-done.2
  328.7 3.7 %lay_out_late.1 = (f32[8,16,6144]{2,1,0:T(8,128)}, f32[8,16,2048]{2,1,0:T(8,128)}, f32[8,16,2048]{2,1,0:T(8,128)}) custom-call(bf16[8,8,16,768]{3,2,1,0:T(8,128)(2,1)S(1)} %copy-done.1, bf16[8,8,16,512]{3,2,1,0:T(8,128)(2,1)S(1)} %copy-done.2), custom_call_target="tpu_custom_call" | custom-call | tf_op jit(solution)/shard_map/lay_out_late/pallas_call | solution.py:1596
  332.5 0.0 copy-start
  332.5 2.8 copy-done
  335.3 0.0 copy-start.4
  335.3 0.0 copy-start.3
  335.3 5.1 %lay_out_early.1 = (f32[8,16,11264]{2,1,0:T(8,128)}, f32[8,16,2048]{2,1,0:T(8,128)}, f32[8,16,2048]{2,1,0:T(8,128)}, f32[8,16,2048]{2,1,0:T(8,128)}, f32[8,16,5632]{2,1,0:T(8,128)}) custom-call(bf16[16,8,2,16,768]{4,3,2,1,0:T(8,128)(2,1)S(1)} %copy-done), custom_call_target="tpu_custom_call" | custom-call | tf_op jit(solution)/shard_map/lay_out_early/pallas_call | solution.py:1574
  340.4 0.0 copy-done.4
  340.4 0.8 copy.34
  341.2 0.0 copy-done.3
  341.2 0.8 copy.35
Async XLA Ops:
  326.1 1.4 copy-start.1
  327.5 1.2 copy-start.2
  332.5 2.8 copy-start
  335.3 5.2 %copy-start.4 = (bf16[128,2048]{1,0:T(8,128)(2,1)S(1)}, bf16[128,2048]{1,0:T(8,128)(2,1)}, u32[]{:S(2)}) copy-start(bf16[128,2048]{1,0:T(8,128)(2,1)} %get-tuple-element.114) | copy-start | bytes 1572868
  335.3 5.9 %copy-start.3 = (bf16[128,2048]{1,0:T(8,128)(2,1)S(1)}, bf16[128,2048]{1,0:T(8,128)(2,1)}, u32[]{:S(2)}) copy-start(bf16[128,2048]{1,0:T(8,128)(2,1)} %get-tuple-element.115) | copy-start | bytes 1572868

commit v4 on v3

--- a/solution.py
+++ b/solution.py
@@ -1291,8 +1291,8 @@
     partial, blocks, g_side, u_side, wd_in, cot_in,
     tokens, cot, mixed, wo, up, gain, down, chosen,
     middle, grad_middle, partial_down, grad_mixed, early,
-    rows2, rows3, cots, wg, wu, wd, partial2, total,
-    gate_s, upper_s, hidden_s, gg_s, gu_s, gate_e, upper_e, down_e, *rest,
+    rows2, rows3, cots, wgu, wd, partial2, total,
+    both_s, hidden_s, grads_s, both_e, down_e, *rest,
 ):
     greet(ring_peers(), line_peers())
     buffers, (send, recv, local) = rest[:-3], rest[-3:]
@@ -1311,6 +1311,8 @@
     ]
     first_gather = [RingGather(line, None, rows2, first, rows // 2) for first in firsts]
     second_gather = [RingGather(line, None, rows3, first, rows // 2) for first in firsts]
+    share = g_side.shape[0]
+    wg, wu = wgu.at[pl.ds(0, share), :], wgu.at[pl.ds(share, share), :]
     weights = [PlaneGather(line, columns_place(o)) for o in (wg, wu)]
     width = tokens.shape[1]
     _, at = line.take(0, 6)
@@ -1330,10 +1332,10 @@
         item.first()
     for copy in others:
         copy.start()
-    for item in first_sum:
-        item.middle()
+    first_sum[0].middle()
     for item in weights:
         item.second()
+    first_sum[1].middle()
     for item in first_sum:
         item.last()
 
@@ -1349,11 +1351,11 @@
     first_sum[0].finish(total)
     by_rows(rows // 2, norm_rows)
     first_gather[0].start()
-    for item in weights:
-        item.third()
+    weights[0].third()
     first_sum[1].finish(total)
     by_rows(rows // 2, norm_rows, rows // 2)
     first_gather[1].start()
+    weights[1].third()
     for item in weights:
         item.fourth()
     for item in weights:
@@ -1369,17 +1371,16 @@
         both = pl.ds(k * 2, 2)
         normed = rows2[both].reshape(pair, width + SIDE)
         grads = cots[both].reshape(pair, width + SIDE)
-        gate_s[...] = mm_nt(normed, wg[...])
-        upper_s[...] = mm_nt(normed, wu[...])
+        both_s[...] = mm_nt(normed, wgu[...])
         hidden = mm_nt(grads, wd[...])
-        gate, upper = gate_s[...], upper_s[...]
+        gate, upper = both_s[:, :share], both_s[:, share:]
         sigma = sigmoid(gate)
         silu = gate * sigma
         hidden_s[k] = (silu * upper).astype(BF16)
-        gg_s[k] = (hidden * upper * sigma * (1.0 + gate * (1.0 - sigma))).astype(BF16)
-        gu_s[k] = (hidden * silu).astype(BF16)
+        grads_s[k, :, :share] = (hidden * upper * sigma * (1.0 + gate * (1.0 - sigma))).astype(BF16)
+        grads_s[k, :, share:] = (hidden * silu).astype(BF16)
         partial2[both] = (
-            (mm(gg_s[k], wg[...]) + mm(gu_s[k], wu[...]))
+            mm(grads_s[k], wgu[...])
             .astype(BF16)
             .reshape(2, pair // 2, width + SIDE)
         )
@@ -1408,8 +1409,7 @@
     second_sum[1].finish(total)
     by_rows(rows // 2, back_rows, rows // 2)
     second_gather[1].start()
-    gate_e[...] = jnp.zeros_like(gate_e)
-    upper_e[...] = jnp.zeros_like(upper_e)
+    both_e[...] = jnp.zeros_like(both_e)
     down_e[...] = jnp.zeros_like(down_e)
 
     def down_project(k, carry):
@@ -1418,8 +1418,7 @@
             mm(hidden_s[k], wd[...]).astype(BF16).reshape(2, rows, width + SIDE)
         )
         side = rows2[both, :, width:].reshape(pair, SIDE)
-        gate_e[...] += mm_tn(side, gg_s[k])
-        upper_e[...] += mm_tn(side, gu_s[k])
+        both_e[...] += mm_tn(side, grads_s[k])
         down_e[...] += mm_tn(cots[both, :, width:].reshape(pair, SIDE), hidden_s[k])
         return carry
 
@@ -1443,11 +1442,7 @@
     own_part = pl.ds(pl.multiple_of(s * part, 128), part)
     flat = lambda v: v.reshape(-1, v.shape[-1])
     side2, side3 = flat(rows2[:, :, width:]), flat(rows3[:, :, width:])
-    first = [
-        gate_e[rank : 2 * rank, :].astype(BF16),
-        upper_e[rank : 2 * rank, :].astype(BF16),
-        chosen[...],
-    ]
+    first = [both_e[rank : 2 * rank, :].astype(BF16), chosen[...]]
     second = [
         mm_tn(side3, mixed[...])[:rank].astype(BF16),
         mm_tn(side2, flat(rows3[:, :, own_part]))[:rank].astype(BF16),
@@ -1473,9 +1468,13 @@
     whole = pltpu.VMEM((seq, rows, wide), BF16)
     weight = pltpu.VMEM((share, wide), BF16)
     buffers = sum_buffers(rows // 2, wide)
-    f32_rows = pltpu.VMEM((2 * rows, share), F32)
-    bf16_rows = pltpu.VMEM((seq // 2, 2 * rows, share), BF16)
-    extra = pltpu.VMEM((SIDE, share), F32)
+    scratch = [
+        pltpu.VMEM((2 * rows, 2 * share), F32),
+        pltpu.VMEM((seq // 2, 2 * rows, share), BF16),
+        pltpu.VMEM((seq // 2, 2 * rows, 2 * share), BF16),
+        pltpu.VMEM((SIDE, 2 * share), F32),
+        pltpu.VMEM((SIDE, share), F32),
+    ]
     return pl.pallas_call(
         feed_forward_kernel,
         out_shape=(
@@ -1487,9 +1486,9 @@
         ),
         in_specs=[ANY] * 6 + [VMEM] * 8,
         out_specs=(VMEM,) * 5,
-        scratch_shapes=[whole, whole, whole, weight, weight, weight, whole]
+        scratch_shapes=[whole, whole, whole, pltpu.VMEM((2 * share, wide), BF16), weight, whole]
         + [pltpu.VMEM((rows, wide), F32)]
-        + [f32_rows, f32_rows, bf16_rows, bf16_rows, bf16_rows, extra, extra, extra]
+        + scratch
         + buffers * 2
         + buffers[1:] * 2
         + sems(4 * RingSum.COPIES + 4 * RingGather.COPIES + 2 * PlaneGather.COPIES, 26),

time: 342 us -> 341 us (level)
  no operation moved by 1% of the time
where the time goes in v4:
time: 341 us
  Pallas kernels  332 us (97%)
  local copies, waits for them, and re-layouts  7 us (2%)
    pallas_call x1, Pallas kernels, feed_forward(): pl.pallas_call(feed_forward_kernel, out_shape=(jax.ShapeDtypeStruct((rows...  116 us
    pallas_call x1, Pallas kernels, mixer_bwd(): pl.pallas_call(functools.partial(mixer_bwd_kernel, heads, chunks), out_sh...  93 us
    pallas_call x1, Pallas kernels, mixer_fwd(): pl.pallas_call(functools.partial(mixer_fwd_kernel, heads, chunks), out_sh...  58.7 us
    pallas_call x1, Pallas kernels, start_gather(): pl.pallas_call(start_kernel, out_shape=(jax.ShapeDtypeStruct((seq,) + pay...  50.2 us
    unnamed x12, local copies, waits for them, and re-layouts  7 us

profile of v4, /device:TPU:1, one launch (start us, length us, event | category | flops | bytes accessed | tf_op | source)
XLA Modules:
  0.0 340.7 jit_solution(7199787874151422377)
XLA Ops:
  1.3 0.6 pad_add_fusion.places
  1.8 4.9 %prepare.1 = (bf16[128,2176]{1,0:T(8,128)(2,1)}, bf16[128,2176]{1,0:T(8,128)(2,1)}, bf16[128,896]{1,0:T(8,128)(2,1)}, bf16[2048,128]{1,0:T(8,128)(2,1)}, bf16[25...) custom-call(s32[2]{0:T(128)} %pad_add_fusion.places, ...), custom_call_target="tpu_custom_call" | custom-call | tf_op jit(solution)/shard_map/prepare/pallas_call | solution.py:1699
  6.8 50.2 %start_gather.1 = (bf16[8,128,2176]{2,1,0:T(8,128)(2,1)}, bf16[2176,896]{1,0:T(8,128)(2,1)}, bf16[2,704,128]{2,1,0:T(8,128)(2,1)}) custom-call(bf16[128,2176]{1,0:T(8,128)(2,1)} %get-tuple-element.57.payload, bf16[2048,384]{1,0:T(8,128)(2,1)} %w_qkv.1, bf16[704,2048]{1,0:T(8,128)(2,1)} %bitcast.19, bf16[128,896]{1,0:T(8,128)(2,1)} %get-tuple-element.58.q_side, ...), custom_call_target="tpu_custom_call" | custom-call | tf_op jit(solution)/shard_map/start_gather/pallas_call | solution.py:1214
  56.9 58.7 %mixer_fwd.1 = (bf16[1024,256]{1,0:T(8,128)(2,1)}, f32[2,1024,128]{2,1,0:T(8,128)}, bf16[2,1024,128]{2,1,0:T(8,128)(2,1)}, bf16[2,1024,128]{2,1,0:T(8,128)(2,1)}...) custom-call(bf16[1024,2176]{1,0:T(8,128)(2,1)} %bitcast.16, ...), custom_call_target="tpu_custom_call" | custom-call | tf_op jit(solution)/shard_map/mixer_fwd/pallas_call | solution.py:232
  115.6 116.1 %feed_forward.1 = (f32[128,2048]{1,0:T(8,128)}, f32[128,2048]{1,0:T(8,128)}, bf16[8,128,2176]{2,1,0:T(8,128)(2,1)}, bf16[1024,256]{1,0:T(8,128)(2,1)}, bf16[2,2,16,768]{3,2,1,0:T(8,128)(2,1)}) custom-call(bf16[8,128,2176]{2,1,0:T(8,128)(2,1)} %get-tuple-element.69.partial, bf16[2,704,128]{2,1,0:T(8,128)(2,1)} %get-tuple-element.70.blocks, ...), custom_call_target="tpu_custom_call" | custom-call | tf_op jit(solution)/shard_map/feed_forward/pallas_call | solution.py:1478
  231.7 93.0 %mixer_bwd.1 = (bf16[128,2048]{1,0:T(8,128)(2,1)}, bf16[128,2048]{1,0:T(8,128)(2,1)}, bf16[16,8,2,16,768]{4,3,2,1,0:T(8,128)(2,1)}, bf16[8,8,16,768]{3,2,1,0:T(8,128)(2,1)}, bf16[8,8,16,512]{3,2,1,0:T(8,128)(2,1)}) custom-call(bf16[1024,896]{1,0:T(8,128)(2,1)} %get-tuple-element.68.source, bf16[8,128,2176]{2,1,0:T(8,128)(2,1)} %get-tuple-element.80.partial, ...), custom_call_target="tpu_custom_call" | custom-call | tf_op jit(solution)/shard_map/mixer_bwd/pallas_call | solution.py:606
  324.8 0.0 copy-start.1
  324.8 1.4 copy-done.1
  326.2 0.0 copy-start.2
  326.2 1.2 copy-done.2
  327.4 3.7 %lay_out_late.1 = (f32[8,16,6144]{2,1,0:T(8,128)}, f32[8,16,2048]{2,1,0:T(8,128)}, f32[8,16,2048]{2,1,0:T(8,128)}) custom-call(bf16[8,8,16,768]{3,2,1,0:T(8,128)(2,1)S(1)} %copy-done.1, bf16[8,8,16,512]{3,2,1,0:T(8,128)(2,1)S(1)} %copy-done.2), custom_call_target="tpu_custom_call" | custom-call | tf_op jit(solution)/shard_map/lay_out_late/pallas_call | solution.py:1595
  331.2 0.0 copy-start
  331.2 2.8 copy-done
  333.9 0.0 copy-start.4
  333.9 0.0 copy-start.3
  333.9 5.1 %lay_out_early.1 = (f32[8,16,11264]{2,1,0:T(8,128)}, f32[8,16,2048]{2,1,0:T(8,128)}, f32[8,16,2048]{2,1,0:T(8,128)}, f32[8,16,2048]{2,1,0:T(8,128)}, f32[8,16,5632]{2,1,0:T(8,128)}) custom-call(bf16[16,8,2,16,768]{4,3,2,1,0:T(8,128)(2,1)S(1)} %copy-done), custom_call_target="tpu_custom_call" | custom-call | tf_op jit(solution)/shard_map/lay_out_early/pallas_call | solution.py:1573
  339.1 0.0 copy-done.4
  339.1 0.8 copy.34
  339.9 0.0 copy-done.3
  339.9 0.8 copy.35
Async XLA Ops:
  324.8 1.4 copy-start.1
  326.2 1.2 copy-start.2
  331.2 2.8 copy-start
  333.9 5.2 %copy-start.4 = (bf16[128,2048]{1,0:T(8,128)(2,1)S(1)}, bf16[128,2048]{1,0:T(8,128)(2,1)}, u32[]{:S(2)}) copy-start(bf16[128,2048]{1,0:T(8,128)(2,1)} %get-tuple-element.114) | copy-start | bytes 1572868
  333.9 5.9 %copy-start.3 = (bf16[128,2048]{1,0:T(8,128)(2,1)S(1)}, bf16[128,2048]{1,0:T(8,128)(2,1)}, u32[]{:S(2)}) copy-start(bf16[128,2048]{1,0:T(8,128)(2,1)} %get-tuple-element.115) | copy-start | bytes 1572868
